TPU v7x, 32 devices: a whole 2x2x4 slice. The times are simulated.
32 devices in a mesh: svc: 8 (over z, x), step: 4 (over y, core).
Axes of the slice: x: 2, y: 2, z: 4, core: 2. Of those that a mesh axis runs over, the one named last changes fastest.
Arguments:
- service_factors: bfloat16 [49152, 256], P('svc'), may hold values from -1.5 to 1.5
- step_factors: bfloat16 [4096, 256], P('step'), may hold values from -1.5 to 1.5
- block_rows: int32 [8, 4, 154], P('svc', 'step'), may hold values from 0 to 47, as said below
- block_cols: int32 [8, 4, 154], P('svc', 'step'), may hold values from 0 to 7
- block_counts: int32 [8, 4], P('svc', 'step'), may hold values from 1 to 154, as said below
- block_values: bfloat16 [8, 4, 154, 128, 128], P('svc', 'step'), may hold values from -6 to 6
Outputs:
- new_services: bfloat16 [49152, 256], P('svc')
- new_steps: bfloat16 [4096, 256], P('step')
Inputs may be any that keep to these rules, and one draw needn't show every extreme that they name: Within one tile's 154 slots the pairs (block_rows, block_cols) are all different. `block_counts`: some tile has all 154 slots observed.
All inputs are finite; a program needn't handle non-finite values.
Results may differ from a plain program's by a relative error of at most 0.002.
The roundings to bfloat16 on the way count: a program that leaves them out, or rounds other values in their place, can miss the bound.
Values may be sent and summed in bfloat16 or wider, within the bound.
No kernel may reach another device: no remote copies, remote signals or barrier semaphores. Data moves between devices by JAX's collectives and lax.ppermute only.
A program may use at most 128 MiB of HBM per device.

v0:
```python
import jax
import jax.numpy as jnp
from jax import lax
from jax.sharding import PartitionSpec as P

step_u = 0.03
step_v = 0.02
ridge = 0.1
smooth = 20.0


def extended(block, sides, width):
    for axis, dim in sides:
        count = lax.axis_size(axis)
        forward = [(i, i + 1) for i in range(count - 1)]
        forward.append((count - 1, 0))
        backward = [(target, source) for source, target in forward]
        low = lax.ppermute(
            lax.slice_in_dim(block, block.shape[dim] - width, None, axis=dim), axis, forward
        )
        high = lax.ppermute(lax.slice_in_dim(block, 0, width, axis=dim), axis, backward)
        block = jnp.concatenate([low, block, high], axis=dim)
    return block


def on_device(service_factors, step_factors, block_rows, block_cols, block_counts, block_values):
    serv_rows, width = service_factors.shape
    time_rows = step_factors.shape[0]
    slot_total = block_rows.shape[2]
    serv_blocks = serv_rows // 128
    time_blocks = time_rows // 128
    row_list = block_rows[0, 0]
    col_list = block_cols[0, 0]
    values = block_values[0, 0]
    live_mask = (jnp.arange(slot_total, dtype=jnp.int32) < block_counts[0, 0]).astype(jnp.float32)
    u_tiles = service_factors.reshape(serv_blocks, 128, width)
    v_tiles = step_factors.reshape(time_blocks, 128, width)
    right_blocks = v_tiles[col_list]

    def residual(left_blocks):
        predicted = jnp.einsum(
            "nir,njr->nij", left_blocks, right_blocks, preferred_element_type=jnp.float32
        )
        return ((predicted - values.astype(jnp.float32)) * live_mask[:, None, None]).astype(
            jnp.bfloat16
        )

    errors = residual(u_tiles[row_list])
    grad_blocks = jnp.einsum(
        "nij,njr->nir", errors, right_blocks, preferred_element_type=jnp.float32
    )
    grad_part = jnp.zeros((serv_blocks, 128, width), jnp.float32).at[row_list].add(grad_blocks)
    grad_part = grad_part.reshape(serv_rows, width)
    grad_whole = lax.psum(grad_part, "step")
    old_u = service_factors.astype(jnp.float32)
    new_services = (old_u - step_u * (grad_whole + ridge * old_u)).astype(jnp.bfloat16)
    new_tiles = new_services.reshape(serv_blocks, 128, width)
    left_blocks = new_tiles[row_list]
    errors_two = residual(left_blocks)
    grad_v_blocks = jnp.einsum(
        "nij,nir->njr", errors_two, left_blocks, preferred_element_type=jnp.float32
    )
    grad_v_part = jnp.zeros((time_blocks, 128, width), jnp.float32).at[col_list].add(grad_v_blocks)
    grad_v_part = grad_v_part.reshape(time_rows, width)
    grad_v = lax.psum(grad_v_part, "svc")
    padded = extended(step_factors, (("step", 0),), 1)
    old_v = step_factors.astype(jnp.float32)
    laplace = 2.0 * old_v - padded[:-2].astype(jnp.float32) - padded[2:].astype(jnp.float32)
    new_steps = (old_v - step_v * (grad_v + ridge * old_v + smooth * laplace)).astype(jnp.bfloat16)
    return (new_services, new_steps)


def solution(mesh):
    return jax.shard_map(
        on_device,
        mesh=mesh,
        in_specs=(
            P("svc", None),
            P("step", None),
            P("svc", "step", None),
            P("svc", "step", None),
            P("svc", "step"),
            P("svc", "step", None, None, None),
        ),
        out_specs=(P("svc", None), P("step", None)),
        check_vma=False,
    )
```

profile of v0, /device:TPU:0, one launch (start us, length us, event | category | flops | bytes accessed | tf_op | source)
XLA Modules:
  0.0 380.7 jit_solution(9016039108349714516)
XLA Ops:
  7.2 0.0 all-reduce.3.cloned.1.call-start
  7.2 0.7 compare_select_fusion.1
  7.9 0.7 compare_select_fusion
  9.3 0.0 copy-start.1
  9.3 9.4 %gather_fusion = bf16[154,128,256]{2,1,0:T(8,128)(2,1)} fusion(bf16[48,128,256]{2,1,0:T(8,128)(2,1)} %bitcast.32, s32[1024]{0:T(1024)S(1)} %pad_clamp_fusion.1), kind=kCustom, calls=%fused_computation | custom fusion | bytes 20185704 | tf_op jit(solution)/shard_map/gather | solution.py:48
  18.6 0.0 copy-done.1
  18.7 7.5 %gather_fusion.1 = bf16[154,128,256]{2,1,0:T(8,128)(2,1)} fusion(bf16[8,128,256]{2,1,0:T(8,128)(2,1)S(1)} %bitcast.30, s32[1024]{0:T(1024)S(1)} %pad_clamp_fusion), kind=kCustom, calls=%fused_computation.1 | custom fusion | bytes 20185704 | tf_op jit(solution)/shard_map/gather | solution.py:38
  26.1 23.4 %fusion.11 = f32[154,128,256]{2,1,0:T(8,128)} fusion(bf16[154,128,256]{2,1,0:T(8,128)(2,1)} %gather_fusion.1, bf16[154,128,256]{2,1,0:T(8,128)(2,1)} %gather_fusion, bf16[1,1,154,128,128]{4,3,2,1,0:T(8,128)(2,1)} %param.11, f32[154]{0:T(256)S(1)} %compare_convert_fusion), kind=kOutput, calls=%fused_computation.18 | convolution fusion | flops 2593783808 | bytes 45417064 | tf_op jit(solution)/shard_map/nij,njr->nir/dot_general | solution.py:49
  49.5 3.4 broadcast_in_dim.4
  52.9 47.2 %scatter_fusion = f32[48,128,256]{2,1,0:T(8,128)} fusion(f32[48,128,256]{2,1,0:T(8,128)} %broadcast_in_dim.4, s32[154]{0:T(256)S(1)} %bitcast.37, f32[154,128,256]{2,1,0:T(8,128)} %fusion.11), kind=kCustom, calls=%fused_computation.3 | custom fusion | flops 5046272 | bytes 60555880 | tf_op jit(solution)/shard_map/scatter-add | solution.py:52
  100.1 0.0 all-reduce.3.cloned.1.call-update
  100.1 0.2 all-reduce.5.cloned.1.call-start
  100.4 122.3 %all-reduce.3.cloned.1.call-done = f32[6144,256]{1,0:T(8,128)} async-done(((f32[6144,256]{1,0:T(8,128)}), f32[6144,256]{1,0:T(8,128)}) %all-reduce.3.cloned.1.call-update) | async-done | bytes 6291472 | tf_op jit(solution)/shard_map/psum | solution.py:54
  222.6 6.5 %fusion.6 = bf16[6144,256]{1,0:T(8,128)(2,1)} fusion(f32[6144,256]{1,0:T(8,128)} %all-reduce.3.cloned.1.call-done, bf16[6144,256]{1,0:T(8,128)(2,1)} %param.6), kind=kLoop, calls=%fused_computation.15 | loop fusion | flops 9437184 | bytes 12582912 | tf_op jit(solution)/shard_map/convert_element_type | solution.py:56
  229.2 9.3 %gather_fusion.2 = bf16[154,128,256]{2,1,0:T(8,128)(2,1)} fusion(bf16[48,128,256]{2,1,0:T(8,128)(2,1)} %bitcast.33, s32[1024]{0:T(1024)S(1)} %pad_clamp_fusion.1), kind=kCustom, calls=%fused_computation.2 | custom fusion | bytes 20185704 | tf_op jit(solution)/shard_map/gather | solution.py:58
  238.5 23.5 %fusion.7 = f32[154,128,256]{2,1,0:T(8,128)} fusion(bf16[154,128,256]{2,1,0:T(8,128)(2,1)} %gather_fusion.2, bf16[154,128,256]{2,1,0:T(8,128)(2,1)} %gather_fusion.1, bf16[1,1,154,128,128]{4,3,2,1,0:T(8,128)(2,1)} %param.11, f32[154]{0:T(256)S(1)} %compare_convert_fusion), kind=kOutput, calls=%fused_computation.16 | convolution fusion | flops 2593783808 | bytes 45417064 | tf_op jit(solution)/shard_map/nij,nir->njr/dot_general | solution.py:60
  261.9 0.1 broadcast_in_dim.5
  262.0 29.8 %scatter_fusion.1 = f32[8,128,256]{2,1,0:T(8,128)S(1)} fusion(f32[8,128,256]{2,1,0:T(8,128)S(1)} %broadcast_in_dim.5, s32[154]{0:T(256)S(1)} %bitcast.35, f32[154,128,256]{2,1,0:T(8,128)} %fusion.7), kind=kCustom, calls=%fused_computation.4 | custom fusion | flops 5046272 | bytes 60555880 | tf_op jit(solution)/shard_map/scatter-add | solution.py:63
  291.9 0.0 copy-start
  291.9 1.0 copy-done
  292.9 0.0 all-reduce.5.cloned.1.call-update
  292.9 0.1 collective-permute-start
  293.0 1.7 collective-permute-start.1
  294.7 1.2 collective-permute-done
  296.0 0.1 collective-permute-done.1
  296.0 75.3 %all-reduce.5.cloned.1.call-done = f32[1024,256]{1,0:T(8,128)} async-done(((f32[1024,256]{1,0:T(8,128)}), f32[1024,256]{1,0:T(8,128)}) %all-reduce.5.cloned.1.call-update) | async-done | bytes 1048592 | tf_op jit(solution)/shard_map/psum | solution.py:65
  371.3 2.5 fusion.25
  (4 shorter events, 0.0 us)
Async XLA Ops:
  7.2 215.5 %all-reduce.3.cloned.1.call-start = ((), (), s32[]{:S(2)}) async-start(), calls=%async_computation | async-start | bytes 12582912 | tf_op jit(solution)/shard_map/psum | solution.py:54
  9.3 9.4 %copy-start.1 = (bf16[1024,256]{1,0:T(8,128)(2,1)S(1)}, bf16[1024,256]{1,0:T(8,128)(2,1)}, u32[]{:S(2)}) copy-start(bf16[1024,256]{1,0:T(8,128)(2,1)} %param.7) | copy-start | bytes 1572868
  100.1 271.2 %all-reduce.5.cloned.1.call-start = ((), (), s32[]{:S(2)}) async-start(), calls=%async_computation.1 | async-start | bytes 2097152 | tf_op jit(solution)/shard_map/psum | solution.py:65
  291.9 1.0 copy-start
  292.9 3.0 collective-permute-start
  293.0 3.0 collective-permute-start.1
Sparse Core Ops, SparseCore 0:
  100.3 122.3 all-reduce.2
  293.1 78.2 all-reduce.4
where the time goes:
time: 381 us
  waiting for transfers between devices  199 us (52%)
  other arithmetic  87.5 us (23%)
  matrix products  46.8 us (12%)
  local copies, waits for them, and re-layouts  30.7 us (8%)
  between operations  14.7 us (4%)
    psum x1, waiting for transfers between devices, on_device(): grad_whole = lax.psum(grad_part, 'step')  122 us
    psum x1, waiting for transfers between devices, on_device(): grad_v = lax.psum(grad_v_part, 'svc')  75.3 us
    scatter-add x1, other arithmetic, on_device(): jnp.zeros((serv_blocks, 128, width), jnp.float32).at[row_list]  47.2 us
    scatter-add x1, other arithmetic, on_device(): jnp.zeros((time_blocks, 128, width), jnp.float32).at[col_list]  29.8 us
    dot_general x1, matrix products, on_device(): jnp.einsum('nij,nir->njr', errors_two, left_blocks, preferred_element_typ...  23.5 us
    dot_general x1, matrix products, on_device(): jnp.einsum('nij,njr->nir', errors, right_blocks, preferred_element_type=j...  23.4 us
    gather x1, local copies, waits for them, and re-layouts, on_device(): errors = residual(u_tiles[row_list])  9.38 us
    gather x1, local copies, waits for them, and re-layouts, on_device(): left_blocks = new_tiles[row_list]  9.32 us
  transfers between devices with their start and end apart: 4, of which 4 were waited for; matrix products, arithmetic and copies ran while one was open for 0% of the time, Pallas kernels for 0%

commit v1 on v0

v1 whole, which is shorter than its diff:
```python
import functools

import jax
import jax.numpy as jnp
from jax import lax
from jax.experimental import pallas as pl
from jax.experimental.pallas import tpu as pltpu
from jax.sharding import PartitionSpec as P

step_u = 0.03
step_v = 0.02
ridge = 0.1
smooth = 20.0

f32, bf16, i32, i16 = jnp.float32, jnp.bfloat16, jnp.int32, jnp.int16
B = 128
PAD = 16
TOP = 32000.0
ROWS_BY_ROWS = (((1,), (1,)), ((), ()))
COLS_BY_COLS = (((0,), (0,)), ((), ()))

SMEM = pl.BlockSpec(memory_space=pltpu.SMEM)
VMEM = pl.BlockSpec(memory_space=pltpu.VMEM)
ANY = pl.BlockSpec(memory_space=pl.ANY)


def params():
    return pltpu.CompilerParams(vmem_limit_bytes=40 * 2**20)


def encode(x):
    rows, width = x.shape
    group = min(rows, B)
    line = lax.broadcasted_iota(i32, (PAD, width), 0)
    powers = jnp.zeros((PAD, width), f32)
    parts = []
    for g in range(rows // group):
        part = x[g * group : (g + 1) * group]
        top = jnp.max(jnp.abs(part), axis=0, keepdims=True)
        power = jnp.ceil(jnp.log2(jnp.maximum(top, 1e-30)))
        parts.append(jnp.round(part * (jnp.exp2(-power) * TOP)))
        powers = jnp.where(line == g, power, powers)
    return [p.astype(i32).astype(i16) for p in parts], powers.astype(i32).astype(i16)


def store_code(ref, x):
    parts, powers = encode(x)
    group = parts[0].shape[0]
    for g, part in enumerate(parts):
        ref[g * group : (g + 1) * group, :] = part
    ref[x.shape[0] :, :] = powers


def decode(ref, g, group):
    rows = ref.shape[0] - PAD
    powers = ref[rows:, :].astype(i32).astype(f32)[g : g + 1]
    return ref[g * group : (g + 1) * group, :].astype(i32).astype(f32) * (
        jnp.exp2(powers) * (1.0 / TOP)
    )


def fetch(slots, values, dense, sem, first, count, across):
    def go(i, started):
        slot = slots[first * across + i]

        @pl.when(slot >= 0)
        def _():
            row = pl.multiple_of((i // across) * B, B)
            pltpu.make_async_copy(
                values.at[slot], dense.at[lax.rem(i, across), pl.ds(row, B)], sem
            ).start()

        return started + (slot >= 0).astype(i32)

    return lax.fori_loop(0, count * across, go, jnp.int32(0), unroll=across)


def drain(started, values, dense, sem):
    def wait(_, c):
        pltpu.make_async_copy(values.at[0], dense.at[0, pl.ds(0, B)], sem).wait()
        return c

    lax.fori_loop(0, started, wait, 0)


def residual(left, v_ref, dense, err, slots, first, count, across):
    wide = min(2, across)
    for t in range(0, across, wide):
        predicted = lax.dot_general(
            left, v_ref[t * B : (t + wide) * B, :], ROWS_BY_ROWS, preferred_element_type=f32
        )
        for r in range(count):
            rows = slice(r * B, (r + 1) * B)
            for c in range(t, t + wide):
                live = slots[(first + r) * across + c] >= 0
                gap = predicted[rows, (c - t) * B : (c - t + 1) * B] - dense[c, rows, :].astype(f32)
                err[rows, c * B : (c + 1) * B] = jnp.where(live, gap, 0.0).astype(bf16)


def u_body(first, count, down, across, opening, *refs):
    if opening:
        row_ref, col_ref, live_ref, u_hbm, v_ref, values, out, slots, dense, err, left, sem, usem = refs
    else:
        slots, u_hbm, v_ref, values, out, dense, err, left, sem, usem = refs
    load = pltpu.make_async_copy(u_hbm.at[pl.ds(first * B, count * B)], left, usem)
    load.start()
    if opening:

        def clear(i, c):
            slots[i] = jnp.int32(-1)
            return c

        lax.fori_loop(0, down * across, clear, 0, unroll=8)

        def enter(k, c):
            slots[row_ref[k] * across + col_ref[k]] = k
            return c

        lax.fori_loop(0, live_ref[0], enter, 0)
    started = fetch(slots, values, dense, sem, first, count, across)
    load.wait()
    drain(started, values, dense, sem)
    residual(left[...], v_ref, dense, err, slots, first, count, across)
    out[...] = jnp.dot(err[...], v_ref[...], preferred_element_type=f32)


def work_scratch(count, across, width):
    return [
        pltpu.VMEM((across, count * B, B), bf16),
        pltpu.VMEM((count * B, across * B), bf16),
        pltpu.VMEM((count * B, width), bf16),
        pltpu.SemaphoreType.DMA,
        pltpu.SemaphoreType.DMA,
    ]


def u_pass(first, count, down, across, width, index, u, v, values):
    opening = isinstance(index, tuple)
    out = [jax.ShapeDtypeStruct((count * B, width), f32)]
    out_specs = [VMEM]
    if opening:
        out.append(jax.ShapeDtypeStruct((down * across,), i32))
        out_specs.append(SMEM)
    ins = list(index) if opening else [index]
    return pl.pallas_call(
        functools.partial(u_body, first, count, down, across, opening),
        out_shape=out,
        in_specs=[SMEM] * len(ins) + [ANY, VMEM, ANY],
        out_specs=out_specs,
        scratch_shapes=work_scratch(count, across, width),
        compiler_params=params(),
        cost_estimate=pl.CostEstimate(
            flops=4 * count * B * across * B * width, bytes_accessed=count * B * width * 6, transcendentals=0
        ),
        name=f"u_pass_{first}",
    )(*ins, u, v, values)


def sum_body(place, own, other, mine_out, rest_out):
    half = own.shape[0] // 2
    core = place[0]
    for out, at in ((mine_out, core), (rest_out, 1 - core)):
        rows = pl.ds(pl.multiple_of(at * half, 8), half)
        store_code(out, own[rows, :] + other[rows, :])


def chip_sum(place, own, other):
    rows, width = own.shape
    code = jax.ShapeDtypeStruct((rows // 2 + PAD, width), i16)
    return pl.pallas_call(
        sum_body,
        out_shape=[code, code],
        in_specs=[SMEM, VMEM, VMEM],
        out_specs=[VMEM, VMEM],
        compiler_params=params(),
        cost_estimate=pl.CostEstimate(flops=rows * width * 8, bytes_accessed=rows * width * 10, transcendentals=0),
        name="chip_sum",
    )(place, own, other)


def again_body(mine, rest, mine_in, rest_in, mine_out, rest_out):
    rows = mine.shape[0] - PAD
    group = min(rows, B)
    for out, a, b in ((mine_out, mine, mine_in), (rest_out, rest, rest_in)):
        whole = [decode(a, g, group) + decode(b, g, group) for g in range(rows // group)]
        store_code(out, jnp.concatenate(whole, axis=0))


def chip_sum_again(*codes):
    code = jax.ShapeDtypeStruct(codes[0].shape, i16)
    return pl.pallas_call(
        again_body,
        out_shape=[code, code],
        in_specs=[VMEM] * 4,
        out_specs=[VMEM, VMEM],
        compiler_params=params(),
        name="chip_sum_again",
    )(*codes)


def v_body(first, count, across, opening, shards, *refs):
    slots, place, u_hbm, v_ref, values, mine, rest, mine_in, rest_in = refs[:9]
    refs = refs[9:]
    if not opening:
        before, _ = refs[:2]
        refs = refs[2:]
    new_out, refs = refs[0], refs[1:]
    if shards:
        own_out, sent, refs = refs[0], refs[1:shards], refs[shards:]
    else:
        total, refs = refs[0], refs[1:]
    dense, err, left, sem, usem = refs[:5]
    load = pltpu.make_async_copy(u_hbm.at[pl.ds(first * B, count * B)], left, usem)
    load.start()
    started = fetch(slots, values, dense, sem, first, count, across)
    load.wait()
    half = count * B // 2
    group = min(half, B)
    for a, b, at in ((mine, mine_in, place[0]), (rest, rest_in, 1 - place[0])):
        for g in range(half // group):
            rows = pl.ds(pl.multiple_of(at * half + g * group, 16), group)
            old = left[rows, :].astype(f32)
            grad = decode(a, g, group) + decode(b, g, group)
            left[rows, :] = (old - step_u * (grad + ridge * old)).astype(bf16)
    save = pltpu.make_async_copy(left, new_out.at[pl.ds(first * B, count * B)], usem)
    save.start()
    drain(started, values, dense, sem)
    residual(left[...], v_ref, dense, err, slots, first, count, across)
    part = lax.dot_general(left[...], err[...], COLS_BY_COLS, preferred_element_type=f32)
    if not opening:
        part = part + before[...]
    if not shards:
        total[...] = part
    else:
        turned = refs[5]
        turned[...] = part.T
        rows = turned.shape[0] // shards
        here = place[1]
        own_out[...] = turned[pl.ds(pl.multiple_of(here * rows, 8), rows), :]
        for d in range(1, shards):
            there = jnp.bitwise_xor(here, d)
            store_code(sent[d - 1], turned[pl.ds(pl.multiple_of(there * rows, 8), rows), :])
    save.wait()


def v_pass(first, count, across, slots, place, u, v, values, codes, before, shards):
    width = u.shape[1]
    times = v.shape[0]
    opening = before is None
    ins = [slots, place, u, v, values, *codes]
    in_specs = [SMEM, SMEM, ANY, VMEM, ANY] + [VMEM] * 4
    aliases = {}
    out = [jax.ShapeDtypeStruct(u.shape, bf16)]
    out_specs = [ANY]
    if not opening:
        ins += [before[1], before[0]]
        in_specs += [VMEM, ANY]
        aliases = {10: 0}
    scratch = work_scratch(count, across, width)
    if shards:
        rows = times // shards
        out.append(jax.ShapeDtypeStruct((rows, width), f32))
        out += [jax.ShapeDtypeStruct((rows + PAD, width), i16)] * (shards - 1)
        out_specs += [VMEM] * shards
        scratch.append(pltpu.VMEM((times, width), f32))
    else:
        out.append(jax.ShapeDtypeStruct((width, times), f32))
        out_specs.append(VMEM)
    return pl.pallas_call(
        functools.partial(v_body, first, count, across, opening, shards),
        out_shape=out,
        in_specs=in_specs,
        out_specs=out_specs,
        input_output_aliases=aliases,
        scratch_shapes=scratch,
        compiler_params=params(),
        cost_estimate=pl.CostEstimate(
            flops=4 * count * B * across * B * width, bytes_accessed=count * B * width * 6, transcendentals=0
        ),
        name=f"v_pass_{first}",
    )(*ins)


def last_body(place, v_ref, low, high, own, *refs):
    codes, out, wide = refs[:-2], refs[-2], refs[-1]
    times = v_ref.shape[0]
    rows = out.shape[0]
    group = min(rows, B)
    wide[:PAD, :] = low[...]
    wide[PAD : PAD + times, :] = v_ref[...]
    wide[PAD + times :, :] = high[...]
    start = pl.multiple_of(place[1] * rows, 16)
    window = wide[pl.ds(start, rows + 2 * PAD), :].astype(f32)
    old = window[PAD : PAD + rows]
    lap = 2.0 * old - window[PAD - 1 : PAD - 1 + rows] - window[PAD + 1 : PAD + 1 + rows]
    for g in range(rows // group):
        at = slice(g * group, (g + 1) * group)
        grad = own[at, :]
        for code in codes:
            grad = grad + decode(code, g, group)
        out[at, :] = (old[at] - step_v * (grad + ridge * old[at] + smooth * lap[at])).astype(bf16)


def last_step(place, v, low, high, own, codes):
    return pl.pallas_call(
        last_body,
        out_shape=jax.ShapeDtypeStruct(own.shape, bf16),
        in_specs=[SMEM] + [VMEM] * (4 + len(codes)),
        out_specs=VMEM,
        scratch_shapes=[pltpu.VMEM((v.shape[0] + 2 * PAD, v.shape[1]), bf16)],
        compiler_params=params(),
        name="last_step",
    )(place, v, low, high, own, *codes)


def join_body(place, *refs):
    out = refs[-1]
    rows = refs[0].shape[0]
    for d, part in enumerate(refs[:-1]):
        there = jnp.bitwise_xor(place[1], d)
        out[pl.ds(pl.multiple_of(there * rows, 16), rows), :] = part[...]


def join(place, parts):
    rows, width = parts[0].shape
    return pl.pallas_call(
        join_body,
        out_shape=jax.ShapeDtypeStruct((rows * len(parts), width), bf16),
        in_specs=[SMEM] + [VMEM] * len(parts),
        out_specs=VMEM,
        compiler_params=params(),
        name="join",
    )(place, *parts)


def swap(x, axis, mask):
    return lax.ppermute(x, axis, [(i, i ^ mask) for i in range(lax.axis_size(axis))])


def shift(x, axis, by):
    n = lax.axis_size(axis)
    return lax.ppermute(x, axis, [(i, (i + by) % n) for i in range(n)])


def chunks_of(down):
    unit = down // 8
    sizes = [unit, 2 * unit, 2 * unit, 2 * unit]
    sizes.append(down - sum(sizes))
    return [(sum(sizes[:i]), size) for i, size in enumerate(sizes)]


def on_device(u, v, block_rows, block_cols, block_counts, block_values):
    width = u.shape[1]
    down, across = u.shape[0] // B, v.shape[0] // B
    values = block_values[0, 0]
    steps, peers = lax.axis_size("step"), lax.axis_size("svc")
    place = jnp.stack([lax.axis_index("step") % 2, lax.axis_index("svc")]).astype(i32)
    low = shift(v[-PAD:], "step", 1)
    high = shift(v[:PAD], "step", -1)
    chunks = chunks_of(down)
    index = (block_rows[0, 0], block_cols[0, 0], block_counts[0])
    codes = []
    for first, count in chunks:
        got = u_pass(first, count, down, across, width, index, u, v, values)
        if first == 0:
            index = got[1]
        mine, rest = chip_sum(place, got[0], swap(got[0], "step", 1))
        mask = 2
        while True:
            mine_in = swap(mine, "step", mask)
            rest_in = swap(mine_in, "step", 1)
            mask *= 2
            if mask >= steps:
                break
            mine, rest = chip_sum_again(mine, rest, mine_in, rest_in)
        codes.append((mine, rest, mine_in, rest_in))
    before = None
    for i, (first, count) in enumerate(chunks):
        shards = peers if i == len(chunks) - 1 else 0
        before = v_pass(first, count, across, index, place, u, v, values, codes[i], before, shards)
    new_services, own, sent = before[0], before[1], before[2:]
    arrived = [swap(x, "svc", d + 1) for d, x in enumerate(sent)]
    part = last_step(place, v, low, high, own, arrived)
    parts = [part] + [swap(part, "svc", d) for d in range(1, peers)]
    return new_services, join(place, parts)


def solution(mesh):
    return jax.shard_map(
        on_device,
        mesh=mesh,
        in_specs=(
            P("svc", None),
            P("step", None),
            P("svc", "step", None),
            P("svc", "step", None),
            P("svc", "step"),
            P("svc", "step", None, None, None),
        ),
        out_specs=(P("svc", None), P("step", None)),
        check_vma=False,
    )
```

time: 381 us -> 148 us (0.39)
  waiting for transfers between devices: 199 us -> 36.4 us
  other arithmetic: 87.5 us -> 0.08 us
  Pallas kernels: 0 us -> 70.2 us
  matrix products: 46.8 us -> 0 us
  starting transfers between devices: 2.05 us -> 32.4 us
  local copies, waits for them, and re-layouts: 30.7 us -> 6.75 us
  between operations: 14.7 us -> 1.58 us
    psum x2 -> x0, waiting for transfers between devices: 198 us -> none  [the longest x1 122 us: on_device(): grad_whole = lax.psum(grad_part, 'step')]
    scatter-add x2 -> x0, other arithmetic: 77.1 us -> none  [the longest x1 47.2 us: on_device(): jnp.zeros((serv_blocks, 128, width), jnp.float32).at[row_list]]
    pallas_call x0 -> x17, Pallas kernels: none -> 70.2 us  [the longest x5 31.5 us: u_pass(): pl.pallas_call(functools.partial(u_body, first, count, down, across, open...]
    dot_general x2 -> x0, matrix products: 46.8 us -> none  [the longest x1 23.5 us: on_device(): jnp.einsum('nij,nir->njr', errors_two, left_blocks, preferred_element_typ...]
    ppermute x2 -> x31, waiting for transfers between devices: 1.3 us -> 36.4 us  [the longest x29 36.4 us: swap(): lax.ppermute(x, axis, [(i, i ^ mask) for i in range(lax.axis_size(axis))])]
    ppermute x2 -> x31, starting transfers between devices: 1.79 us -> 32.4 us  [the longest x29 30.6 us: swap(): lax.ppermute(x, axis, [(i, i ^ mask) for i in range(lax.axis_size(axis))])]
    gather x3 -> x0, local copies, waits for them, and re-layouts: 26.2 us -> none  [the longest x1 9.38 us: on_device(): errors = residual(u_tiles[row_list])]
    convert_element_type x3 -> x0, other arithmetic: 9.05 us -> none  [the longest x1 6.54 us: on_device(): (old_u - step_u * (grad_whole + ridge * old_u)).astype(jnp.bfloat16)]
  transfers between devices with their start and end apart: 4 -> 31, of which waited for: 4 -> 8; matrix products, arithmetic and copies ran while one was open for 0% -> 0% of each run, Pallas kernels for 0% -> 34%
where the time goes in v1:
time: 148 us; the launch traced here: 147 us
  Pallas kernels  70.2 us (47%)
  waiting for transfers between devices  36.4 us (25%)
  starting transfers between devices  32.4 us (22%)
  local copies, waits for them, and re-layouts  6.75 us (5%)
  between operations  1.58 us (1%)
    ppermute x29, waiting for transfers between devices, swap(): lax.ppermute(x, axis, [(i, i ^ mask) for i in range(lax.axis_size(axis))])  36.4 us
    pallas_call x5, Pallas kernels, u_pass(): pl.pallas_call(functools.partial(u_body, first, count, down, across, open...  31.5 us
    ppermute x29, starting transfers between devices, swap(): lax.ppermute(x, axis, [(i, i ^ mask) for i in range(lax.axis_size(axis))])  30.6 us
    pallas_call x5, Pallas kernels, v_pass(): pl.pallas_call(functools.partial(v_body, first, count, across, opening, s...  27.1 us
    pallas_call x5, Pallas kernels, chip_sum(): pl.pallas_call(sum_body, out_shape=[code, code], in_specs=[SMEM, VMEM, VM...  9.4 us
    unnamed x22, local copies, waits for them, and re-layouts  6.75 us
  transfers between devices with their start and end apart: 31, of which 8 were waited for; matrix products, arithmetic and copies ran while one was open for 0% of the time, Pallas kernels for 34%

profile of v1, /device:TPU:0, one launch (start us, length us, event | category | flops | bytes accessed | tf_op | source)
XLA Modules:
  0.0 147.3 jit_solution(7129804038644478136)
XLA Ops:
  1.3 2.4 %copy-done = bf16[1,1,154,128,128]{4,3,2,1,0:T(8,128)(2,1)S(1)} copy-done((bf16[1,1,154,128,128]{4,3,2,1,0:T(8,128)(2,1)S(1)}, bf16[1,1,154,128,128]{4,3,2,1,0:T(8,128)(2,1)}, u32[]{:S(2)}) %copy-start) | copy-done | bytes 5046296
  3.7 1.9 %copy-done.2 = bf16[6144,256]{1,0:T(8,128)(2,1)S(1)} copy-done((bf16[6144,256]{1,0:T(8,128)(2,1)S(1)}, bf16[6144,256]{1,0:T(8,128)(2,1)}, u32[]{:S(2)}) %copy-start.2) | copy-done | bytes 3145752
  5.6 1.0 copy-done.5
  6.6 0.7 copy-done.7
  7.3 0.7 copy-done.8
  8.0 6.6 %u_pass_0.1 = (f32[768,256]{1,0:T(8,128)}, s32[384]{0:T(512)S(1)}) custom-call(s32[154]{0:T(256)S(1)} %bitcast.19, s32[154]{0:T(256)S(1)} %bitcast.20, s32[1]{0:T(128)} %bitcast.6.refs_2_, bf16[6144,256]{1,0:T(8,128)(2,1)S(1)} %copy-done.2, bf16[1024,256]{1,0:T(8,128)(2,1)S(1)} %copy-done.5, bf16[154,128,128]{2,1,0:T(8,128)(2,1)S(1)} %bitcast.7), custom_call_target="tpu_custom_call" | custom-call | flops 805306368 | bytes 1179648 | tf_op jit(solution)/shard_map/u_pass_0/pallas_call | solution.py:145
  14.7 7.9 %u_pass_6.1.own = f32[1536,256]{1,0:T(8,128)} custom-call(s32[384]{0:T(512)S(1)} %get-tuple-element.31.refs_0_, bf16[6144,256]{1,0:T(8,128)(2,1)S(1)} %copy-done.3, bf16[1024,256]{1,0:T(8,128)(2,1)S(1)} %copy-done.5, bf16[154,128,128]{2,1,0:T(8,128)(2,1)S(1)} %bitcast.8), custom_call_target="tpu_custom_call" | custom-call | flops 1610612736 | bytes 2359296 | tf_op jit(solution)/shard_map/u_pass_6/pallas_call | solution.py:145
  22.7 7.4 %u_pass_18.1.own = f32[1536,256]{1,0:T(8,128)} custom-call(s32[384]{0:T(512)S(1)} %get-tuple-element.31.refs_0_, bf16[6144,256]{1,0:T(8,128)(2,1)S(1)} %copy-done.3, bf16[1024,256]{1,0:T(8,128)(2,1)S(1)} %copy-done.5, bf16[154,128,128]{2,1,0:T(8,128)(2,1)S(1)} %bitcast.9), custom_call_target="tpu_custom_call" | custom-call | flops 1610612736 | bytes 2359296 | tf_op jit(solution)/shard_map/u_pass_18/pallas_call | solution.py:145
  30.5 5.7 %u_pass_30.1.own = f32[1536,256]{1,0:T(8,128)S(1)} custom-call(s32[384]{0:T(512)S(1)} %get-tuple-element.31.refs_0_, bf16[6144,256]{1,0:T(8,128)(2,1)S(1)} %copy-done.3, bf16[1024,256]{1,0:T(8,128)(2,1)S(1)} %copy-done.5, bf16[154,128,128]{2,1,0:T(8,128)(2,1)S(1)} %bitcast.10), custom_call_target="tpu_custom_call" | custom-call | flops 1610612736 | bytes 2359296 | tf_op jit(solution)/shard_map/u_pass_30/pallas_call | solution.py:145
  36.8 3.8 %u_pass_42.1.own = f32[768,256]{1,0:T(8,128)S(1)} custom-call(s32[384]{0:T(512)S(1)} %get-tuple-element.31.refs_0_, bf16[6144,256]{1,0:T(8,128)(2,1)S(1)} %copy-done.3, bf16[1024,256]{1,0:T(8,128)(2,1)S(1)} %copy-done.5, bf16[154,128,128]{2,1,0:T(8,128)(2,1)S(1)} %bitcast.11), custom_call_target="tpu_custom_call" | custom-call | flops 805306368 | bytes 1179648 | tf_op jit(solution)/shard_map/u_pass_42/pallas_call | solution.py:145
  40.8 2.3 %chip_sum.8 = (s16[784,256]{1,0:T(8,128)(2,1)S(1)}, s16[784,256]{1,0:T(8,128)(2,1)S(1)}) custom-call(s32[2]{0:T(128)S(1)} %pad_add_fusion.place.refs_1_, f32[1536,256]{1,0:T(8,128)} %u_pass_6.1.own, f32[1536,256]{1,0:T(8,128)} %collective-permute-done.9.other), custom_call_target="tpu_custom_call" | custom-call | flops 3145728 | bytes 3932160 | tf_op jit(solution)/shard_map/chip_sum/pallas_call | solution.py:170
  43.1 0.6 collective-permute-start.10
  43.7 2.5 %chip_sum.7 = (s16[784,256]{1,0:T(8,128)(2,1)S(1)}, s16[784,256]{1,0:T(8,128)(2,1)S(1)}) custom-call(s32[2]{0:T(128)S(1)} %pad_add_fusion.place.refs_1_, f32[1536,256]{1,0:T(8,128)} %u_pass_18.1.own, f32[1536,256]{1,0:T(8,128)} %collective-permute-done.6.other), custom_call_target="tpu_custom_call" | custom-call | flops 3145728 | bytes 3932160 | tf_op jit(solution)/shard_map/chip_sum/pallas_call | solution.py:170
  46.2 1.3 collective-permute-start.7
  47.5 1.7 %chip_sum.6 = (s16[784,256]{1,0:T(8,128)(2,1)S(1)}, s16[784,256]{1,0:T(8,128)(2,1)S(1)}) custom-call(s32[2]{0:T(128)S(1)} %pad_add_fusion.place.refs_1_, f32[1536,256]{1,0:T(8,128)S(1)} %u_pass_30.1.own, f32[1536,256]{1,0:T(8,128)} %collective-permute-done.3.other), custom_call_target="tpu_custom_call" | custom-call | flops 3145728 | bytes 3932160 | tf_op jit(solution)/shard_map/chip_sum/pallas_call | solution.py:170
  49.3 1.1 collective-permute-start.4
  50.4 1.6 %chip_sum.9 = (s16[400,256]{1,0:T(8,128)(2,1)S(1)}, s16[400,256]{1,0:T(8,128)(2,1)S(1)}) custom-call(s32[2]{0:T(128)S(1)} %pad_add_fusion.place.refs_1_, f32[768,256]{1,0:T(8,128)} %get-tuple-element.40.own, f32[768,256]{1,0:T(8,128)} %collective-permute-done.12.other), custom_call_target="tpu_custom_call" | custom-call | flops 1572864 | bytes 1966080 | tf_op jit(solution)/shard_map/chip_sum/pallas_call | solution.py:170
  51.9 1.1 collective-permute-start.13
  53.0 2.3 %collective-permute-done.10.refs_7_ = s16[784,256]{1,0:T(8,128)(2,1)S(1)} collective-permute-done((s16[784,256]{1,0:T(8,128)(2,1)S(1)}, s16[784,256]{1,0:T(8,128)(2,1)S(1)}, u32[]{:S(2)}, u32[]{:S(2)}) %collective-permute-start.10) | collective-permute-done | bytes 401440 | tf_op jit(solution)/shard_map/ppermute | solution.py:337
  55.3 1.3 chip_sum.5
  56.6 0.6 collective-permute-start.1
  57.2 19.7 %collective-permute-done.13.refs_7_ = s16[400,256]{1,0:T(8,128)(2,1)S(1)} collective-permute-done((s16[400,256]{1,0:T(8,128)(2,1)S(1)}, s16[400,256]{1,0:T(8,128)(2,1)S(1)}, u32[]{:S(2)}, u32[]{:S(2)}) %collective-permute-start.13) | collective-permute-done | bytes 204832 | tf_op jit(solution)/shard_map/ppermute | solution.py:337
  76.9 0.5 collective-permute-start.8
  77.5 3.4 %collective-permute-done.1.refs_7_ = s16[400,256]{1,0:T(8,128)(2,1)S(1)} collective-permute-done((s16[400,256]{1,0:T(8,128)(2,1)S(1)}, s16[400,256]{1,0:T(8,128)(2,1)S(1)}, u32[]{:S(2)}, u32[]{:S(2)}) %collective-permute-start.1) | collective-permute-done | bytes 204832 | tf_op jit(solution)/shard_map/ppermute | solution.py:337
  80.9 3.7 %v_pass_0.1 = (bf16[6144,256]{1,0:T(8,128)(2,1)}, f32[256,1024]{1,0:T(8,128)S(1)}) custom-call(s32[384]{0:T(512)S(1)} %get-tuple-element.31.refs_0_, s32[2]{0:T(128)S(1)} %pad_add_fusion.place.refs_1_, bf16[6144,256]{1,0:T(8,128)(2,1)S(1)} %copy-done.4, bf16[1024,256]{1,0:T(8,128)(2,1)S(1)} %copy-done.6, bf16[154,128,128]{2,1,0:T(8,128)(2,1)S(1)} %bitcast.14, ...), custom_call_target="tpu_custom_call" | custom-call | flops 805306368 | bytes 1179648 | tf_op jit(solution)/shard_map/v_pass_0/pallas_call | solution.py:269
  84.6 6.9 %v_pass_6.1 = (bf16[6144,256]{1,0:T(8,128)(2,1)}, f32[256,1024]{1,0:T(8,128)S(1)}) custom-call(s32[384]{0:T(512)S(1)} %get-tuple-element.31.refs_0_, s32[2]{0:T(128)S(1)} %pad_add_fusion.place.refs_1_, bf16[6144,256]{1,0:T(8,128)(2,1)S(1)} %copy-done.4, bf16[1024,256]{1,0:T(8,128)(2,1)S(1)} %copy-done.6, ...), custom_call_target="tpu_custom_call", output_to_operand_aliasing={{0}: (10, {})} | custom-call | flops 1610612736 | bytes 2359296 | tf_op jit(solution)/shard_map/v_pass_6/pallas_call | solution.py:269
  91.5 6.4 %v_pass_18.1 = (bf16[6144,256]{1,0:T(8,128)(2,1)}, f32[256,1024]{1,0:T(8,128)S(1)}) custom-call(s32[384]{0:T(512)S(1)} %get-tuple-element.31.refs_0_, s32[2]{0:T(128)S(1)} %pad_add_fusion.place.refs_1_, bf16[6144,256]{1,0:T(8,128)(2,1)S(1)} %copy-done.4, bf16[1024,256]{1,0:T(8,128)(2,1)S(1)} %copy-done.6, ...), custom_call_target="tpu_custom_call", output_to_operand_aliasing={{0}: (10, {})} | custom-call | flops 1610612736 | bytes 2359296 | tf_op jit(solution)/shard_map/v_pass_18/pallas_call | solution.py:269
  97.9 6.1 %v_pass_30.1 = (bf16[6144,256]{1,0:T(8,128)(2,1)}, f32[256,1024]{1,0:T(8,128)S(1)}) custom-call(s32[384]{0:T(512)S(1)} %get-tuple-element.31.refs_0_, s32[2]{0:T(128)S(1)} %pad_add_fusion.place.refs_1_, bf16[6144,256]{1,0:T(8,128)(2,1)S(1)} %copy-done.4, bf16[1024,256]{1,0:T(8,128)(2,1)S(1)} %copy-done.6, ...), custom_call_target="tpu_custom_call", output_to_operand_aliasing={{0}: (10, {})} | custom-call | flops 1610612736 | bytes 2359296 | tf_op jit(solution)/shard_map/v_pass_30/pallas_call | solution.py:269
  104.0 4.0 %v_pass_42.1 = (bf16[6144,256]{1,0:T(8,128)(2,1)}, f32[128,256]{1,0:T(8,128)S(1)}, s16[144,256]{1,0:T(8,128)(2,1)S(1)}, s16[144,256]{1,0:T(8,128)(2,1)S(1)}, s16...) custom-call(s32[384]{0:T(512)S(1)} %get-tuple-element.31.refs_0_, ...), custom_call_target="tpu_custom_call", output_to_operand_aliasing={{0}: (10, {})} | custom-call | flops 805306368 | bytes 1179648 | tf_op jit(solution)/shard_map/v_pass_42/pallas_call | solution.py:269
  108.1 0.7 collective-permute-start.17
  108.8 1.6 %collective-permute-start.15 = (bf16[16,256]{1,0:T(8,128)(2,1)S(1)}, bf16[16,256]{1,0:T(8,128)(2,1)S(1)}, u32[]{:S(2)}, u32[]{:S(2)}) collective-permute-start(bf16[16,256]{1,0:T(8,128)(2,1)S(1)} %get-tuple-element.61), channel_id=1, source_target_pairs={{0,1},{1,2},{2,3},{3,0},{4,5},{5,6},{6,7},{7,4},{8,9},{9,10},{10,1... | collective-permute-start | bytes 24584 | tf_op jit(solution)/shard_map/ppermute | solution.py:342
  110.5 2.8 %collective-permute-start.19 = (s16[144,256]{1,0:T(8,128)(2,1)S(1)}, s16[144,256]{1,0:T(8,128)(2,1)S(1)}, u32[]{:S(2)}, u32[]{:S(2)}) collective-permute-start(s16[144,256]{1,0:T(8,128)(2,1)S(1)} %get-tuple-element.55), channel_id=1, source_target_pairs={{0,12},{4,8},{8,4},{12,0},{16,28},{20,24},{24,20},{28,16},{1,13},{... | collective-permute-start | bytes 221192 | tf_op jit(solution)/shard_map/ppermute | solution.py:337
  113.4 3.5 %collective-permute-start.20 = (s16[144,256]{1,0:T(8,128)(2,1)S(1)}, s16[144,256]{1,0:T(8,128)(2,1)S(1)}, u32[]{:S(2)}, u32[]{:S(2)}) collective-permute-start(s16[144,256]{1,0:T(8,128)(2,1)S(1)} %get-tuple-element.56), channel_id=1, source_target_pairs={{0,16},{4,20},{8,24},{12,28},{16,0},{20,4},{24,8},{28,12},{1,17},{... | collective-permute-start | bytes 221192 | tf_op jit(solution)/shard_map/ppermute | solution.py:337
  116.9 3.7 %collective-permute-start.22 = (s16[144,256]{1,0:T(8,128)(2,1)S(1)}, s16[144,256]{1,0:T(8,128)(2,1)S(1)}, u32[]{:S(2)}, u32[]{:S(2)}) collective-permute-start(s16[144,256]{1,0:T(8,128)(2,1)S(1)} %get-tuple-element.58), channel_id=1, source_target_pairs={{0,24},{4,28},{8,16},{12,20},{16,8},{20,12},{24,0},{28,4},{1,25},{... | collective-permute-start | bytes 221192 | tf_op jit(solution)/shard_map/ppermute | solution.py:337
  120.5 1.1 collective-permute-start.23
  121.7 4.9 %collective-permute-done.21.refs_4_ = s16[144,256]{1,0:T(8,128)(2,1)S(1)} collective-permute-done((s16[144,256]{1,0:T(8,128)(2,1)S(1)}, s16[144,256]{1,0:T(8,128)(2,1)S(1)}, u32[]{:S(2)}, u32[]{:S(2)}) %collective-permute-start.21) | collective-permute-done | bytes 73760 | tf_op jit(solution)/shard_map/ppermute | solution.py:337
  126.6 1.1 collective-permute-done.23.refs_6_
  127.7 0.8 last_step.1.refs_0_
  128.5 0.8 collective-permute-start.24
  129.2 3.2 %collective-permute-start.25 = (bf16[128,256]{1,0:T(8,128)(2,1)S(1)}, bf16[128,256]{1,0:T(8,128)(2,1)S(1)}, u32[]{:S(2)}, u32[]{:S(2)}) collective-permute-start(bf16[128,256]{1,0:T(8,128)(2,1)S(1)} %last_step.1.refs_0_), channel_id=1, source_target_pairs={{0,8},{4,12},{8,0},{12,4},{16,24},{20,28},{24,16},{28,20},{1,9},{5... | collective-permute-start | bytes 196616 | tf_op jit(solution)/shard_map/ppermute | solution.py:337
  132.5 0.9 collective-permute-start.26
  133.3 2.9 %collective-permute-start.27 = (bf16[128,256]{1,0:T(8,128)(2,1)S(1)}, bf16[128,256]{1,0:T(8,128)(2,1)S(1)}, u32[]{:S(2)}, u32[]{:S(2)}) collective-permute-start(bf16[128,256]{1,0:T(8,128)(2,1)S(1)} %last_step.1.refs_0_), channel_id=1, source_target_pairs={{0,16},{4,20},{8,24},{12,28},{16,0},{20,4},{24,8},{28,12},{1,17},{... | collective-permute-start | bytes 196616 | tf_op jit(solution)/shard_map/ppermute | solution.py:337
  136.5 2.4 %collective-permute-start.29 = (bf16[128,256]{1,0:T(8,128)(2,1)S(1)}, bf16[128,256]{1,0:T(8,128)(2,1)S(1)}, u32[]{:S(2)}, u32[]{:S(2)}) collective-permute-start(bf16[128,256]{1,0:T(8,128)(2,1)S(1)} %last_step.1.refs_0_), channel_id=1, source_target_pairs={{0,24},{4,28},{8,16},{12,20},{16,8},{20,12},{24,0},{28,4},{1,25},{... | collective-permute-start | bytes 196616 | tf_op jit(solution)/shard_map/ppermute | solution.py:337
  138.9 2.1 %collective-permute-start.30 = (bf16[128,256]{1,0:T(8,128)(2,1)S(1)}, bf16[128,256]{1,0:T(8,128)(2,1)S(1)}, u32[]{:S(2)}, u32[]{:S(2)}) collective-permute-start(bf16[128,256]{1,0:T(8,128)(2,1)S(1)} %last_step.1.refs_0_), channel_id=1, source_target_pairs={{0,28},{4,24},{8,20},{12,16},{16,12},{20,8},{24,4},{28,0},{1,29},{... | collective-permute-start | bytes 196616 | tf_op jit(solution)/shard_map/ppermute | solution.py:337
  141.0 2.9 %collective-permute-done.27.refs_4_ = bf16[128,256]{1,0:T(8,128)(2,1)S(1)} collective-permute-done((bf16[128,256]{1,0:T(8,128)(2,1)S(1)}, bf16[128,256]{1,0:T(8,128)(2,1)S(1)}, u32[]{:S(2)}, u32[]{:S(2)}) %collective-permute-start.27) | collective-permute-done | bytes 65568 | tf_op jit(solution)/shard_map/ppermute | solution.py:337
  143.9 1.3 collective-permute-done.28.refs_5_
  145.1 0.8 collective-permute-done.30.refs_7_
  146.0 1.4 join.1
  (56 shorter events, 1.8 us)
Async XLA Ops:
  1.3 2.4 %copy-start = (bf16[1,1,154,128,128]{4,3,2,1,0:T(8,128)(2,1)S(1)}, bf16[1,1,154,128,128]{4,3,2,1,0:T(8,128)(2,1)}, u32[]{:S(2)}) copy-start(bf16[1,1,154,128,128]{4,3,2,1,0:T(8,128)(2,1)} %param.11) | copy-start | bytes 15138820
  3.7 1.9 %copy-start.2 = (bf16[6144,256]{1,0:T(8,128)(2,1)S(1)}, bf16[6144,256]{1,0:T(8,128)(2,1)}, u32[]{:S(2)}) copy-start(bf16[6144,256]{1,0:T(8,128)(2,1)} %refs_2_.17) | copy-start | bytes 9437188
  5.6 1.0 copy-start.5
  6.6 0.7 copy-start.7
  7.3 0.7 copy-start.8
  8.0 6.7 %copy-start.1 = (bf16[1,1,154,128,128]{4,3,2,1,0:T(8,128)(2,1)S(1)}, bf16[1,1,154,128,128]{4,3,2,1,0:T(8,128)(2,1)}, u32[]{:S(2)}) copy-start(bf16[1,1,154,128,128]{4,3,2,1,0:T(8,128)(2,1)} %param.11) | copy-start | bytes 15138820
  8.0 6.7 %copy-start.3 = (bf16[6144,256]{1,0:T(8,128)(2,1)S(1)}, bf16[6144,256]{1,0:T(8,128)(2,1)}, u32[]{:S(2)}) copy-start(bf16[6144,256]{1,0:T(8,128)(2,1)} %refs_2_.17) | copy-start | bytes 9437188
  22.6 18.2 %collective-permute-start.9 = (f32[1536,256]{1,0:T(8,128)}, f32[1536,256]{1,0:T(8,128)}, u32[]{:S(2)}, u32[]{:S(2)}) collective-permute-start(f32[1536,256]{1,0:T(8,128)} %u_pass_6.1.own), channel_id=1, source_target_pairs={{0,1},{1,0},{2,3},{3,2},{4,5},{5,4},{6,7},{7,6},{8,9},{9,8},{10,11... | collective-permute-start | bytes 4718600 | tf_op jit(solution)/shard_map/ppermute | solution.py:337
  30.1 13.6 %collective-permute-start.6 = (f32[1536,256]{1,0:T(8,128)}, f32[1536,256]{1,0:T(8,128)}, u32[]{:S(2)}, u32[]{:S(2)}) collective-permute-start(f32[1536,256]{1,0:T(8,128)} %u_pass_18.1.own), channel_id=1, source_target_pairs={{0,1},{1,0},{2,3},{3,2},{4,5},{5,4},{6,7},{7,6},{8,9},{9,8},{10,11... | collective-permute-start | bytes 4718600 | tf_op jit(solution)/shard_map/ppermute | solution.py:337
  36.2 11.3 %collective-permute-start.3 = (f32[1536,256]{1,0:T(8,128)S(1)}, f32[1536,256]{1,0:T(8,128)}, u32[]{:S(2)}, u32[]{:S(2)}) collective-permute-start(f32[1536,256]{1,0:T(8,128)S(1)} %u_pass_30.1.own), channel_id=1, source_target_pairs={{0,1},{1,0},{2,3},{3,2},{4,5},{5,4},{6,7},{7,6},{8,9},{9,8},{10,11... | collective-permute-start | bytes 4718600 | tf_op jit(solution)/shard_map/ppermute | solution.py:337
  36.5 13.9 %collective-permute-start.12 = (f32[768,256]{1,0:T(8,128)}, f32[768,256]{1,0:T(8,128)}, u32[]{:S(2)}, u32[]{:S(2)}) collective-permute-start(f32[768,256]{1,0:T(8,128)} %get-tuple-element.40.own), channel_id=1, source_target_pairs={{0,1},{1,0},{2,3},{3,2},{4,5},{5,4},{6,7},{7,6},{8,9},{9,8},{10,11... | collective-permute-start | bytes 2359304 | tf_op jit(solution)/shard_map/ppermute | solution.py:337
  40.6 14.6 %collective-permute-start = (f32[768,256]{1,0:T(8,128)S(1)}, f32[768,256]{1,0:T(8,128)}, u32[]{:S(2)}, u32[]{:S(2)}) collective-permute-start(f32[768,256]{1,0:T(8,128)S(1)} %u_pass_42.1.own), channel_id=1, source_target_pairs={{0,1},{1,0},{2,3},{3,2},{4,5},{5,4},{6,7},{7,6},{8,9},{9,8},{10,11... | collective-permute-start | bytes 2359304 | tf_op jit(solution)/shard_map/ppermute | solution.py:337
  40.7 40.1 %slice-start = ((s8[5046272]{0:T(1024)(128)(4,1)}), s8[851968]{0:T(1024)(128)(4,1)S(1)}, s32[]{:S(2)}) async-start(s8[5046272]{0:T(1024)(128)(4,1)} %bitcast.12), calls=%async_computation | async-start | bytes 1703936
  43.1 37.7 %slice-start.1 = ((s8[5046272]{0:T(1024)(128)(4,1)}), s8[4194304]{0:T(1024)(128)(4,1)S(1)}, s32[]{:S(2)}) async-start(s8[5046272]{0:T(1024)(128)(4,1)} %bitcast.12), calls=%async_computation.1 | async-start | bytes 8388608
  43.1 12.2 %collective-permute-start.10 = (s16[784,256]{1,0:T(8,128)(2,1)S(1)}, s16[784,256]{1,0:T(8,128)(2,1)S(1)}, u32[]{:S(2)}, u32[]{:S(2)}) collective-permute-start(s16[784,256]{1,0:T(8,128)(2,1)S(1)} %get-tuple-element.38.refs_5_), channel_id=1, source_target_pairs={{0,2},{1,3},{2,0},{3,1},{4,6},{5,7},{6,4},{7,5},{8,10},{9,11},{10,... | collective-permute-start | bytes 1204232 | tf_op jit(solution)/shard_map/ppermute | solution.py:337
  46.2 34.7 %copy-start.4 = (bf16[6144,256]{1,0:T(8,128)(2,1)S(1)}, bf16[6144,256]{1,0:T(8,128)(2,1)}, u32[]{:S(2)}) copy-start(bf16[6144,256]{1,0:T(8,128)(2,1)} %refs_2_.17) | copy-start | bytes 9437188
  46.2 34.7 %copy-start.6 = (bf16[1024,256]{1,0:T(8,128)(2,1)S(1)}, bf16[1024,256]{1,0:T(8,128)(2,1)}, u32[]{:S(2)}) copy-start(bf16[1024,256]{1,0:T(8,128)(2,1)} %v_ref.1) | copy-start | bytes 1572868
  46.2 30.7 %collective-permute-start.7 = (s16[784,256]{1,0:T(8,128)(2,1)S(1)}, s16[784,256]{1,0:T(8,128)(2,1)S(1)}, u32[]{:S(2)}, u32[]{:S(2)}) collective-permute-start(s16[784,256]{1,0:T(8,128)(2,1)S(1)} %get-tuple-element.36.refs_5_), channel_id=1, source_target_pairs={{0,2},{1,3},{2,0},{3,1},{4,6},{5,7},{6,4},{7,5},{8,10},{9,11},{10,... | collective-permute-start | bytes 1204232 | tf_op jit(solution)/shard_map/ppermute | solution.py:337
  49.3 28.1 %collective-permute-start.4 = (s16[784,256]{1,0:T(8,128)(2,1)S(1)}, s16[784,256]{1,0:T(8,128)(2,1)S(1)}, u32[]{:S(2)}, u32[]{:S(2)}) collective-permute-start(s16[784,256]{1,0:T(8,128)(2,1)S(1)} %get-tuple-element.34.refs_5_), channel_id=1, source_target_pairs={{0,2},{1,3},{2,0},{3,1},{4,6},{5,7},{6,4},{7,5},{8,10},{9,11},{10,... | collective-permute-start | bytes 1204232 | tf_op jit(solution)/shard_map/ppermute | solution.py:337
  51.9 24.9 %collective-permute-start.13 = (s16[400,256]{1,0:T(8,128)(2,1)S(1)}, s16[400,256]{1,0:T(8,128)(2,1)S(1)}, u32[]{:S(2)}, u32[]{:S(2)}) collective-permute-start(s16[400,256]{1,0:T(8,128)(2,1)S(1)} %get-tuple-element.41.refs_5_), channel_id=1, source_target_pairs={{0,2},{1,3},{2,0},{3,1},{4,6},{5,7},{6,4},{7,5},{8,10},{9,11},{10,... | collective-permute-start | bytes 614408 | tf_op jit(solution)/shard_map/ppermute | solution.py:337
  55.3 29.4 %collective-permute-start.11 = (s16[784,256]{1,0:T(8,128)(2,1)S(1)}, s16[784,256]{1,0:T(8,128)(2,1)S(1)}, u32[]{:S(2)}, u32[]{:S(2)}) collective-permute-start(s16[784,256]{1,0:T(8,128)(2,1)S(1)} %collective-permute-done.10.refs_7_), channel_id=1, source_target_pairs={{0,1},{1,0},{2,3},{3,2},{4,5},{5,4},{6,7},{7,6},{8,9},{9,8},{10,11... | collective-permute-start | bytes 1204232 | tf_op jit(solution)/shard_map/ppermute | solution.py:337
  56.6 24.2 %collective-permute-start.1 = (s16[400,256]{1,0:T(8,128)(2,1)S(1)}, s16[400,256]{1,0:T(8,128)(2,1)S(1)}, u32[]{:S(2)}, u32[]{:S(2)}) collective-permute-start(s16[400,256]{1,0:T(8,128)(2,1)S(1)} %get-tuple-element.32.refs_5_), channel_id=1, source_target_pairs={{0,2},{1,3},{2,0},{3,1},{4,6},{5,7},{6,4},{7,5},{8,10},{9,11},{10,... | collective-permute-start | bytes 614408 | tf_op jit(solution)/shard_map/ppermute | solution.py:337
  76.9 4.0 %collective-permute-start.14 = (s16[400,256]{1,0:T(8,128)(2,1)S(1)}, s16[400,256]{1,0:T(8,128)(2,1)S(1)}, u32[]{:S(2)}, u32[]{:S(2)}) collective-permute-start(s16[400,256]{1,0:T(8,128)(2,1)S(1)} %collective-permute-done.13.refs_7_), channel_id=1, source_target_pairs={{0,1},{1,0},{2,3},{3,2},{4,5},{5,4},{6,7},{7,6},{8,9},{9,8},{10,11... | collective-permute-start | bytes 614408 | tf_op jit(solution)/shard_map/ppermute | solution.py:337
  76.9 14.6 %collective-permute-start.8 = (s16[784,256]{1,0:T(8,128)(2,1)S(1)}, s16[784,256]{1,0:T(8,128)(2,1)S(1)}, u32[]{:S(2)}, u32[]{:S(2)}) collective-permute-start(s16[784,256]{1,0:T(8,128)(2,1)S(1)} %collective-permute-done.7.refs_7_), channel_id=1, source_target_pairs={{0,1},{1,0},{2,3},{3,2},{4,5},{5,4},{6,7},{7,6},{8,9},{9,8},{10,11... | collective-permute-start | bytes 1204232 | tf_op jit(solution)/shard_map/ppermute | solution.py:337
  77.4 20.5 %collective-permute-start.5 = (s16[784,256]{1,0:T(8,128)(2,1)S(1)}, s16[784,256]{1,0:T(8,128)(2,1)S(1)}, u32[]{:S(2)}, u32[]{:S(2)}) collective-permute-start(s16[784,256]{1,0:T(8,128)(2,1)S(1)} %collective-permute-done.4.refs_7_), channel_id=1, source_target_pairs={{0,1},{1,0},{2,3},{3,2},{4,5},{5,4},{6,7},{7,6},{8,9},{9,8},{10,11... | collective-permute-start | bytes 1204232 | tf_op jit(solution)/shard_map/ppermute | solution.py:337
  80.8 23.2 %collective-permute-start.2 = (s16[400,256]{1,0:T(8,128)(2,1)S(1)}, s16[400,256]{1,0:T(8,128)(2,1)S(1)}, u32[]{:S(2)}, u32[]{:S(2)}) collective-permute-start(s16[400,256]{1,0:T(8,128)(2,1)S(1)} %collective-permute-done.1.refs_7_), channel_id=1, source_target_pairs={{0,1},{1,0},{2,3},{3,2},{4,5},{5,4},{6,7},{7,6},{8,9},{9,8},{10,11... | collective-permute-start | bytes 614408 | tf_op jit(solution)/shard_map/ppermute | solution.py:337
  108.1 8.8 %collective-permute-start.17 = (s16[144,256]{1,0:T(8,128)(2,1)S(1)}, s16[144,256]{1,0:T(8,128)(2,1)S(1)}, u32[]{:S(2)}, u32[]{:S(2)}) collective-permute-start(s16[144,256]{1,0:T(8,128)(2,1)S(1)} %get-tuple-element.53), channel_id=1, source_target_pairs={{0,4},{4,0},{8,12},{12,8},{16,20},{20,16},{24,28},{28,24},{1,5},{5... | collective-permute-start | bytes 221192 | tf_op jit(solution)/shard_map/ppermute | solution.py:337
  108.8 11.8 %collective-permute-start.18 = (s16[144,256]{1,0:T(8,128)(2,1)S(1)}, s16[144,256]{1,0:T(8,128)(2,1)S(1)}, u32[]{:S(2)}, u32[]{:S(2)}) collective-permute-start(s16[144,256]{1,0:T(8,128)(2,1)S(1)} %get-tuple-element.54), channel_id=1, source_target_pairs={{0,8},{4,12},{8,0},{12,4},{16,24},{20,28},{24,16},{28,20},{1,9},{5... | collective-permute-start | bytes 221192 | tf_op jit(solution)/shard_map/ppermute | solution.py:337
  108.8 4.6 %collective-permute-start.15 = (bf16[16,256]{1,0:T(8,128)(2,1)S(1)}, bf16[16,256]{1,0:T(8,128)(2,1)S(1)}, u32[]{:S(2)}, u32[]{:S(2)}) collective-permute-start(bf16[16,256]{1,0:T(8,128)(2,1)S(1)} %get-tuple-element.61), channel_id=1, source_target_pairs={{0,1},{1,2},{2,3},{3,0},{4,5},{5,6},{6,7},{7,4},{8,9},{9,10},{10,1... | collective-permute-start | bytes 24584 | tf_op jit(solution)/shard_map/ppermute | solution.py:342
  110.3 6.5 %collective-permute-start.16 = (bf16[16,256]{1,0:T(8,128)(2,1)S(1)}, bf16[16,256]{1,0:T(8,128)(2,1)S(1)}, u32[]{:S(2)}, u32[]{:S(2)}) collective-permute-start(bf16[16,256]{1,0:T(8,128)(2,1)S(1)} %get-tuple-element.60), channel_id=1, source_target_pairs={{0,3},{1,0},{2,1},{3,2},{4,7},{5,4},{6,5},{7,6},{8,11},{9,8},{10,9... | collective-permute-start | bytes 24584 | tf_op jit(solution)/shard_map/ppermute | solution.py:342
  110.5 11.1 %collective-permute-start.19 = (s16[144,256]{1,0:T(8,128)(2,1)S(1)}, s16[144,256]{1,0:T(8,128)(2,1)S(1)}, u32[]{:S(2)}, u32[]{:S(2)}) collective-permute-start(s16[144,256]{1,0:T(8,128)(2,1)S(1)} %get-tuple-element.55), channel_id=1, source_target_pairs={{0,12},{4,8},{8,4},{12,0},{16,28},{20,24},{24,20},{28,16},{1,13},{... | collective-permute-start | bytes 221192 | tf_op jit(solution)/shard_map/ppermute | solution.py:337
  113.4 8.3 %collective-permute-start.20 = (s16[144,256]{1,0:T(8,128)(2,1)S(1)}, s16[144,256]{1,0:T(8,128)(2,1)S(1)}, u32[]{:S(2)}, u32[]{:S(2)}) collective-permute-start(s16[144,256]{1,0:T(8,128)(2,1)S(1)} %get-tuple-element.56), channel_id=1, source_target_pairs={{0,16},{4,20},{8,24},{12,28},{16,0},{20,4},{24,8},{28,12},{1,17},{... | collective-permute-start | bytes 221192 | tf_op jit(solution)/shard_map/ppermute | solution.py:337
  116.8 9.8 %collective-permute-start.21 = (s16[144,256]{1,0:T(8,128)(2,1)S(1)}, s16[144,256]{1,0:T(8,128)(2,1)S(1)}, u32[]{:S(2)}, u32[]{:S(2)}) collective-permute-start(s16[144,256]{1,0:T(8,128)(2,1)S(1)} %get-tuple-element.57), channel_id=1, source_target_pairs={{0,20},{4,16},{8,28},{12,24},{16,4},{20,0},{24,12},{28,8},{1,21},{... | collective-permute-start | bytes 221192 | tf_op jit(solution)/shard_map/ppermute | solution.py:337
  116.9 9.7 %collective-permute-start.22 = (s16[144,256]{1,0:T(8,128)(2,1)S(1)}, s16[144,256]{1,0:T(8,128)(2,1)S(1)}, u32[]{:S(2)}, u32[]{:S(2)}) collective-permute-start(s16[144,256]{1,0:T(8,128)(2,1)S(1)} %get-tuple-element.58), channel_id=1, source_target_pairs={{0,24},{4,28},{8,16},{12,20},{16,8},{20,12},{24,0},{28,4},{1,25},{... | collective-permute-start | bytes 221192 | tf_op jit(solution)/shard_map/ppermute | solution.py:337
  120.5 7.2 %collective-permute-start.23 = (s16[144,256]{1,0:T(8,128)(2,1)S(1)}, s16[144,256]{1,0:T(8,128)(2,1)S(1)}, u32[]{:S(2)}, u32[]{:S(2)}) collective-permute-start(s16[144,256]{1,0:T(8,128)(2,1)S(1)} %get-tuple-element.59), channel_id=1, source_target_pairs={{0,28},{4,24},{8,20},{12,16},{16,12},{20,8},{24,4},{28,0},{1,29},{... | collective-permute-start | bytes 221192 | tf_op jit(solution)/shard_map/ppermute | solution.py:337
  128.5 8.0 %collective-permute-start.24 = (bf16[128,256]{1,0:T(8,128)(2,1)S(1)}, bf16[128,256]{1,0:T(8,128)(2,1)S(1)}, u32[]{:S(2)}, u32[]{:S(2)}) collective-permute-start(bf16[128,256]{1,0:T(8,128)(2,1)S(1)} %last_step.1.refs_0_), channel_id=1, source_target_pairs={{0,4},{4,0},{8,12},{12,8},{16,20},{20,16},{24,28},{28,24},{1,5},{5... | collective-permute-start | bytes 196616 | tf_op jit(solution)/shard_map/ppermute | solution.py:337
  129.2 9.6 %collective-permute-start.25 = (bf16[128,256]{1,0:T(8,128)(2,1)S(1)}, bf16[128,256]{1,0:T(8,128)(2,1)S(1)}, u32[]{:S(2)}, u32[]{:S(2)}) collective-permute-start(bf16[128,256]{1,0:T(8,128)(2,1)S(1)} %last_step.1.refs_0_), channel_id=1, source_target_pairs={{0,8},{4,12},{8,0},{12,4},{16,24},{20,28},{24,16},{28,20},{1,9},{5... | collective-permute-start | bytes 196616 | tf_op jit(solution)/shard_map/ppermute | solution.py:337
  132.5 8.5 %collective-permute-start.26 = (bf16[128,256]{1,0:T(8,128)(2,1)S(1)}, bf16[128,256]{1,0:T(8,128)(2,1)S(1)}, u32[]{:S(2)}, u32[]{:S(2)}) collective-permute-start(bf16[128,256]{1,0:T(8,128)(2,1)S(1)} %last_step.1.refs_0_), channel_id=1, source_target_pairs={{0,12},{4,8},{8,4},{12,0},{16,28},{20,24},{24,20},{28,16},{1,13},{... | collective-permute-start | bytes 196616 | tf_op jit(solution)/shard_map/ppermute | solution.py:337
  133.3 10.5 %collective-permute-start.27 = (bf16[128,256]{1,0:T(8,128)(2,1)S(1)}, bf16[128,256]{1,0:T(8,128)(2,1)S(1)}, u32[]{:S(2)}, u32[]{:S(2)}) collective-permute-start(bf16[128,256]{1,0:T(8,128)(2,1)S(1)} %last_step.1.refs_0_), channel_id=1, source_target_pairs={{0,16},{4,20},{8,24},{12,28},{16,0},{20,4},{24,8},{28,12},{1,17},{... | collective-permute-start | bytes 196616 | tf_op jit(solution)/shard_map/ppermute | solution.py:337
  136.2 8.9 %collective-permute-start.28 = (bf16[128,256]{1,0:T(8,128)(2,1)S(1)}, bf16[128,256]{1,0:T(8,128)(2,1)S(1)}, u32[]{:S(2)}, u32[]{:S(2)}) collective-permute-start(bf16[128,256]{1,0:T(8,128)(2,1)S(1)} %last_step.1.refs_0_), channel_id=1, source_target_pairs={{0,20},{4,16},{8,28},{12,24},{16,4},{20,0},{24,12},{28,8},{1,21},{... | collective-permute-start | bytes 196616 | tf_op jit(solution)/shard_map/ppermute | solution.py:337
  136.5 8.6 %collective-permute-start.29 = (bf16[128,256]{1,0:T(8,128)(2,1)S(1)}, bf16[128,256]{1,0:T(8,128)(2,1)S(1)}, u32[]{:S(2)}, u32[]{:S(2)}) collective-permute-start(bf16[128,256]{1,0:T(8,128)(2,1)S(1)} %last_step.1.refs_0_), channel_id=1, source_target_pairs={{0,24},{4,28},{8,16},{12,20},{16,8},{20,12},{24,0},{28,4},{1,25},{... | collective-permute-start | bytes 196616 | tf_op jit(solution)/shard_map/ppermute | solution.py:337
  138.9 7.1 %collective-permute-start.30 = (bf16[128,256]{1,0:T(8,128)(2,1)S(1)}, bf16[128,256]{1,0:T(8,128)(2,1)S(1)}, u32[]{:S(2)}, u32[]{:S(2)}) collective-permute-start(bf16[128,256]{1,0:T(8,128)(2,1)S(1)} %last_step.1.refs_0_), channel_id=1, source_target_pairs={{0,28},{4,24},{8,20},{12,16},{16,12},{20,8},{24,4},{28,0},{1,29},{... | collective-permute-start | bytes 196616 | tf_op jit(solution)/shard_map/ppermute | solution.py:337

commit v2 on v1

v2 whole, which is shorter than its diff:
```python
import functools

import jax
import jax.numpy as jnp
from jax import lax
from jax.experimental import pallas as pl
from jax.experimental.pallas import tpu as pltpu
from jax.sharding import PartitionSpec as P

step_u = 0.03
step_v = 0.02
ridge = 0.1
smooth = 20.0

f32, bf16, i32, i16 = jnp.float32, jnp.bfloat16, jnp.int32, jnp.int16
B = 128
PAD = 16
TOP = 32000.0
ROWS_BY_ROWS = (((1,), (1,)), ((), ()))
COLS_BY_COLS = (((0,), (0,)), ((), ()))

SMEM = pl.BlockSpec(memory_space=pltpu.SMEM)
VMEM = pl.BlockSpec(memory_space=pltpu.VMEM)
ANY = pl.BlockSpec(memory_space=pl.ANY)


SMALL = pl.CostEstimate(flops=1, bytes_accessed=1, transcendentals=0)


def params():
    return pltpu.CompilerParams(vmem_limit_bytes=24 * 2**20)


def encode(x):
    rows, width = x.shape
    group = min(rows, B)
    line = lax.broadcasted_iota(i32, (PAD, width), 0)
    powers = jnp.zeros((PAD, width), f32)
    parts = []
    for g in range(rows // group):
        part = x[g * group : (g + 1) * group]
        top = jnp.max(jnp.abs(part), axis=0, keepdims=True)
        power = jnp.ceil(jnp.log2(jnp.maximum(top, 1e-30)))
        parts.append(jnp.round(part * (jnp.exp2(-power) * TOP)))
        powers = jnp.where(line == g, power, powers)
    return [p.astype(i32).astype(i16) for p in parts], powers.astype(i32).astype(i16)


def store_code(ref, x):
    parts, powers = encode(x)
    group = parts[0].shape[0]
    for g, part in enumerate(parts):
        ref[g * group : (g + 1) * group, :] = part
    ref[x.shape[0] :, :] = powers


def decode(ref, g, group):
    rows = ref.shape[0] - PAD
    powers = ref[rows:, :].astype(i32).astype(f32)[g : g + 1]
    return ref[g * group : (g + 1) * group, :].astype(i32).astype(f32) * (
        jnp.exp2(powers) * (1.0 / TOP)
    )


def my_core():
    return lax.rem(lax.axis_index("step"), 2)


def two_halves(rows):
    half = rows // 2
    core = my_core()
    return [pl.ds(pl.multiple_of(at * half, 16), half) for at in (core, 1 - core)]


def residual(left, v_ref, block, err, slots, first, count, across):
    wide = min(2, across)
    for t in range(0, across, wide):
        predicted = lax.dot_general(
            left, v_ref[t * B : (t + wide) * B, :], ROWS_BY_ROWS, preferred_element_type=f32
        )
        for r in range(count):
            rows = slice(r * B, (r + 1) * B)
            for c in range(t, t + wide):
                slot = slots[(first + r) * across + c]
                gap = predicted[rows, (c - t) * B : (c - t + 1) * B] - block(slot, r, c).astype(f32)
                err[rows, c * B : (c + 1) * B] = jnp.where(slot >= 0, gap, 0.0).astype(bf16)


def split_product(err, v_ref, outs):
    for out, rows in zip(outs, two_halves(err.shape[0])):
        out[...] = jnp.dot(err[rows, :], v_ref[...], preferred_element_type=f32)


def first_u_body(
    count, down, across, row_hbm, col_hbm, live_hbm, u_hbm, v_hbm, values,
    keep, send, slots, row_ref, col_ref, live_ref, dense, err, left, v_ref, sems
):
    loads = [
        pltpu.make_async_copy(src, dst, sems.at[i])
        for i, (src, dst) in enumerate(
            (
                (row_hbm, row_ref),
                (col_hbm, col_ref),
                (live_hbm, live_ref),
                (u_hbm.at[pl.ds(0, count * B)], left),
                (v_hbm, v_ref),
            )
        )
    ]
    for load in loads:
        load.start()

    def clear(i, c):
        slots[i] = jnp.int32(-1)
        return c

    lax.fori_loop(0, down * across, clear, 0, unroll=8)
    for load in loads[:3]:
        load.wait()
    live = live_ref[0, 0]

    def enter(k, c):
        slots[row_ref[0, 0, k] * across + col_ref[0, 0, k]] = jnp.where(k < live, k, -1)
        return c

    lax.fori_loop(0, row_ref.shape[2], enter, 0, unroll=7)
    sem = sems.at[len(loads)]

    def fetch(i, started):
        slot = slots[i]

        @pl.when(slot >= 0)
        def _():
            row = pl.multiple_of((i // across) * B, B)
            pltpu.make_async_copy(
                values.at[slot], dense.at[lax.rem(i, across), pl.ds(row, B)], sem
            ).start()

        return started + (slot >= 0).astype(i32)

    started = lax.fori_loop(0, count * across, fetch, jnp.int32(0), unroll=across)
    for load in loads[3:]:
        load.wait()

    def wait(_, c):
        pltpu.make_async_copy(values.at[0], dense.at[0, pl.ds(0, B)], sem).wait()
        return c

    lax.fori_loop(0, started, wait, 0)
    block = lambda slot, r, c: dense[c, r * B : (r + 1) * B, :]
    residual(left[...], v_ref, block, err, slots, 0, count, across)
    split_product(err, v_ref, (keep, send))


def in_hbm(x):
    return pltpu.with_memory_space_constraint(x, pltpu.HBM)


def first_u_pass(count, down, across, index, u, v, values):
    rows, width = count * B, u.shape[1]
    hbm = pl.BlockSpec(memory_space=pltpu.HBM)
    part = jax.ShapeDtypeStruct((rows // 2, width), f32)
    return pl.pallas_call(
        functools.partial(first_u_body, count, down, across),
        out_shape=[part, part, jax.ShapeDtypeStruct((down * across,), i32)],
        in_specs=[hbm, hbm, ANY, hbm, hbm, hbm],
        out_specs=[VMEM, VMEM, SMEM],
        scratch_shapes=[
            *(pltpu.SMEM(x.shape, i32) for x in index),
            pltpu.VMEM((across, rows, B), bf16),
            pltpu.VMEM((rows, across * B), bf16),
            pltpu.VMEM((rows, width), bf16),
            pltpu.VMEM(v.shape, bf16),
            pltpu.SemaphoreType.DMA((6,)),
        ],
        compiler_params=params(),
        cost_estimate=SMALL,
        name="u_pass_0",
    )(*(in_hbm(x) for x in index[:2]), index[2], *(in_hbm(x) for x in (u, v, values)))


def u_body(first, count, across, waits, slots, u_ref, v_ref, values, *refs):
    keep, send, err = refs[waits:]
    block = lambda slot, r, c: values[jnp.maximum(slot, 0)]
    residual(u_ref[first * B : (first + count) * B, :], v_ref, block, err, slots, first, count, across)
    split_product(err, v_ref, (keep, send))


def u_pass(first, count, across, slots, u, v, values, after):
    rows, width = count * B, u.shape[1]
    part = jax.ShapeDtypeStruct((rows // 2, width), f32)
    return pl.pallas_call(
        functools.partial(u_body, first, count, across, len(after)),
        out_shape=[part, part],
        in_specs=[SMEM, VMEM, VMEM, VMEM] + [ANY] * len(after),
        out_specs=[VMEM, VMEM],
        scratch_shapes=[pltpu.VMEM((rows, across * B), bf16)],
        compiler_params=params(),
        cost_estimate=SMALL,
        name=f"u_pass_{first}",
    )(slots, u, v, values, *after)


def sum_body(own, other, *refs):
    store_code(refs[-1], own[...] + other[...])


def core_sum(own, other, after):
    rows, width = own.shape
    return pl.pallas_call(
        sum_body,
        out_shape=jax.ShapeDtypeStruct((rows + PAD, width), i16),
        in_specs=[VMEM, VMEM] + [ANY] * len(after),
        out_specs=VMEM,
        compiler_params=params(),
        cost_estimate=SMALL,
        name="core_sum",
    )(own, other, *after)


def again_body(mine, mine_in, out):
    rows = mine.shape[0] - PAD
    group = min(rows, B)
    whole = [decode(mine, g, group) + decode(mine_in, g, group) for g in range(rows // group)]
    store_code(out, jnp.concatenate(whole, axis=0))


def chip_sum(code, code_in):
    return pl.pallas_call(
        again_body,
        out_shape=jax.ShapeDtypeStruct(code.shape, i16),
        in_specs=[VMEM, VMEM],
        out_specs=VMEM,
        compiler_params=params(),
        name="chip_sum",
    )(code, code_in)


def update_body(first, code, code_in, u_ref, *refs):
    out = refs[-1]
    half = out.shape[0]
    group = min(half, B)
    start = first * B + my_core() * half
    for g in range(half // group):
        old = u_ref[pl.ds(pl.multiple_of(start + g * group, 16), group), :].astype(f32)
        grad = decode(code, g, group) + decode(code_in, g, group)
        out[g * group : (g + 1) * group, :] = (old - step_u * (grad + ridge * old)).astype(bf16)


def update(first, code, code_in, u, after):
    rows, width = code.shape[0] - PAD, code.shape[1]
    return pl.pallas_call(
        functools.partial(update_body, first),
        out_shape=jax.ShapeDtypeStruct((rows, width), bf16),
        in_specs=[VMEM, VMEM, VMEM] + [ANY] * len(after),
        out_specs=VMEM,
        compiler_params=params(),
        cost_estimate=SMALL,
        name=f"update_{first}",
    )(code, code_in, u, *after)


def v_body(first, count, across, opening, shards, *refs):
    slots, v_ref, values, own, other = refs[:5]
    refs = refs[5:]
    if not opening:
        before = refs[0]
        refs = refs[2:]
    new_out, refs = refs[0], refs[1:]
    if shards:
        own_out, sent, refs = refs[0], refs[1:shards], refs[shards:]
    else:
        total, refs = refs[0], refs[1:]
    err, left, sem = refs[:3]
    for src, rows in zip((own, other), two_halves(count * B)):
        left[rows, :] = src[...]
    save = pltpu.make_async_copy(left, new_out.at[pl.ds(first * B, count * B)], sem)
    save.start()
    block = lambda slot, r, c: values[jnp.maximum(slot, 0)]
    residual(left[...], v_ref, block, err, slots, first, count, across)
    part = lax.dot_general(left[...], err[...], COLS_BY_COLS, preferred_element_type=f32)
    if not opening:
        part = part + before[...]
    if not shards:
        total[...] = part
    else:
        turned = refs[3]
        turned[...] = part.T
        rows = turned.shape[0] // shards
        here = lax.axis_index("svc")
        own_out[...] = turned[pl.ds(pl.multiple_of(here * rows, 8), rows), :]
        for d in range(1, shards):
            there = jnp.bitwise_xor(here, d)
            store_code(sent[d - 1], turned[pl.ds(pl.multiple_of(there * rows, 8), rows), :])
    save.wait()


def v_pass(first, count, across, slots, shape, v, values, halves, before, shards):
    width = v.shape[1]
    times = v.shape[0]
    opening = before is None
    ins = [slots, v, values, *halves]
    in_specs = [SMEM] + [VMEM] * 4
    aliases = {}
    out = [jax.ShapeDtypeStruct(shape, bf16)]
    out_specs = [ANY]
    if not opening:
        ins += [before[1], before[0]]
        in_specs += [VMEM, ANY]
        aliases = {6: 0}
    scratch = [
        pltpu.VMEM((count * B, across * B), bf16),
        pltpu.VMEM((count * B, width), bf16),
        pltpu.SemaphoreType.DMA,
    ]
    if shards:
        rows = times // shards
        out.append(jax.ShapeDtypeStruct((rows, width), f32))
        out += [jax.ShapeDtypeStruct((rows + PAD, width), i16)] * (shards - 1)
        out_specs += [VMEM] * shards
        scratch.append(pltpu.VMEM((times, width), f32))
    else:
        out.append(jax.ShapeDtypeStruct((width, times), f32))
        out_specs.append(VMEM)
    return pl.pallas_call(
        functools.partial(v_body, first, count, across, opening, shards),
        out_shape=out,
        in_specs=in_specs,
        out_specs=out_specs,
        input_output_aliases=aliases,
        scratch_shapes=scratch,
        compiler_params=params(),
        cost_estimate=SMALL,
        name=f"v_pass_{first}",
    )(*ins)


def last_body(v_ref, low, high, own, *refs):
    codes, out, wide = refs[:-2], refs[-2], refs[-1]
    times = v_ref.shape[0]
    rows = out.shape[0]
    group = min(rows, B)
    wide[:PAD, :] = low[...]
    wide[PAD : PAD + times, :] = v_ref[...]
    wide[PAD + times :, :] = high[...]
    start = pl.multiple_of(lax.axis_index("svc") * rows, 16)
    window = wide[pl.ds(start, rows + 2 * PAD), :].astype(f32)
    old = window[PAD : PAD + rows]
    lap = 2.0 * old - window[PAD - 1 : PAD - 1 + rows] - window[PAD + 1 : PAD + 1 + rows]
    for g in range(rows // group):
        at = slice(g * group, (g + 1) * group)
        grad = own[at, :]
        for code in codes:
            grad = grad + decode(code, g, group)
        out[at, :] = (old[at] - step_v * (grad + ridge * old[at] + smooth * lap[at])).astype(bf16)


def last_step(v, low, high, own, codes):
    return pl.pallas_call(
        last_body,
        out_shape=jax.ShapeDtypeStruct(own.shape, bf16),
        in_specs=[VMEM] * (4 + len(codes)),
        out_specs=VMEM,
        scratch_shapes=[pltpu.VMEM((v.shape[0] + 2 * PAD, v.shape[1]), bf16)],
        compiler_params=params(),
        name="last_step",
    )(v, low, high, own, *codes)


def join_body(*refs):
    out = refs[-1]
    rows = refs[0].shape[0]
    for d, part in enumerate(refs[:-1]):
        there = jnp.bitwise_xor(lax.axis_index("svc"), d)
        out[pl.ds(pl.multiple_of(there * rows, 16), rows), :] = part[...]


def join(parts):
    rows, width = parts[0].shape
    return pl.pallas_call(
        join_body,
        out_shape=jax.ShapeDtypeStruct((rows * len(parts), width), bf16),
        in_specs=[VMEM] * len(parts),
        out_specs=VMEM,
        compiler_params=params(),
        name="join",
    )(*parts)


def swap(x, axis, mask):
    return lax.ppermute(x, axis, [(i, i ^ mask) for i in range(lax.axis_size(axis))])


def shift(x, axis, by):
    n = lax.axis_size(axis)
    return lax.ppermute(x, axis, [(i, (i + by) % n) for i in range(n)])


def chunks_of(down):
    unit = down // 8
    sizes = [unit, 2 * unit, 2 * unit, 2 * unit]
    sizes.append(down - sum(sizes))
    return [(sum(sizes[:i]), size) for i, size in enumerate(sizes)]


def on_device(u, v, block_rows, block_cols, block_counts, block_values):
    down, across = u.shape[0] // B, v.shape[0] // B
    values = block_values[0, 0]
    steps, peers = lax.axis_size("step"), lax.axis_size("svc")
    low = shift(v[-PAD:], "step", 1)
    high = shift(v[:PAD], "step", -1)
    chunks = chunks_of(down)
    keep, send, slots = first_u_pass(chunks[0][1], down, across, (block_rows, block_cols, block_counts), u, v, values)
    codes = [core_sum(keep, swap(send, "step", 1), [])]
    waiting = None
    for first, count in chunks[1:]:
        keep, send = u_pass(first, count, across, slots, u, v, values, codes[-1:])
        if waiting:
            codes.append(core_sum(*waiting, [keep]))
        waiting = (keep, swap(send, "step", 1))
    codes.append(core_sum(*waiting, codes[-1:]))
    arrived = []
    for code in codes:
        code_in = swap(code, "step", 2)
        mask = 4
        while mask < steps:
            code = chip_sum(code, code_in)
            code_in = swap(code, "step", mask)
            mask *= 2
        arrived.append((code, code_in))
    before = None
    for i, (first, count) in enumerate(chunks):
        after = [codes[-1]] if before is None else [before[1]]
        if i == len(chunks) - 1:
            after += [low, high]
        half = update(first, *arrived[i], u, after)
        halves = (half, swap(half, "step", 1))
        shards = peers if i == len(chunks) - 1 else 0
        before = v_pass(first, count, across, slots, u.shape, v, values, halves, before, shards)
    new_services, own, sent = before[0], before[1], before[2:]
    part = last_step(v, low, high, own, [swap(x, "svc", d + 1) for d, x in enumerate(sent)])
    column = [part] + [swap(part, "svc", d) for d in range(2, peers, 2)]
    return new_services, join([x for y in column for x in (y, swap(y, "svc", 1))])


def solution(mesh):
    return jax.shard_map(
        on_device,
        mesh=mesh,
        in_specs=(
            P("svc", None),
            P("step", None),
            P("svc", "step", None),
            P("svc", "step", None),
            P("svc", "step"),
            P("svc", "step", None, None, None),
        ),
        out_specs=(P("svc", None), P("step", None)),
        check_vma=False,
    )
```

time: 148 us -> 101 us (0.68)
  Pallas kernels: 70.2 us -> 29.8 us
  local copies, waits for them, and re-layouts: 6.75 us -> 0.02 us
  starting transfers between devices: 32.4 us -> 34.2 us
    pallas_call x10 -> x15, Pallas kernels: 40.9 us -> 16.3 us  [the longest x4 9.56 us: u_pass(): pl.pallas_call(functools.partial(u_body, first, count, across, len(after)...]
    pallas_call x5, Pallas kernels: 27.1 us -> 12.5 us  [v_pass(): pl.pallas_call(functools.partial(v_body, first, count, across, opening, s...]
    unnamed x22 -> x8, local copies, waits for them, and re-layouts: 6.75 us -> 0.02 us
    ppermute x29, waiting for transfers between devices: 36.4 us -> 34.5 us  [swap(): lax.ppermute(x, axis, [(i, i ^ mask) for i in range(lax.axis_size(axis))])]
    ppermute x29, starting transfers between devices: 30.6 us -> 32.5 us  [swap(): lax.ppermute(x, axis, [(i, i ^ mask) for i in range(lax.axis_size(axis))])]
  transfers between devices with their start and end apart: 31 -> 31, of which waited for: 8 -> 14; matrix products, arithmetic and copies ran while one was open for 0% -> 0% of each run, Pallas kernels for 34% -> 18%
where the time goes in v2:
time: 101 us
  waiting for transfers between devices  35.5 us (35%)
  starting transfers between devices  34.2 us (34%)
  Pallas kernels  29.8 us (30%)
  between operations  1.53 us (2%)
    ppermute x29, waiting for transfers between devices, swap(): lax.ppermute(x, axis, [(i, i ^ mask) for i in range(lax.axis_size(axis))])  34.5 us
    ppermute x29, starting transfers between devices, swap(): lax.ppermute(x, axis, [(i, i ^ mask) for i in range(lax.axis_size(axis))])  32.5 us
    pallas_call x5, Pallas kernels, v_pass(): pl.pallas_call(functools.partial(v_body, first, count, across, opening, s...  12.5 us
    pallas_call x4, Pallas kernels, u_pass(): pl.pallas_call(functools.partial(u_body, first, count, across, len(after)...  9.56 us
    pallas_call x1, Pallas kernels, first_u_pass(): pl.pallas_call(functools.partial(first_u_body, count, down, across), out_...  4.62 us
  transfers between devices with their start and end apart: 31, of which 14 were waited for; matrix products, arithmetic and copies ran while one was open for 0% of the time, Pallas kernels for 18%

profile of v2, /device:TPU:0, one launch (start us, length us, event | category | flops | bytes accessed | tf_op | source)
XLA Modules:
  0.0 101.2 jit_solution(7035070323761463329)
XLA Ops:
  1.3 4.6 %u_pass_0.1 = (f32[384,256]{1,0:T(8,128)S(1)}, f32[384,256]{1,0:T(8,128)S(1)}, s32[384]{0:T(512)S(1)}) custom-call(s32[1,1,154]{2,1,0:T(1,128)} %row_hbm.1, s32[1,1,154]{2,1,0:T(1,128)} %col_hbm.1, s32[1,1]{1,0:T(1,128)S(6)} %copy.16.live_hbm, bf16[6144,256]{1,0:T(8,128)(2,1)} %u_ref.17, bf16[1024,256]{1,0:T(8,128)(2,1)} %v_ref.9, bf16[154,128,128]{2,1,0:T(8,128)(2,1)} %bitcast.1), custom_call_target="tpu_custom_call" | custom-call | flops 1 | bytes 1 | tf_op jit(solution)/shard_map/u_pass_0/pallas_call | solution.py:163
  5.9 0.5 collective-permute-start
  6.4 1.3 %collective-permute-done.other = f32[384,256]{1,0:T(8,128)S(1)} collective-permute-done((f32[384,256]{1,0:T(8,128)S(1)}, f32[384,256]{1,0:T(8,128)S(1)}, u32[]{:S(2)}, u32[]{:S(2)}) %collective-permute-start) | collective-permute-done | bytes 393248 | tf_op jit(solution)/shard_map/ppermute | solution.py:391
  7.9 2.6 %u_pass_6.1 = (f32[768,256]{1,0:T(8,128)S(1)}, f32[768,256]{1,0:T(8,128)S(1)}) custom-call(s32[384]{0:T(512)S(1)} %get-tuple-element.30.slots.refs_0_, bf16[6144,256]{1,0:T(8,128)(2,1)S(1)} %copy-done, bf16[1024,256]{1,0:T(8,128)(2,1)S(1)} %copy-done.1, bf16[154,128,128]{2,1,0:T(8,128)(2,1)S(1)} %bitcast.4, s16[400,256]{1,0:T(8,128)(2,1)S(1)} %core_sum.5.refs_0_.code), custom_call_target="tpu_custom_call" | custom-call | flops 1 | bytes 1 | tf_op jit(solution)/shard_map/u_pass_6/pallas_call | solution.py:192
  10.5 0.4 collective-permute-start.2
  11.0 2.6 %u_pass_18.1 = (f32[768,256]{1,0:T(8,128)S(1)}, f32[768,256]{1,0:T(8,128)S(1)}) custom-call(s32[384]{0:T(512)S(1)} %get-tuple-element.30.slots.refs_0_, bf16[6144,256]{1,0:T(8,128)(2,1)S(1)} %copy-done, bf16[1024,256]{1,0:T(8,128)(2,1)S(1)} %copy-done.1, bf16[154,128,128]{2,1,0:T(8,128)(2,1)S(1)} %bitcast.5, s16[400,256]{1,0:T(8,128)(2,1)S(1)} %core_sum.5.refs_0_.code), custom_call_target="tpu_custom_call" | custom-call | flops 1 | bytes 1 | tf_op jit(solution)/shard_map/u_pass_18/pallas_call | solution.py:192
  13.9 2.6 %u_pass_30.1 = (f32[768,256]{1,0:T(8,128)S(1)}, f32[768,256]{1,0:T(8,128)S(1)}) custom-call(s32[384]{0:T(512)S(1)} %get-tuple-element.30.slots.refs_0_, bf16[6144,256]{1,0:T(8,128)(2,1)S(1)} %copy-done, bf16[1024,256]{1,0:T(8,128)(2,1)S(1)} %copy-done.1, bf16[154,128,128]{2,1,0:T(8,128)(2,1)S(1)} %bitcast.6, s16[784,256]{1,0:T(8,128)(2,1)S(1)} %core_sum.6.refs_0_.code), custom_call_target="tpu_custom_call" | custom-call | flops 1 | bytes 1 | tf_op jit(solution)/shard_map/u_pass_30/pallas_call | solution.py:192
  16.5 0.4 collective-permute-start.4
  17.2 1.8 %u_pass_42.1 = (f32[384,256]{1,0:T(8,128)S(1)}, f32[384,256]{1,0:T(8,128)S(1)}) custom-call(s32[384]{0:T(512)S(1)} %get-tuple-element.30.slots.refs_0_, bf16[6144,256]{1,0:T(8,128)(2,1)S(1)} %copy-done, bf16[1024,256]{1,0:T(8,128)(2,1)S(1)} %copy-done.1, bf16[154,128,128]{2,1,0:T(8,128)(2,1)S(1)} %bitcast.7, s16[784,256]{1,0:T(8,128)(2,1)S(1)} %core_sum.7.refs_0_.code), custom_call_target="tpu_custom_call" | custom-call | flops 1 | bytes 1 | tf_op jit(solution)/shard_map/u_pass_42/pallas_call | solution.py:192
  19.2 2.8 %collective-permute-start.9 = (s16[400,256]{1,0:T(8,128)(2,1)S(1)}, s16[400,256]{1,0:T(8,128)(2,1)S(1)}, u32[]{:S(2)}, u32[]{:S(2)}) collective-permute-start(s16[400,256]{1,0:T(8,128)(2,1)S(1)} %core_sum.5.refs_0_.code), channel_id=1, source_target_pairs={{0,2},{1,3},{2,0},{3,1},{4,6},{5,7},{6,4},{7,5},{8,10},{9,11},{10,... | collective-permute-start | bytes 614408 | tf_op jit(solution)/shard_map/ppermute | solution.py:391
  22.3 5.5 %collective-permute-done.9.code_in = s16[400,256]{1,0:T(8,128)(2,1)S(1)} collective-permute-done((s16[400,256]{1,0:T(8,128)(2,1)S(1)}, s16[400,256]{1,0:T(8,128)(2,1)S(1)}, u32[]{:S(2)}, u32[]{:S(2)}) %collective-permute-start.9) | collective-permute-done | bytes 204832 | tf_op jit(solution)/shard_map/ppermute | solution.py:391
  28.1 2.1 %collective-permute-start.7 = (s16[784,256]{1,0:T(8,128)(2,1)S(1)}, s16[784,256]{1,0:T(8,128)(2,1)S(1)}, u32[]{:S(2)}, u32[]{:S(2)}) collective-permute-start(s16[784,256]{1,0:T(8,128)(2,1)S(1)} %core_sum.7.refs_0_.code), channel_id=1, source_target_pairs={{0,2},{1,3},{2,0},{3,1},{4,6},{5,7},{6,4},{7,5},{8,10},{9,11},{10,... | collective-permute-start | bytes 1204232 | tf_op jit(solution)/shard_map/ppermute | solution.py:391
  30.2 2.0 %v_pass_0.1 = (bf16[6144,256]{1,0:T(8,128)(2,1)}, f32[256,1024]{1,0:T(8,128)S(1)}) custom-call(s32[384]{0:T(512)S(1)} %get-tuple-element.30.slots.refs_0_, bf16[1024,256]{1,0:T(8,128)(2,1)S(1)} %copy-done.1, bf16[154,128,128]{2,1,0:T(8,128)(2,1)S(1)} %bitcast.8, bf16[384,256]{1,0:T(8,128)(2,1)S(1)} %update_0.1.refs_3_, ...), custom_call_target="tpu_custom_call" | custom-call | flops 1 | bytes 1 | tf_op jit(solution)/shard_map/v_pass_0/pallas_call | solution.py:325
  32.3 4.2 %collective-permute-done.8.code_in = s16[784,256]{1,0:T(8,128)(2,1)S(1)} collective-permute-done((s16[784,256]{1,0:T(8,128)(2,1)S(1)}, s16[784,256]{1,0:T(8,128)(2,1)S(1)}, u32[]{:S(2)}, u32[]{:S(2)}) %collective-permute-start.8) | collective-permute-done | bytes 401440 | tf_op jit(solution)/shard_map/ppermute | solution.py:391
  36.5 0.3 update_6.1.refs_3_
  36.9 2.1 %collective-permute-start.6 = (s16[784,256]{1,0:T(8,128)(2,1)S(1)}, s16[784,256]{1,0:T(8,128)(2,1)S(1)}, u32[]{:S(2)}, u32[]{:S(2)}) collective-permute-start(s16[784,256]{1,0:T(8,128)(2,1)S(1)} %core_sum.8.refs_0_.code), channel_id=1, source_target_pairs={{0,2},{1,3},{2,0},{3,1},{4,6},{5,7},{6,4},{7,5},{8,10},{9,11},{10,... | collective-permute-start | bytes 1204232 | tf_op jit(solution)/shard_map/ppermute | solution.py:391
  39.0 2.8 %v_pass_6.1 = (bf16[6144,256]{1,0:T(8,128)(2,1)}, f32[256,1024]{1,0:T(8,128)S(1)}) custom-call(s32[384]{0:T(512)S(1)} %get-tuple-element.30.slots.refs_0_, bf16[1024,256]{1,0:T(8,128)(2,1)S(1)} %copy-done.1, bf16[154,128,128]{2,1,0:T(8,128)(2,1)S(1)} %bitcast.9, bf16[768,256]{1,0:T(8,128)(2,1)S(1)} %update_6.1.refs_3_, ...), custom_call_target="tpu_custom_call", output_to_operand_aliasing={{0}: (6, {})} | custom-call | flops 1 | bytes 1 | tf_op jit(solution)/shard_map/v_pass_6/pallas_call | solution.py:325
  41.8 3.3 %collective-permute-done.7.code_in = s16[784,256]{1,0:T(8,128)(2,1)S(1)} collective-permute-done((s16[784,256]{1,0:T(8,128)(2,1)S(1)}, s16[784,256]{1,0:T(8,128)(2,1)S(1)}, u32[]{:S(2)}, u32[]{:S(2)}) %collective-permute-start.7) | collective-permute-done | bytes 401440 | tf_op jit(solution)/shard_map/ppermute | solution.py:391
  45.1 0.3 update_18.1.refs_3_
  45.5 1.7 %collective-permute-done.12.refs_4_ = bf16[768,256]{1,0:T(8,128)(2,1)S(1)} collective-permute-done((bf16[768,256]{1,0:T(8,128)(2,1)S(1)}, bf16[768,256]{1,0:T(8,128)(2,1)S(1)}, u32[]{:S(2)}, u32[]{:S(2)}) %collective-permute-start.12) | collective-permute-done | bytes 393248 | tf_op jit(solution)/shard_map/ppermute | solution.py:391
  47.2 2.6 %v_pass_18.1 = (bf16[6144,256]{1,0:T(8,128)(2,1)}, f32[256,1024]{1,0:T(8,128)S(1)}) custom-call(s32[384]{0:T(512)S(1)} %get-tuple-element.30.slots.refs_0_, bf16[1024,256]{1,0:T(8,128)(2,1)S(1)} %copy-done.1, bf16[154,128,128]{2,1,0:T(8,128)(2,1)S(1)} %bitcast.10, bf16[768,256]{1,0:T(8,128)(2,1)S(1)} %update_18.1.refs_3_, ...), custom_call_target="tpu_custom_call", output_to_operand_aliasing={{0}: (6, {})} | custom-call | flops 1 | bytes 1 | tf_op jit(solution)/shard_map/v_pass_18/pallas_call | solution.py:325
  49.8 3.4 %collective-permute-done.6.code_in = s16[784,256]{1,0:T(8,128)(2,1)S(1)} collective-permute-done((s16[784,256]{1,0:T(8,128)(2,1)S(1)}, s16[784,256]{1,0:T(8,128)(2,1)S(1)}, u32[]{:S(2)}, u32[]{:S(2)}) %collective-permute-start.6) | collective-permute-done | bytes 401440 | tf_op jit(solution)/shard_map/ppermute | solution.py:391
  53.2 0.3 update_30.1.refs_3_
  53.6 1.8 %collective-permute-start.5 = (s16[400,256]{1,0:T(8,128)(2,1)S(1)}, s16[400,256]{1,0:T(8,128)(2,1)S(1)}, u32[]{:S(2)}, u32[]{:S(2)}) collective-permute-start(s16[400,256]{1,0:T(8,128)(2,1)S(1)} %core_sum.9.refs_0_.code), channel_id=1, source_target_pairs={{0,2},{1,3},{2,0},{3,1},{4,6},{5,7},{6,4},{7,5},{8,10},{9,11},{10,... | collective-permute-start | bytes 614408 | tf_op jit(solution)/shard_map/ppermute | solution.py:391
  55.6 1.6 %collective-permute-start.15 = (bf16[16,256]{1,0:T(8,128)(2,1)S(1)}, bf16[16,256]{1,0:T(8,128)(2,1)S(1)}, u32[]{:S(2)}, u32[]{:S(2)}) collective-permute-start(bf16[16,256]{1,0:T(8,128)(2,1)S(1)} %get-tuple-element.58), channel_id=1, source_target_pairs={{0,3},{1,0},{2,1},{3,2},{4,7},{5,4},{6,5},{7,6},{8,11},{9,8},{10,9... | collective-permute-start | bytes 24584 | tf_op jit(solution)/shard_map/ppermute | solution.py:396
  57.2 2.6 %v_pass_30.1 = (bf16[6144,256]{1,0:T(8,128)(2,1)}, f32[256,1024]{1,0:T(8,128)S(1)}) custom-call(s32[384]{0:T(512)S(1)} %get-tuple-element.30.slots.refs_0_, bf16[1024,256]{1,0:T(8,128)(2,1)S(1)} %copy-done.1, bf16[154,128,128]{2,1,0:T(8,128)(2,1)S(1)} %bitcast.11, bf16[768,256]{1,0:T(8,128)(2,1)S(1)} %update_30.1.refs_3_, ...), custom_call_target="tpu_custom_call", output_to_operand_aliasing={{0}: (6, {})} | custom-call | flops 1 | bytes 1 | tf_op jit(solution)/shard_map/v_pass_30/pallas_call | solution.py:325
  59.8 1.0 %collective-permute-done.14.refs_1_.low = bf16[16,256]{1,0:T(8,128)(2,1)S(1)} collective-permute-done((bf16[16,256]{1,0:T(8,128)(2,1)S(1)}, bf16[16,256]{1,0:T(8,128)(2,1)S(1)}, u32[]{:S(2)}, u32[]{:S(2)}) %collective-permute-start.14) | collective-permute-done | bytes 8224 | tf_op jit(solution)/shard_map/ppermute | solution.py:396
  60.8 0.4 collective-permute-done.5.code_in
  61.6 1.3 %collective-permute-done.16.refs_4_ = bf16[384,256]{1,0:T(8,128)(2,1)S(1)} collective-permute-done((bf16[384,256]{1,0:T(8,128)(2,1)S(1)}, bf16[384,256]{1,0:T(8,128)(2,1)S(1)}, u32[]{:S(2)}, u32[]{:S(2)}) %collective-permute-start.16) | collective-permute-done | bytes 196640 | tf_op jit(solution)/shard_map/ppermute | solution.py:391
  62.9 2.4 %v_pass_42.1 = (bf16[6144,256]{1,0:T(8,128)(2,1)}, f32[128,256]{1,0:T(8,128)S(1)}, s16[144,256]{1,0:T(8,128)(2,1)S(1)}, s16[144,256]{1,0:T(8,128)(2,1)S(1)}, s16...) custom-call(s32[384]{0:T(512)S(1)} %get-tuple-element.30.slots.refs_, ...), custom_call_target="tpu_custom_call", output_to_operand_aliasing={{0}: (6, {})} | custom-call | flops 1 | bytes 1 | tf_op jit(solution)/shard_map/v_pass_42/pallas_call | solution.py:325
  65.3 1.7 %collective-permute-start.17 = (s16[144,256]{1,0:T(8,128)(2,1)S(1)}, s16[144,256]{1,0:T(8,128)(2,1)S(1)}, u32[]{:S(2)}, u32[]{:S(2)}) collective-permute-start(s16[144,256]{1,0:T(8,128)(2,1)S(1)} %get-tuple-element.51), channel_id=1, source_target_pairs={{0,4},{4,0},{8,12},{12,8},{16,20},{20,16},{24,28},{28,24},{1,5},{5... | collective-permute-start | bytes 221192 | tf_op jit(solution)/shard_map/ppermute | solution.py:391
  67.1 1.8 %collective-permute-start.18 = (s16[144,256]{1,0:T(8,128)(2,1)S(1)}, s16[144,256]{1,0:T(8,128)(2,1)S(1)}, u32[]{:S(2)}, u32[]{:S(2)}) collective-permute-start(s16[144,256]{1,0:T(8,128)(2,1)S(1)} %get-tuple-element.52), channel_id=1, source_target_pairs={{0,8},{4,12},{8,0},{12,4},{16,24},{20,28},{24,16},{28,20},{1,9},{5... | collective-permute-start | bytes 221192 | tf_op jit(solution)/shard_map/ppermute | solution.py:391
  68.9 2.7 %collective-permute-start.20 = (s16[144,256]{1,0:T(8,128)(2,1)S(1)}, s16[144,256]{1,0:T(8,128)(2,1)S(1)}, u32[]{:S(2)}, u32[]{:S(2)}) collective-permute-start(s16[144,256]{1,0:T(8,128)(2,1)S(1)} %get-tuple-element.54), channel_id=1, source_target_pairs={{0,16},{4,20},{8,24},{12,28},{16,0},{20,4},{24,8},{28,12},{1,17},{... | collective-permute-start | bytes 221192 | tf_op jit(solution)/shard_map/ppermute | solution.py:391
  71.6 1.3 %collective-permute-start.21 = (s16[144,256]{1,0:T(8,128)(2,1)S(1)}, s16[144,256]{1,0:T(8,128)(2,1)S(1)}, u32[]{:S(2)}, u32[]{:S(2)}) collective-permute-start(s16[144,256]{1,0:T(8,128)(2,1)S(1)} %get-tuple-element.55), channel_id=1, source_target_pairs={{0,20},{4,16},{8,28},{12,24},{16,4},{20,0},{24,12},{28,8},{1,21},{... | collective-permute-start | bytes 221192 | tf_op jit(solution)/shard_map/ppermute | solution.py:391
  72.9 3.7 %collective-permute-start.22 = (s16[144,256]{1,0:T(8,128)(2,1)S(1)}, s16[144,256]{1,0:T(8,128)(2,1)S(1)}, u32[]{:S(2)}, u32[]{:S(2)}) collective-permute-start(s16[144,256]{1,0:T(8,128)(2,1)S(1)} %get-tuple-element.56), channel_id=1, source_target_pairs={{0,24},{4,28},{8,16},{12,20},{16,8},{20,12},{24,0},{28,4},{1,25},{... | collective-permute-start | bytes 221192 | tf_op jit(solution)/shard_map/ppermute | solution.py:391
  76.7 6.1 %collective-permute-done.21.refs_4_ = s16[144,256]{1,0:T(8,128)(2,1)S(1)} collective-permute-done((s16[144,256]{1,0:T(8,128)(2,1)S(1)}, s16[144,256]{1,0:T(8,128)(2,1)S(1)}, u32[]{:S(2)}, u32[]{:S(2)}) %collective-permute-start.21) | collective-permute-done | bytes 73760 | tf_op jit(solution)/shard_map/ppermute | solution.py:391
  82.9 0.9 collective-permute-done.23.refs_6_
  84.1 3.1 %collective-permute-start.25 = (bf16[128,256]{1,0:T(8,128)(2,1)S(1)}, bf16[128,256]{1,0:T(8,128)(2,1)S(1)}, u32[]{:S(2)}, u32[]{:S(2)}) collective-permute-start(bf16[128,256]{1,0:T(8,128)(2,1)S(1)} %last_step.1.refs_0_), channel_id=1, source_target_pairs={{0,8},{4,12},{8,0},{12,4},{16,24},{20,28},{24,16},{28,20},{1,9},{5... | collective-permute-start | bytes 196616 | tf_op jit(solution)/shard_map/ppermute | solution.py:391
  87.2 1.4 %collective-permute-start.27 = (bf16[128,256]{1,0:T(8,128)(2,1)S(1)}, bf16[128,256]{1,0:T(8,128)(2,1)S(1)}, u32[]{:S(2)}, u32[]{:S(2)}) collective-permute-start(bf16[128,256]{1,0:T(8,128)(2,1)S(1)} %last_step.1.refs_0_), channel_id=1, source_target_pairs={{0,16},{4,20},{8,24},{12,28},{16,0},{20,4},{24,8},{28,12},{1,17},{... | collective-permute-start | bytes 196616 | tf_op jit(solution)/shard_map/ppermute | solution.py:391
  88.6 1.4 %collective-permute-start.29 = (bf16[128,256]{1,0:T(8,128)(2,1)S(1)}, bf16[128,256]{1,0:T(8,128)(2,1)S(1)}, u32[]{:S(2)}, u32[]{:S(2)}) collective-permute-start(bf16[128,256]{1,0:T(8,128)(2,1)S(1)} %last_step.1.refs_0_), channel_id=1, source_target_pairs={{0,24},{4,28},{8,16},{12,20},{16,8},{20,12},{24,0},{28,4},{1,25},{... | collective-permute-start | bytes 196616 | tf_op jit(solution)/shard_map/ppermute | solution.py:391
  90.0 0.7 collective-permute-start.24
  90.7 1.3 %collective-permute-start.26 = (bf16[128,256]{1,0:T(8,128)(2,1)S(1)}, bf16[128,256]{1,0:T(8,128)(2,1)S(1)}, u32[]{:S(2)}, u32[]{:S(2)}) collective-permute-start(bf16[128,256]{1,0:T(8,128)(2,1)S(1)} %collective-permute-done.25.refs_2_), channel_id=1, source_target_pairs={{0,4},{4,0},{8,12},{12,8},{16,20},{20,16},{24,28},{28,24},{1,5},{5... | collective-permute-start | bytes 196616 | tf_op jit(solution)/shard_map/ppermute | solution.py:391
  92.0 3.3 %collective-permute-done.27.refs_4_ = bf16[128,256]{1,0:T(8,128)(2,1)S(1)} collective-permute-done((bf16[128,256]{1,0:T(8,128)(2,1)S(1)}, bf16[128,256]{1,0:T(8,128)(2,1)S(1)}, u32[]{:S(2)}, u32[]{:S(2)}) %collective-permute-start.27) | collective-permute-done | bytes 65568 | tf_op jit(solution)/shard_map/ppermute | solution.py:391
  95.4 0.4 collective-permute-start.28
  95.8 1.6 %collective-permute-start.30 = (bf16[128,256]{1,0:T(8,128)(2,1)S(1)}, bf16[128,256]{1,0:T(8,128)(2,1)S(1)}, u32[]{:S(2)}, u32[]{:S(2)}) collective-permute-start(bf16[128,256]{1,0:T(8,128)(2,1)S(1)} %collective-permute-done.29.refs_6_), channel_id=1, source_target_pairs={{0,4},{4,0},{8,12},{12,8},{16,20},{20,16},{24,28},{28,24},{1,5},{5... | collective-permute-start | bytes 196616 | tf_op jit(solution)/shard_map/ppermute | solution.py:391
  97.4 2.2 %collective-permute-done.28.refs_5_ = bf16[128,256]{1,0:T(8,128)(2,1)S(1)} collective-permute-done((bf16[128,256]{1,0:T(8,128)(2,1)S(1)}, bf16[128,256]{1,0:T(8,128)(2,1)S(1)}, u32[]{:S(2)}, u32[]{:S(2)}) %collective-permute-start.28) | collective-permute-done | bytes 65568 | tf_op jit(solution)/shard_map/ppermute | solution.py:391
  99.6 0.7 collective-permute-done.30.refs_7_
  100.3 0.8 join.1
  (46 shorter events, 2.6 us)
Async XLA Ops:
  1.3 6.6 %slice-start = ((s8[5046272]{0:T(1024)(128)(4,1)}), s8[4194304]{0:T(1024)(128)(4,1)S(1)}, s32[]{:S(2)}) async-start(s8[5046272]{0:T(1024)(128)(4,1)} %bitcast.2), calls=%async_computation | async-start | bytes 8388608
  1.3 6.6 %slice-start.1 = ((s8[5046272]{0:T(1024)(128)(4,1)}), s8[851968]{0:T(1024)(128)(4,1)S(1)}, s32[]{:S(2)}) async-start(s8[5046272]{0:T(1024)(128)(4,1)} %bitcast.2), calls=%async_computation.1 | async-start | bytes 1703936
  1.3 6.6 %copy-start = (bf16[6144,256]{1,0:T(8,128)(2,1)S(1)}, bf16[6144,256]{1,0:T(8,128)(2,1)}, u32[]{:S(2)}) copy-start(bf16[6144,256]{1,0:T(8,128)(2,1)} %u_ref.17) | copy-start | bytes 9437188
  1.3 6.6 %copy-start.1 = (bf16[1024,256]{1,0:T(8,128)(2,1)S(1)}, bf16[1024,256]{1,0:T(8,128)(2,1)}, u32[]{:S(2)}) copy-start(bf16[1024,256]{1,0:T(8,128)(2,1)} %v_ref.9) | copy-start | bytes 1572868
  5.9 1.8 %collective-permute-start = (f32[384,256]{1,0:T(8,128)S(1)}, f32[384,256]{1,0:T(8,128)S(1)}, u32[]{:S(2)}, u32[]{:S(2)}) collective-permute-start(f32[384,256]{1,0:T(8,128)S(1)} %get-tuple-element.32), channel_id=1, source_target_pairs={{0,1},{1,0},{2,3},{3,2},{4,5},{5,4},{6,7},{7,6},{8,9},{9,8},{10,11... | collective-permute-start | bytes 1179656 | tf_op jit(solution)/shard_map/ppermute | solution.py:391
  10.5 3.2 %collective-permute-start.2 = (f32[768,256]{1,0:T(8,128)S(1)}, f32[768,256]{1,0:T(8,128)S(1)}, u32[]{:S(2)}, u32[]{:S(2)}) collective-permute-start(f32[768,256]{1,0:T(8,128)S(1)} %get-tuple-element.36), channel_id=1, source_target_pairs={{0,1},{1,0},{2,3},{3,2},{4,5},{5,4},{6,7},{7,6},{8,9},{9,8},{10,11... | collective-permute-start | bytes 2359304 | tf_op jit(solution)/shard_map/ppermute | solution.py:391
  13.5 3.4 %collective-permute-start.1 = (f32[768,256]{1,0:T(8,128)S(1)}, f32[768,256]{1,0:T(8,128)S(1)}, u32[]{:S(2)}, u32[]{:S(2)}) collective-permute-start(f32[768,256]{1,0:T(8,128)S(1)} %get-tuple-element.34), channel_id=1, source_target_pairs={{0,1},{1,0},{2,3},{3,2},{4,5},{5,4},{6,7},{7,6},{8,9},{9,8},{10,11... | collective-permute-start | bytes 2359304 | tf_op jit(solution)/shard_map/ppermute | solution.py:391
  16.5 5.5 %collective-permute-start.4 = (f32[768,256]{1,0:T(8,128)S(1)}, f32[768,256]{1,0:T(8,128)S(1)}, u32[]{:S(2)}, u32[]{:S(2)}) collective-permute-start(f32[768,256]{1,0:T(8,128)S(1)} %get-tuple-element.40), channel_id=1, source_target_pairs={{0,1},{1,0},{2,3},{3,2},{4,5},{5,4},{6,7},{7,6},{8,9},{9,8},{10,11... | collective-permute-start | bytes 2359304 | tf_op jit(solution)/shard_map/ppermute | solution.py:391
  19.0 3.2 %collective-permute-start.3 = (f32[384,256]{1,0:T(8,128)S(1)}, f32[384,256]{1,0:T(8,128)S(1)}, u32[]{:S(2)}, u32[]{:S(2)}) collective-permute-start(f32[384,256]{1,0:T(8,128)S(1)} %get-tuple-element.39), channel_id=1, source_target_pairs={{0,1},{1,0},{2,3},{3,2},{4,5},{5,4},{6,7},{7,6},{8,9},{9,8},{10,11... | collective-permute-start | bytes 1179656 | tf_op jit(solution)/shard_map/ppermute | solution.py:391
  19.2 8.6 %collective-permute-start.9 = (s16[400,256]{1,0:T(8,128)(2,1)S(1)}, s16[400,256]{1,0:T(8,128)(2,1)S(1)}, u32[]{:S(2)}, u32[]{:S(2)}) collective-permute-start(s16[400,256]{1,0:T(8,128)(2,1)S(1)} %core_sum.5.refs_0_.code), channel_id=1, source_target_pairs={{0,2},{1,3},{2,0},{3,1},{4,6},{5,7},{6,4},{7,5},{8,10},{9,11},{10,... | collective-permute-start | bytes 614408 | tf_op jit(solution)/shard_map/ppermute | solution.py:391
  22.0 14.5 %collective-permute-start.8 = (s16[784,256]{1,0:T(8,128)(2,1)S(1)}, s16[784,256]{1,0:T(8,128)(2,1)S(1)}, u32[]{:S(2)}, u32[]{:S(2)}) collective-permute-start(s16[784,256]{1,0:T(8,128)(2,1)S(1)} %core_sum.6.refs_0_.code), channel_id=1, source_target_pairs={{0,2},{1,3},{2,0},{3,1},{4,6},{5,7},{6,4},{7,5},{8,10},{9,11},{10,... | collective-permute-start | bytes 1204232 | tf_op jit(solution)/shard_map/ppermute | solution.py:391
  28.0 2.2 %collective-permute-start.10 = (bf16[384,256]{1,0:T(8,128)(2,1)S(1)}, bf16[384,256]{1,0:T(8,128)(2,1)S(1)}, u32[]{:S(2)}, u32[]{:S(2)}) collective-permute-start(bf16[384,256]{1,0:T(8,128)(2,1)S(1)} %update_0.1.refs_3_), channel_id=1, source_target_pairs={{0,1},{1,0},{2,3},{3,2},{4,5},{5,4},{6,7},{7,6},{8,9},{9,8},{10,11... | collective-permute-start | bytes 589832 | tf_op jit(solution)/shard_map/ppermute | solution.py:391
  28.1 17.0 %collective-permute-start.7 = (s16[784,256]{1,0:T(8,128)(2,1)S(1)}, s16[784,256]{1,0:T(8,128)(2,1)S(1)}, u32[]{:S(2)}, u32[]{:S(2)}) collective-permute-start(s16[784,256]{1,0:T(8,128)(2,1)S(1)} %core_sum.7.refs_0_.code), channel_id=1, source_target_pairs={{0,2},{1,3},{2,0},{3,1},{4,6},{5,7},{6,4},{7,5},{8,10},{9,11},{10,... | collective-permute-start | bytes 1204232 | tf_op jit(solution)/shard_map/ppermute | solution.py:391
  36.8 2.2 %collective-permute-start.11 = (bf16[768,256]{1,0:T(8,128)(2,1)S(1)}, bf16[768,256]{1,0:T(8,128)(2,1)S(1)}, u32[]{:S(2)}, u32[]{:S(2)}) collective-permute-start(bf16[768,256]{1,0:T(8,128)(2,1)S(1)} %update_6.1.refs_3_), channel_id=1, source_target_pairs={{0,1},{1,0},{2,3},{3,2},{4,5},{5,4},{6,7},{7,6},{8,9},{9,8},{10,11... | collective-permute-start | bytes 1179656 | tf_op jit(solution)/shard_map/ppermute | solution.py:391
  36.9 16.3 %collective-permute-start.6 = (s16[784,256]{1,0:T(8,128)(2,1)S(1)}, s16[784,256]{1,0:T(8,128)(2,1)S(1)}, u32[]{:S(2)}, u32[]{:S(2)}) collective-permute-start(s16[784,256]{1,0:T(8,128)(2,1)S(1)} %core_sum.8.refs_0_.code), channel_id=1, source_target_pairs={{0,2},{1,3},{2,0},{3,1},{4,6},{5,7},{6,4},{7,5},{8,10},{9,11},{10,... | collective-permute-start | bytes 1204232 | tf_op jit(solution)/shard_map/ppermute | solution.py:391
  45.4 1.8 %collective-permute-start.12 = (bf16[768,256]{1,0:T(8,128)(2,1)S(1)}, bf16[768,256]{1,0:T(8,128)(2,1)S(1)}, u32[]{:S(2)}, u32[]{:S(2)}) collective-permute-start(bf16[768,256]{1,0:T(8,128)(2,1)S(1)} %update_18.1.refs_3_), channel_id=1, source_target_pairs={{0,1},{1,0},{2,3},{3,2},{4,5},{5,4},{6,7},{7,6},{8,9},{9,8},{10,11... | collective-permute-start | bytes 1179656 | tf_op jit(solution)/shard_map/ppermute | solution.py:391
  53.5 3.6 %collective-permute-start.13 = (bf16[768,256]{1,0:T(8,128)(2,1)S(1)}, bf16[768,256]{1,0:T(8,128)(2,1)S(1)}, u32[]{:S(2)}, u32[]{:S(2)}) collective-permute-start(bf16[768,256]{1,0:T(8,128)(2,1)S(1)} %update_30.1.refs_3_), channel_id=1, source_target_pairs={{0,1},{1,0},{2,3},{3,2},{4,5},{5,4},{6,7},{7,6},{8,9},{9,8},{10,11... | collective-permute-start | bytes 1179656 | tf_op jit(solution)/shard_map/ppermute | solution.py:391
  53.6 7.6 %collective-permute-start.5 = (s16[400,256]{1,0:T(8,128)(2,1)S(1)}, s16[400,256]{1,0:T(8,128)(2,1)S(1)}, u32[]{:S(2)}, u32[]{:S(2)}) collective-permute-start(s16[400,256]{1,0:T(8,128)(2,1)S(1)} %core_sum.9.refs_0_.code), channel_id=1, source_target_pairs={{0,2},{1,3},{2,0},{3,1},{4,6},{5,7},{6,4},{7,5},{8,10},{9,11},{10,... | collective-permute-start | bytes 614408 | tf_op jit(solution)/shard_map/ppermute | solution.py:391
  55.4 5.4 %collective-permute-start.14 = (bf16[16,256]{1,0:T(8,128)(2,1)S(1)}, bf16[16,256]{1,0:T(8,128)(2,1)S(1)}, u32[]{:S(2)}, u32[]{:S(2)}) collective-permute-start(bf16[16,256]{1,0:T(8,128)(2,1)S(1)} %get-tuple-element.59), channel_id=1, source_target_pairs={{0,1},{1,2},{2,3},{3,0},{4,5},{5,6},{6,7},{7,4},{8,9},{9,10},{10,1... | collective-permute-start | bytes 24584 | tf_op jit(solution)/shard_map/ppermute | solution.py:396
  55.6 5.2 %collective-permute-start.15 = (bf16[16,256]{1,0:T(8,128)(2,1)S(1)}, bf16[16,256]{1,0:T(8,128)(2,1)S(1)}, u32[]{:S(2)}, u32[]{:S(2)}) collective-permute-start(bf16[16,256]{1,0:T(8,128)(2,1)S(1)} %get-tuple-element.58), channel_id=1, source_target_pairs={{0,3},{1,0},{2,1},{3,2},{4,7},{5,4},{6,5},{7,6},{8,11},{9,8},{10,9... | collective-permute-start | bytes 24584 | tf_op jit(solution)/shard_map/ppermute | solution.py:396
  61.4 1.5 %collective-permute-start.16 = (bf16[384,256]{1,0:T(8,128)(2,1)S(1)}, bf16[384,256]{1,0:T(8,128)(2,1)S(1)}, u32[]{:S(2)}, u32[]{:S(2)}) collective-permute-start(bf16[384,256]{1,0:T(8,128)(2,1)S(1)} %update_42.1.refs_3_), channel_id=1, source_target_pairs={{0,1},{1,0},{2,3},{3,2},{4,5},{5,4},{6,7},{7,6},{8,9},{9,8},{10,11... | collective-permute-start | bytes 589832 | tf_op jit(solution)/shard_map/ppermute | solution.py:391
  65.3 7.6 %collective-permute-start.17 = (s16[144,256]{1,0:T(8,128)(2,1)S(1)}, s16[144,256]{1,0:T(8,128)(2,1)S(1)}, u32[]{:S(2)}, u32[]{:S(2)}) collective-permute-start(s16[144,256]{1,0:T(8,128)(2,1)S(1)} %get-tuple-element.51), channel_id=1, source_target_pairs={{0,4},{4,0},{8,12},{12,8},{16,20},{20,16},{24,28},{28,24},{1,5},{5... | collective-permute-start | bytes 221192 | tf_op jit(solution)/shard_map/ppermute | solution.py:391
  67.1 9.6 %collective-permute-start.18 = (s16[144,256]{1,0:T(8,128)(2,1)S(1)}, s16[144,256]{1,0:T(8,128)(2,1)S(1)}, u32[]{:S(2)}, u32[]{:S(2)}) collective-permute-start(s16[144,256]{1,0:T(8,128)(2,1)S(1)} %get-tuple-element.52), channel_id=1, source_target_pairs={{0,8},{4,12},{8,0},{12,4},{16,24},{20,28},{24,16},{28,20},{1,9},{5... | collective-permute-start | bytes 221192 | tf_op jit(solution)/shard_map/ppermute | solution.py:391
  68.9 7.9 %collective-permute-start.19 = (s16[144,256]{1,0:T(8,128)(2,1)S(1)}, s16[144,256]{1,0:T(8,128)(2,1)S(1)}, u32[]{:S(2)}, u32[]{:S(2)}) collective-permute-start(s16[144,256]{1,0:T(8,128)(2,1)S(1)} %get-tuple-element.53), channel_id=1, source_target_pairs={{0,12},{4,8},{8,4},{12,0},{16,28},{20,24},{24,20},{28,16},{1,13},{... | collective-permute-start | bytes 221192 | tf_op jit(solution)/shard_map/ppermute | solution.py:391
  68.9 7.9 %collective-permute-start.20 = (s16[144,256]{1,0:T(8,128)(2,1)S(1)}, s16[144,256]{1,0:T(8,128)(2,1)S(1)}, u32[]{:S(2)}, u32[]{:S(2)}) collective-permute-start(s16[144,256]{1,0:T(8,128)(2,1)S(1)} %get-tuple-element.54), channel_id=1, source_target_pairs={{0,16},{4,20},{8,24},{12,28},{16,0},{20,4},{24,8},{28,12},{1,17},{... | collective-permute-start | bytes 221192 | tf_op jit(solution)/shard_map/ppermute | solution.py:391
  71.6 11.3 %collective-permute-start.21 = (s16[144,256]{1,0:T(8,128)(2,1)S(1)}, s16[144,256]{1,0:T(8,128)(2,1)S(1)}, u32[]{:S(2)}, u32[]{:S(2)}) collective-permute-start(s16[144,256]{1,0:T(8,128)(2,1)S(1)} %get-tuple-element.55), channel_id=1, source_target_pairs={{0,20},{4,16},{8,28},{12,24},{16,4},{20,0},{24,12},{28,8},{1,21},{... | collective-permute-start | bytes 221192 | tf_op jit(solution)/shard_map/ppermute | solution.py:391
  72.9 9.9 %collective-permute-start.22 = (s16[144,256]{1,0:T(8,128)(2,1)S(1)}, s16[144,256]{1,0:T(8,128)(2,1)S(1)}, u32[]{:S(2)}, u32[]{:S(2)}) collective-permute-start(s16[144,256]{1,0:T(8,128)(2,1)S(1)} %get-tuple-element.56), channel_id=1, source_target_pairs={{0,24},{4,28},{8,16},{12,20},{16,8},{20,12},{24,0},{28,4},{1,25},{... | collective-permute-start | bytes 221192 | tf_op jit(solution)/shard_map/ppermute | solution.py:391
  76.6 7.2 %collective-permute-start.23 = (s16[144,256]{1,0:T(8,128)(2,1)S(1)}, s16[144,256]{1,0:T(8,128)(2,1)S(1)}, u32[]{:S(2)}, u32[]{:S(2)}) collective-permute-start(s16[144,256]{1,0:T(8,128)(2,1)S(1)} %get-tuple-element.57), channel_id=1, source_target_pairs={{0,28},{4,24},{8,20},{12,16},{16,12},{20,8},{24,4},{28,0},{1,29},{... | collective-permute-start | bytes 221192 | tf_op jit(solution)/shard_map/ppermute | solution.py:391
  84.1 6.6 %collective-permute-start.25 = (bf16[128,256]{1,0:T(8,128)(2,1)S(1)}, bf16[128,256]{1,0:T(8,128)(2,1)S(1)}, u32[]{:S(2)}, u32[]{:S(2)}) collective-permute-start(bf16[128,256]{1,0:T(8,128)(2,1)S(1)} %last_step.1.refs_0_), channel_id=1, source_target_pairs={{0,8},{4,12},{8,0},{12,4},{16,24},{20,28},{24,16},{28,20},{1,9},{5... | collective-permute-start | bytes 196616 | tf_op jit(solution)/shard_map/ppermute | solution.py:391
  87.2 8.2 %collective-permute-start.27 = (bf16[128,256]{1,0:T(8,128)(2,1)S(1)}, bf16[128,256]{1,0:T(8,128)(2,1)S(1)}, u32[]{:S(2)}, u32[]{:S(2)}) collective-permute-start(bf16[128,256]{1,0:T(8,128)(2,1)S(1)} %last_step.1.refs_0_), channel_id=1, source_target_pairs={{0,16},{4,20},{8,24},{12,28},{16,0},{20,4},{24,8},{28,12},{1,17},{... | collective-permute-start | bytes 196616 | tf_op jit(solution)/shard_map/ppermute | solution.py:391
  88.6 7.2 %collective-permute-start.29 = (bf16[128,256]{1,0:T(8,128)(2,1)S(1)}, bf16[128,256]{1,0:T(8,128)(2,1)S(1)}, u32[]{:S(2)}, u32[]{:S(2)}) collective-permute-start(bf16[128,256]{1,0:T(8,128)(2,1)S(1)} %last_step.1.refs_0_), channel_id=1, source_target_pairs={{0,24},{4,28},{8,16},{12,20},{16,8},{20,12},{24,0},{28,4},{1,25},{... | collective-permute-start | bytes 196616 | tf_op jit(solution)/shard_map/ppermute | solution.py:391
  90.0 7.4 %collective-permute-start.24 = (bf16[128,256]{1,0:T(8,128)(2,1)S(1)}, bf16[128,256]{1,0:T(8,128)(2,1)S(1)}, u32[]{:S(2)}, u32[]{:S(2)}) collective-permute-start(bf16[128,256]{1,0:T(8,128)(2,1)S(1)} %last_step.1.refs_0_), channel_id=1, source_target_pairs={{0,4},{4,0},{8,12},{12,8},{16,20},{20,16},{24,28},{28,24},{1,5},{5... | collective-permute-start | bytes 196616 | tf_op jit(solution)/shard_map/ppermute | solution.py:391
  90.7 6.7 %collective-permute-start.26 = (bf16[128,256]{1,0:T(8,128)(2,1)S(1)}, bf16[128,256]{1,0:T(8,128)(2,1)S(1)}, u32[]{:S(2)}, u32[]{:S(2)}) collective-permute-start(bf16[128,256]{1,0:T(8,128)(2,1)S(1)} %collective-permute-done.25.refs_2_), channel_id=1, source_target_pairs={{0,4},{4,0},{8,12},{12,8},{16,20},{20,16},{24,28},{28,24},{1,5},{5... | collective-permute-start | bytes 196616 | tf_op jit(solution)/shard_map/ppermute | solution.py:391
  95.4 4.3 %collective-permute-start.28 = (bf16[128,256]{1,0:T(8,128)(2,1)S(1)}, bf16[128,256]{1,0:T(8,128)(2,1)S(1)}, u32[]{:S(2)}, u32[]{:S(2)}) collective-permute-start(bf16[128,256]{1,0:T(8,128)(2,1)S(1)} %collective-permute-done.27.refs_4_), channel_id=1, source_target_pairs={{0,4},{4,0},{8,12},{12,8},{16,20},{20,16},{24,28},{28,24},{1,5},{5... | collective-permute-start | bytes 196616 | tf_op jit(solution)/shard_map/ppermute | solution.py:391
  95.8 4.6 %collective-permute-start.30 = (bf16[128,256]{1,0:T(8,128)(2,1)S(1)}, bf16[128,256]{1,0:T(8,128)(2,1)S(1)}, u32[]{:S(2)}, u32[]{:S(2)}) collective-permute-start(bf16[128,256]{1,0:T(8,128)(2,1)S(1)} %collective-permute-done.29.refs_6_), channel_id=1, source_target_pairs={{0,4},{4,0},{8,12},{12,8},{16,20},{20,16},{24,28},{28,24},{1,5},{5... | collective-permute-start | bytes 196616 | tf_op jit(solution)/shard_map/ppermute | solution.py:391

commit v3 on v2

--- a/solution.py
+++ b/solution.py
@@ -87,8 +87,11 @@
 
 
 def split_product(err, v_ref, outs):
-    for out, rows in zip(outs, two_halves(err.shape[0])):
-        out[...] = jnp.dot(err[rows, :], v_ref[...], preferred_element_type=f32)
+    for out, rows in zip((outs[:1], outs[1:]), two_halves(err.shape[0])):
+        whole = jnp.dot(err[rows, :], v_ref[...], preferred_element_type=f32)
+        size = out[0].shape[0]
+        for i, piece in enumerate(out):
+            piece[...] = whole[i * size : (i + 1) * size]
 
 
 def first_u_body(
@@ -180,20 +183,21 @@
 
 
 def u_body(first, count, across, waits, slots, u_ref, v_ref, values, *refs):
-    keep, send, err = refs[waits:]
+    outs, err = refs[waits:-1], refs[-1]
     block = lambda slot, r, c: values[jnp.maximum(slot, 0)]
     residual(u_ref[first * B : (first + count) * B, :], v_ref, block, err, slots, first, count, across)
-    split_product(err, v_ref, (keep, send))
-
-
-def u_pass(first, count, across, slots, u, v, values, after):
+    split_product(err, v_ref, outs)
+
+
+def u_pass(first, count, across, pieces, slots, u, v, values, after):
     rows, width = count * B, u.shape[1]
     part = jax.ShapeDtypeStruct((rows // 2, width), f32)
+    piece = jax.ShapeDtypeStruct((rows // 2 // pieces, width), f32)
     return pl.pallas_call(
         functools.partial(u_body, first, count, across, len(after)),
-        out_shape=[part, part],
+        out_shape=[part] + [piece] * pieces,
         in_specs=[SMEM, VMEM, VMEM, VMEM] + [ANY] * len(after),
-        out_specs=[VMEM, VMEM],
+        out_specs=[VMEM] * (1 + pieces),
         scratch_shapes=[pltpu.VMEM((rows, across * B), bf16)],
         compiler_params=params(),
         cost_estimate=SMALL,
@@ -201,21 +205,21 @@
     )(slots, u, v, values, *after)
 
 
-def sum_body(own, other, *refs):
-    store_code(refs[-1], own[...] + other[...])
-
-
-def core_sum(own, other, after):
+def sum_body(own, *refs):
+    store_code(refs[-1], own[...] + jnp.concatenate([x[...] for x in refs[:-1]], axis=0))
+
+
+def core_sum(own, others):
     rows, width = own.shape
     return pl.pallas_call(
         sum_body,
         out_shape=jax.ShapeDtypeStruct((rows + PAD, width), i16),
-        in_specs=[VMEM, VMEM] + [ANY] * len(after),
+        in_specs=[VMEM] * (1 + len(others)),
         out_specs=VMEM,
         compiler_params=params(),
         cost_estimate=SMALL,
         name="core_sum",
-    )(own, other, *after)
+    )(own, *others)
 
 
 def again_body(mine, mine_in, out):
@@ -411,36 +415,52 @@
     high = shift(v[:PAD], "step", -1)
     chunks = chunks_of(down)
     keep, send, slots = first_u_pass(chunks[0][1], down, across, (block_rows, block_cols, block_counts), u, v, values)
-    codes = [core_sum(keep, swap(send, "step", 1), [])]
-    waiting = None
-    for first, count in chunks[1:]:
-        keep, send = u_pass(first, count, across, slots, u, v, values, codes[-1:])
-        if waiting:
-            codes.append(core_sum(*waiting, [keep]))
-        waiting = (keep, swap(send, "step", 1))
-    codes.append(core_sum(*waiting, codes[-1:]))
-    arrived = []
-    for code in codes:
+    codes = [core_sum(keep, [swap(send, "step", 1)])]
+    arrived, halves = [], []
+    before = None
+    last = len(chunks) - 1
+
+    def cross(k):
+        code, mask = codes[k], 4
         code_in = swap(code, "step", 2)
-        mask = 4
         while mask < steps:
             code = chip_sum(code, code_in)
             code_in = swap(code, "step", mask)
             mask *= 2
         arrived.append((code, code_in))
-    before = None
-    for i, (first, count) in enumerate(chunks):
-        after = [codes[-1]] if before is None else [before[1]]
-        if i == len(chunks) - 1:
-            after += [low, high]
-        half = update(first, *arrived[i], u, after)
-        halves = (half, swap(half, "step", 1))
-        shards = peers if i == len(chunks) - 1 else 0
-        before = v_pass(first, count, across, slots, u.shape, v, values, halves, before, shards)
+
+    def renew(k, after):
+        half = update(chunks[k][0], *arrived[k], u, after)
+        halves.append((half, swap(half, "step", 1)))
+
+    cross(0)
+    token = codes[0]
+    for k in range(1, last + 2):
+        if k <= last:
+            first, count = chunks[k]
+            pieces = pl.cdiv(2 * count, chunks[k - 1][1])
+            while count * B // 2 % (8 * pieces):
+                pieces += 1
+            keep, *send = u_pass(first, count, across, pieces, slots, u, v, values, [token])
+            codes.append(core_sum(keep, [swap(x, "step", 1) for x in send]))
+            cross(k)
+        if k >= 2:
+            first, count = chunks[k - 2]
+            before = v_pass(first, count, across, slots, u.shape, v, values, halves[k - 2], before, 0)
+        renew(k - 1, [codes[-1]] + ([before[1]] if before else []) + ([low, high] if k > last else []))
+        token = halves[k - 1][0]
+    first, count = chunks[last]
+    before = v_pass(first, count, across, slots, u.shape, v, values, halves[last], before, peers)
     new_services, own, sent = before[0], before[1], before[2:]
-    part = last_step(v, low, high, own, [swap(x, "svc", d + 1) for d, x in enumerate(sent)])
-    column = [part] + [swap(part, "svc", d) for d in range(2, peers, 2)]
-    return new_services, join([x for y in column for x in (y, swap(y, "svc", 1))])
+    far_first = sorted(range(1, peers), reverse=True)
+    part = last_step(v, low, high, own, [swap(sent[d - 1], "svc", d) for d in far_first])
+    column = {0: part}
+    for d in far_first:
+        if d % 2 == 0:
+            column[d] = swap(part, "svc", d)
+    for d in (0, *(x for x in far_first if x % 2 == 0)):
+        column[d + 1] = swap(column[d], "svc", 1)
+    return new_services, join([column[d] for d in range(peers)])
 
 
 def solution(mesh):

time: 101 us -> 89.8 us (0.89)
  waiting for transfers between devices: 35.5 us -> 26 us
  starting transfers between devices: 34.2 us -> 32.1 us
    ppermute x29 -> x34, waiting for transfers between devices: 34.5 us -> 23.9 us  [swap(): lax.ppermute(x, axis, [(i, i ^ mask) for i in range(lax.axis_size(axis))])]
    ppermute x29 -> x34, starting transfers between devices: 32.5 us -> 30.3 us  [swap(): lax.ppermute(x, axis, [(i, i ^ mask) for i in range(lax.axis_size(axis))])]
    ppermute x2, waiting for transfers between devices: 1.02 us -> 2.11 us  [shift(): return lax.ppermute(x, axis, [(i, (i + by) % n) for i in range(n)])]
  transfers between devices with their start and end apart: 31 -> 36, of which waited for: 14 -> 23; matrix products, arithmetic and copies ran while one was open for 0% -> 0% of each run, Pallas kernels for 18% -> 24%
where the time goes in v3:
time: 89.8 us; the launch traced here: 89.6 us
  starting transfers between devices  32.1 us (36%)
  Pallas kernels  30 us (33%)
  waiting for transfers between devices  26 us (29%)
  between operations  1.53 us (2%)
    ppermute x34, starting transfers between devices, swap(): lax.ppermute(x, axis, [(i, i ^ mask) for i in range(lax.axis_size(axis))])  30.3 us
    ppermute x34, waiting for transfers between devices, swap(): lax.ppermute(x, axis, [(i, i ^ mask) for i in range(lax.axis_size(axis))])  23.9 us
    pallas_call x5, Pallas kernels, v_pass(): pl.pallas_call(functools.partial(v_body, first, count, across, opening, s...  12.3 us
    pallas_call x4, Pallas kernels, u_pass(): pl.pallas_call(functools.partial(u_body, first, count, across, len(after)...  9.82 us
    pallas_call x1, Pallas kernels, first_u_pass(): pl.pallas_call(functools.partial(first_u_body, count, down, across), out_...  4.67 us
    ppermute x2, waiting for transfers between devices, shift(): return lax.ppermute(x, axis, [(i, (i + by) % n) for i in range(n)])  2.11 us
  transfers between devices with their start and end apart: 36, of which 23 were waited for; matrix products, arithmetic and copies ran while one was open for 0% of the time, Pallas kernels for 24%

profile of v3, /device:TPU:0, one launch (start us, length us, event | category | flops | bytes accessed | tf_op | source)
XLA Modules:
  0.0 89.6 jit_solution(6486459484883005239)
XLA Ops:
  1.3 4.7 %u_pass_0.1 = (f32[384,256]{1,0:T(8,128)S(1)}, f32[384,256]{1,0:T(8,128)S(1)}, s32[384]{0:T(512)S(1)}) custom-call(s32[1,1,154]{2,1,0:T(1,128)} %row_hbm.1, s32[1,1,154]{2,1,0:T(1,128)} %col_hbm.1, s32[1,1]{1,0:T(1,128)S(6)} %copy.16.live_hbm, bf16[6144,256]{1,0:T(8,128)(2,1)} %u_ref.17, bf16[1024,256]{1,0:T(8,128)(2,1)} %v_ref.9, bf16[154,128,128]{2,1,0:T(8,128)(2,1)} %bitcast.1), custom_call_target="tpu_custom_call" | custom-call | flops 1 | bytes 1 | tf_op jit(solution)/shard_map/u_pass_0/pallas_call | solution.py:166
  6.0 0.5 collective-permute-start
  6.5 1.3 %collective-permute-done.refs_0_ = f32[384,256]{1,0:T(8,128)S(1)} collective-permute-done((f32[384,256]{1,0:T(8,128)S(1)}, f32[384,256]{1,0:T(8,128)S(1)}, u32[]{:S(2)}, u32[]{:S(2)}) %collective-permute-start) | collective-permute-done | bytes 393248 | tf_op jit(solution)/shard_map/ppermute | solution.py:395
  8.0 2.6 %collective-permute-start.1 = (s16[400,256]{1,0:T(8,128)(2,1)S(1)}, s16[400,256]{1,0:T(8,128)(2,1)S(1)}, u32[]{:S(2)}, u32[]{:S(2)}) collective-permute-start(s16[400,256]{1,0:T(8,128)(2,1)S(1)} %core_sum.5.refs_0_.code), channel_id=1, source_target_pairs={{0,2},{1,3},{2,0},{3,1},{4,6},{5,7},{6,4},{7,5},{8,10},{9,11},{10,... | collective-permute-start | bytes 614408 | tf_op jit(solution)/shard_map/ppermute | solution.py:395
  10.6 2.6 %u_pass_6.1 = (f32[768,256]{1,0:T(8,128)S(1)}, f32[192,256]{1,0:T(8,128)S(1)}, f32[192,256]{1,0:T(8,128)S(1)}, f32[192,256]{1,0:T(8,128)S(1)}, f32[192,256]{1,0:T(8,128)S(1)}) custom-call(s32[384]{0:T(512)S(1)} %get-tuple-element.35.slots.refs_0_, bf16[6144,256]{1,0:T(8,128)(2,1)S(1)} %copy-done, bf16[1024,256]{1,0:T(8,128)(2,1)S(1)} %copy-done.1, ...), custom_call_target="tpu_custom_call" | custom-call | flops 1 | bytes 1 | tf_op jit(solution)/shard_map/u_pass_6/pallas_call | solution.py:196
  13.2 0.5 collective-permute-start.3
  13.8 0.4 collective-permute-start.5
  16.1 2.6 %u_pass_18.1 = (f32[768,256]{1,0:T(8,128)S(1)}, f32[384,256]{1,0:T(8,128)S(1)}, f32[384,256]{1,0:T(8,128)S(1)}) custom-call(s32[384]{0:T(512)S(1)} %get-tuple-element.35.slots.refs_0_, bf16[6144,256]{1,0:T(8,128)(2,1)S(1)} %copy-done, bf16[1024,256]{1,0:T(8,128)(2,1)S(1)} %copy-done.1, bf16[154,128,128]{2,1,0:T(8,128)(2,1)S(1)} %bitcast.5, ...), custom_call_target="tpu_custom_call" | custom-call | flops 1 | bytes 1 | tf_op jit(solution)/shard_map/u_pass_18/pallas_call | solution.py:196
  19.4 2.0 %collective-permute-done.10.refs_4_ = bf16[384,256]{1,0:T(8,128)(2,1)S(1)} collective-permute-done((bf16[384,256]{1,0:T(8,128)(2,1)S(1)}, bf16[384,256]{1,0:T(8,128)(2,1)S(1)}, u32[]{:S(2)}, u32[]{:S(2)}) %collective-permute-start.10) | collective-permute-done | bytes 196640 | tf_op jit(solution)/shard_map/ppermute | solution.py:395
  21.3 2.0 %v_pass_0.1 = (bf16[6144,256]{1,0:T(8,128)(2,1)}, f32[256,1024]{1,0:T(8,128)S(1)}) custom-call(s32[384]{0:T(512)S(1)} %get-tuple-element.35.slots.refs_0_, bf16[1024,256]{1,0:T(8,128)(2,1)S(1)} %copy-done.1, bf16[154,128,128]{2,1,0:T(8,128)(2,1)S(1)} %bitcast.6, bf16[384,256]{1,0:T(8,128)(2,1)S(1)} %update_0.1.refs_0_.refs_3_, ...), custom_call_target="tpu_custom_call" | custom-call | flops 1 | bytes 1 | tf_op jit(solution)/shard_map/v_pass_0/pallas_call | solution.py:329
  23.6 1.9 %collective-permute-start.8 = (s16[784,256]{1,0:T(8,128)(2,1)S(1)}, s16[784,256]{1,0:T(8,128)(2,1)S(1)}, u32[]{:S(2)}, u32[]{:S(2)}) collective-permute-start(s16[784,256]{1,0:T(8,128)(2,1)S(1)} %core_sum.7.refs_0_.code), channel_id=1, source_target_pairs={{0,2},{1,3},{2,0},{3,1},{4,6},{5,7},{6,4},{7,5},{8,10},{9,11},{10,... | collective-permute-start | bytes 1204232 | tf_op jit(solution)/shard_map/ppermute | solution.py:395
  25.5 2.4 %collective-permute-done.9.code_in = s16[784,256]{1,0:T(8,128)(2,1)S(1)} collective-permute-done((s16[784,256]{1,0:T(8,128)(2,1)S(1)}, s16[784,256]{1,0:T(8,128)(2,1)S(1)}, u32[]{:S(2)}, u32[]{:S(2)}) %collective-permute-start.9) | collective-permute-done | bytes 401440 | tf_op jit(solution)/shard_map/ppermute | solution.py:395
  28.2 2.6 %u_pass_30.1 = (f32[768,256]{1,0:T(8,128)S(1)}, f32[384,256]{1,0:T(8,128)S(1)}, f32[384,256]{1,0:T(8,128)S(1)}) custom-call(s32[384]{0:T(512)S(1)} %get-tuple-element.35.slots.refs_0_, bf16[6144,256]{1,0:T(8,128)(2,1)S(1)} %copy-done, bf16[1024,256]{1,0:T(8,128)(2,1)S(1)} %copy-done.1, bf16[154,128,128]{2,1,0:T(8,128)(2,1)S(1)} %bitcast.7, ...), custom_call_target="tpu_custom_call" | custom-call | flops 1 | bytes 1 | tf_op jit(solution)/shard_map/u_pass_30/pallas_call | solution.py:196
  30.9 0.5 collective-permute-start.12
  31.5 1.1 %collective-permute-done.11.refs_0_ = f32[384,256]{1,0:T(8,128)S(1)} collective-permute-done((f32[384,256]{1,0:T(8,128)S(1)}, f32[384,256]{1,0:T(8,128)S(1)}, u32[]{:S(2)}, u32[]{:S(2)}) %collective-permute-start.11) | collective-permute-done | bytes 393248 | tf_op jit(solution)/shard_map/ppermute | solution.py:395
  32.6 0.6 collective-permute-done.12.refs_1_
  33.7 2.6 %v_pass_6.1 = (bf16[6144,256]{1,0:T(8,128)(2,1)}, f32[256,1024]{1,0:T(8,128)S(1)}) custom-call(s32[384]{0:T(512)S(1)} %get-tuple-element.35.slots.refs_0_, bf16[1024,256]{1,0:T(8,128)(2,1)S(1)} %copy-done.1, bf16[154,128,128]{2,1,0:T(8,128)(2,1)S(1)} %bitcast.8, bf16[768,256]{1,0:T(8,128)(2,1)S(1)} %update_6.1.refs_0_.refs_3_, ...), custom_call_target="tpu_custom_call", output_to_operand_aliasing={{0}: (6, {})} | custom-call | flops 1 | bytes 1 | tf_op jit(solution)/shard_map/v_pass_6/pallas_call | solution.py:329
  36.9 2.1 %u_pass_42.1 = (f32[384,256]{1,0:T(8,128)S(1)}, f32[384,256]{1,0:T(8,128)S(1)}) custom-call(s32[384]{0:T(512)S(1)} %get-tuple-element.35.slots.refs_0_, bf16[6144,256]{1,0:T(8,128)(2,1)S(1)} %copy-done, bf16[1024,256]{1,0:T(8,128)(2,1)S(1)} %copy-done.1, bf16[154,128,128]{2,1,0:T(8,128)(2,1)S(1)} %bitcast.9, bf16[768,256]{1,0:T(8,128)(2,1)S(1)} %update_18.1.refs_0_.refs_3_), custom_call_target="tpu_custom_call" | custom-call | flops 1 | bytes 1 | tf_op jit(solution)/shard_map/u_pass_42/pallas_call | solution.py:196
  39.0 0.4 collective-permute-start.14
  39.4 2.6 %v_pass_18.1 = (bf16[6144,256]{1,0:T(8,128)(2,1)}, f32[256,1024]{1,0:T(8,128)S(1)}) custom-call(s32[384]{0:T(512)S(1)} %get-tuple-element.35.slots.refs_0_, bf16[1024,256]{1,0:T(8,128)(2,1)S(1)} %copy-done.1, bf16[154,128,128]{2,1,0:T(8,128)(2,1)S(1)} %bitcast.10, bf16[768,256]{1,0:T(8,128)(2,1)S(1)} %update_18.1.refs_0_.refs_3_, ...), custom_call_target="tpu_custom_call", output_to_operand_aliasing={{0}: (6, {})} | custom-call | flops 1 | bytes 1 | tf_op jit(solution)/shard_map/v_pass_18/pallas_call | solution.py:329
  42.2 2.6 %collective-permute-done.16.code_in = s16[784,256]{1,0:T(8,128)(2,1)S(1)} collective-permute-done((s16[784,256]{1,0:T(8,128)(2,1)S(1)}, s16[784,256]{1,0:T(8,128)(2,1)S(1)}, u32[]{:S(2)}, u32[]{:S(2)}) %collective-permute-start.16) | collective-permute-done | bytes 401440 | tf_op jit(solution)/shard_map/ppermute | solution.py:395
  45.2 0.7 collective-permute-start.15
  46.1 1.6 %collective-permute-start.20 = (bf16[16,256]{1,0:T(8,128)(2,1)S(1)}, bf16[16,256]{1,0:T(8,128)(2,1)S(1)}, u32[]{:S(2)}, u32[]{:S(2)}) collective-permute-start(bf16[16,256]{1,0:T(8,128)(2,1)S(1)} %get-tuple-element.68), channel_id=1, source_target_pairs={{0,3},{1,0},{2,1},{3,2},{4,7},{5,4},{6,5},{7,6},{8,11},{9,8},{10,9... | collective-permute-start | bytes 24584 | tf_op jit(solution)/shard_map/ppermute | solution.py:400
  47.6 2.6 %v_pass_30.1 = (bf16[6144,256]{1,0:T(8,128)(2,1)}, f32[256,1024]{1,0:T(8,128)S(1)}) custom-call(s32[384]{0:T(512)S(1)} %get-tuple-element.35.slots.refs_0_, bf16[1024,256]{1,0:T(8,128)(2,1)S(1)} %copy-done.1, bf16[154,128,128]{2,1,0:T(8,128)(2,1)S(1)} %bitcast.11, bf16[768,256]{1,0:T(8,128)(2,1)S(1)} %update_30.1.refs_3_, ...), custom_call_target="tpu_custom_call", output_to_operand_aliasing={{0}: (6, {})} | custom-call | flops 1 | bytes 1 | tf_op jit(solution)/shard_map/v_pass_30/pallas_call | solution.py:329
  50.3 2.1 %collective-permute-done.19.refs_2_.low = bf16[16,256]{1,0:T(8,128)(2,1)S(1)} collective-permute-done((bf16[16,256]{1,0:T(8,128)(2,1)S(1)}, bf16[16,256]{1,0:T(8,128)(2,1)S(1)}, u32[]{:S(2)}, u32[]{:S(2)}) %collective-permute-start.19) | collective-permute-done | bytes 8224 | tf_op jit(solution)/shard_map/ppermute | solution.py:400
  53.1 1.3 %collective-permute-done.21.refs_4_ = bf16[384,256]{1,0:T(8,128)(2,1)S(1)} collective-permute-done((bf16[384,256]{1,0:T(8,128)(2,1)S(1)}, bf16[384,256]{1,0:T(8,128)(2,1)S(1)}, u32[]{:S(2)}, u32[]{:S(2)}) %collective-permute-start.21) | collective-permute-done | bytes 196640 | tf_op jit(solution)/shard_map/ppermute | solution.py:395
  54.4 2.5 %v_pass_42.1 = (bf16[6144,256]{1,0:T(8,128)(2,1)}, f32[128,256]{1,0:T(8,128)S(1)}, s16[144,256]{1,0:T(8,128)(2,1)S(1)}, s16[144,256]{1,0:T(8,128)(2,1)S(1)}, s16...) custom-call(s32[384]{0:T(512)S(1)} %get-tuple-element.35.slots.refs_, ...), custom_call_target="tpu_custom_call", output_to_operand_aliasing={{0}: (6, {})} | custom-call | flops 1 | bytes 1 | tf_op jit(solution)/shard_map/v_pass_42/pallas_call | solution.py:329
  56.9 4.5 %collective-permute-start.22 = (s16[144,256]{1,0:T(8,128)(2,1)S(1)}, s16[144,256]{1,0:T(8,128)(2,1)S(1)}, u32[]{:S(2)}, u32[]{:S(2)}) collective-permute-start(s16[144,256]{1,0:T(8,128)(2,1)S(1)} %get-tuple-element.61), channel_id=1, source_target_pairs={{0,28},{4,24},{8,20},{12,16},{16,12},{20,8},{24,4},{28,0},{1,29},{... | collective-permute-start | bytes 221192 | tf_op jit(solution)/shard_map/ppermute | solution.py:395
  61.7 0.8 collective-permute-start.24
  62.6 2.0 %collective-permute-start.25 = (s16[144,256]{1,0:T(8,128)(2,1)S(1)}, s16[144,256]{1,0:T(8,128)(2,1)S(1)}, u32[]{:S(2)}, u32[]{:S(2)}) collective-permute-start(s16[144,256]{1,0:T(8,128)(2,1)S(1)} %get-tuple-element.64), channel_id=1, source_target_pairs={{0,16},{4,20},{8,24},{12,28},{16,0},{20,4},{24,8},{28,12},{1,17},{... | collective-permute-start | bytes 221192 | tf_op jit(solution)/shard_map/ppermute | solution.py:395
  64.6 2.1 %collective-permute-start.26 = (s16[144,256]{1,0:T(8,128)(2,1)S(1)}, s16[144,256]{1,0:T(8,128)(2,1)S(1)}, u32[]{:S(2)}, u32[]{:S(2)}) collective-permute-start(s16[144,256]{1,0:T(8,128)(2,1)S(1)} %get-tuple-element.65), channel_id=1, source_target_pairs={{0,12},{4,8},{8,4},{12,0},{16,28},{20,24},{24,20},{28,16},{1,13},{... | collective-permute-start | bytes 221192 | tf_op jit(solution)/shard_map/ppermute | solution.py:395
  66.7 0.9 %collective-permute-start.27 = (s16[144,256]{1,0:T(8,128)(2,1)S(1)}, s16[144,256]{1,0:T(8,128)(2,1)S(1)}, u32[]{:S(2)}, u32[]{:S(2)}) collective-permute-start(s16[144,256]{1,0:T(8,128)(2,1)S(1)} %get-tuple-element.66), channel_id=1, source_target_pairs={{0,8},{4,12},{8,0},{12,4},{16,24},{20,28},{24,16},{28,20},{1,9},{5... | collective-permute-start | bytes 221192 | tf_op jit(solution)/shard_map/ppermute | solution.py:395
  67.6 0.6 collective-permute-done.23.refs_1_
  68.2 2.0 %collective-permute-start.28 = (s16[144,256]{1,0:T(8,128)(2,1)S(1)}, s16[144,256]{1,0:T(8,128)(2,1)S(1)}, u32[]{:S(2)}, u32[]{:S(2)}) collective-permute-start(s16[144,256]{1,0:T(8,128)(2,1)S(1)} %get-tuple-element.67), channel_id=1, source_target_pairs={{0,4},{4,0},{8,12},{12,8},{16,20},{20,16},{24,28},{28,24},{1,5},{5... | collective-permute-start | bytes 221192 | tf_op jit(solution)/shard_map/ppermute | solution.py:395
  70.2 3.1 %collective-permute-done.24.refs_2_ = s16[144,256]{1,0:T(8,128)(2,1)S(1)} collective-permute-done((s16[144,256]{1,0:T(8,128)(2,1)S(1)}, s16[144,256]{1,0:T(8,128)(2,1)S(1)}, u32[]{:S(2)}, u32[]{:S(2)}) %collective-permute-start.24) | collective-permute-done | bytes 73760 | tf_op jit(solution)/shard_map/ppermute | solution.py:395
  73.3 0.6 collective-permute-done.25.refs_3_
  74.3 1.7 %collective-permute-start.30 = (bf16[128,256]{1,0:T(8,128)(2,1)S(1)}, bf16[128,256]{1,0:T(8,128)(2,1)S(1)}, u32[]{:S(2)}, u32[]{:S(2)}) collective-permute-start(bf16[128,256]{1,0:T(8,128)(2,1)S(1)} %last_step.1.refs_0_), channel_id=1, source_target_pairs={{0,8},{4,12},{8,0},{12,4},{16,24},{20,28},{24,16},{28,20},{1,9},{5... | collective-permute-start | bytes 196616 | tf_op jit(solution)/shard_map/ppermute | solution.py:395
  76.0 2.4 %collective-permute-start.32 = (bf16[128,256]{1,0:T(8,128)(2,1)S(1)}, bf16[128,256]{1,0:T(8,128)(2,1)S(1)}, u32[]{:S(2)}, u32[]{:S(2)}) collective-permute-start(bf16[128,256]{1,0:T(8,128)(2,1)S(1)} %last_step.1.refs_0_), channel_id=1, source_target_pairs={{0,16},{4,20},{8,24},{12,28},{16,0},{20,4},{24,8},{28,12},{1,17},{... | collective-permute-start | bytes 196616 | tf_op jit(solution)/shard_map/ppermute | solution.py:395
  78.4 0.6 collective-permute-start.34
  79.0 1.2 %collective-permute-start.29 = (bf16[128,256]{1,0:T(8,128)(2,1)S(1)}, bf16[128,256]{1,0:T(8,128)(2,1)S(1)}, u32[]{:S(2)}, u32[]{:S(2)}) collective-permute-start(bf16[128,256]{1,0:T(8,128)(2,1)S(1)} %last_step.1.refs_0_), channel_id=1, source_target_pairs={{0,4},{4,0},{8,12},{12,8},{16,20},{20,16},{24,28},{28,24},{1,5},{5... | collective-permute-start | bytes 196616 | tf_op jit(solution)/shard_map/ppermute | solution.py:395
  80.3 0.8 collective-permute-start.31
  81.1 0.7 collective-permute-done.32.refs_4_
  81.8 1.0 %collective-permute-start.33 = (bf16[128,256]{1,0:T(8,128)(2,1)S(1)}, bf16[128,256]{1,0:T(8,128)(2,1)S(1)}, u32[]{:S(2)}, u32[]{:S(2)}) collective-permute-start(bf16[128,256]{1,0:T(8,128)(2,1)S(1)} %collective-permute-done.32.refs_4_), channel_id=1, source_target_pairs={{0,4},{4,0},{8,12},{12,8},{16,20},{20,16},{24,28},{28,24},{1,5},{5... | collective-permute-start | bytes 196616 | tf_op jit(solution)/shard_map/ppermute | solution.py:395
  82.8 1.6 %collective-permute-done.34.refs_6_ = bf16[128,256]{1,0:T(8,128)(2,1)S(1)} collective-permute-done((bf16[128,256]{1,0:T(8,128)(2,1)S(1)}, bf16[128,256]{1,0:T(8,128)(2,1)S(1)}, u32[]{:S(2)}, u32[]{:S(2)}) %collective-permute-start.34) | collective-permute-done | bytes 65568 | tf_op jit(solution)/shard_map/ppermute | solution.py:395
  84.5 0.6 collective-permute-start.35
  85.1 1.0 %collective-permute-done.33.refs_5_ = bf16[128,256]{1,0:T(8,128)(2,1)S(1)} collective-permute-done((bf16[128,256]{1,0:T(8,128)(2,1)S(1)}, bf16[128,256]{1,0:T(8,128)(2,1)S(1)}, u32[]{:S(2)}, u32[]{:S(2)}) %collective-permute-start.33) | collective-permute-done | bytes 65568 | tf_op jit(solution)/shard_map/ppermute | solution.py:395
  86.1 2.7 %collective-permute-done.35.refs_7_ = bf16[128,256]{1,0:T(8,128)(2,1)S(1)} collective-permute-done((bf16[128,256]{1,0:T(8,128)(2,1)S(1)}, bf16[128,256]{1,0:T(8,128)(2,1)S(1)}, u32[]{:S(2)}, u32[]{:S(2)}) %collective-permute-start.35) | collective-permute-done | bytes 65568 | tf_op jit(solution)/shard_map/ppermute | solution.py:395
  88.7 0.8 join.1
  (56 shorter events, 6.6 us)
Async XLA Ops:
  1.3 9.3 %slice-start = ((s8[5046272]{0:T(1024)(128)(4,1)}), s8[4194304]{0:T(1024)(128)(4,1)S(1)}, s32[]{:S(2)}) async-start(s8[5046272]{0:T(1024)(128)(4,1)} %bitcast.2), calls=%async_computation | async-start | bytes 8388608
  1.3 9.3 %slice-start.1 = ((s8[5046272]{0:T(1024)(128)(4,1)}), s8[851968]{0:T(1024)(128)(4,1)S(1)}, s32[]{:S(2)}) async-start(s8[5046272]{0:T(1024)(128)(4,1)} %bitcast.2), calls=%async_computation.1 | async-start | bytes 1703936
  1.3 9.3 %copy-start = (bf16[6144,256]{1,0:T(8,128)(2,1)S(1)}, bf16[6144,256]{1,0:T(8,128)(2,1)}, u32[]{:S(2)}) copy-start(bf16[6144,256]{1,0:T(8,128)(2,1)} %u_ref.17) | copy-start | bytes 9437188
  1.3 9.3 %copy-start.1 = (bf16[1024,256]{1,0:T(8,128)(2,1)S(1)}, bf16[1024,256]{1,0:T(8,128)(2,1)}, u32[]{:S(2)}) copy-start(bf16[1024,256]{1,0:T(8,128)(2,1)} %v_ref.9) | copy-start | bytes 1572868
  6.0 1.9 %collective-permute-start = (f32[384,256]{1,0:T(8,128)S(1)}, f32[384,256]{1,0:T(8,128)S(1)}, u32[]{:S(2)}, u32[]{:S(2)}) collective-permute-start(f32[384,256]{1,0:T(8,128)S(1)} %get-tuple-element.37), channel_id=1, source_target_pairs={{0,1},{1,0},{2,3},{3,2},{4,5},{5,4},{6,7},{7,6},{8,9},{9,8},{10,11... | collective-permute-start | bytes 1179656 | tf_op jit(solution)/shard_map/ppermute | solution.py:395
  8.0 8.0 %collective-permute-start.1 = (s16[400,256]{1,0:T(8,128)(2,1)S(1)}, s16[400,256]{1,0:T(8,128)(2,1)S(1)}, u32[]{:S(2)}, u32[]{:S(2)}) collective-permute-start(s16[400,256]{1,0:T(8,128)(2,1)S(1)} %core_sum.5.refs_0_.code), channel_id=1, source_target_pairs={{0,2},{1,3},{2,0},{3,1},{4,6},{5,7},{6,4},{7,5},{8,10},{9,11},{10,... | collective-permute-start | bytes 614408 | tf_op jit(solution)/shard_map/ppermute | solution.py:395
  13.2 1.5 %collective-permute-start.2 = (f32[192,256]{1,0:T(8,128)S(1)}, f32[192,256]{1,0:T(8,128)S(1)}, u32[]{:S(2)}, u32[]{:S(2)}) collective-permute-start(f32[192,256]{1,0:T(8,128)S(1)} %get-tuple-element.39), channel_id=1, source_target_pairs={{0,1},{1,0},{2,3},{3,2},{4,5},{5,4},{6,7},{7,6},{8,9},{9,8},{10,11... | collective-permute-start | bytes 589832 | tf_op jit(solution)/shard_map/ppermute | solution.py:395
  13.2 1.7 %collective-permute-start.3 = (f32[192,256]{1,0:T(8,128)S(1)}, f32[192,256]{1,0:T(8,128)S(1)}, u32[]{:S(2)}, u32[]{:S(2)}) collective-permute-start(f32[192,256]{1,0:T(8,128)S(1)} %get-tuple-element.40), channel_id=1, source_target_pairs={{0,1},{1,0},{2,3},{3,2},{4,5},{5,4},{6,7},{7,6},{8,9},{9,8},{10,11... | collective-permute-start | bytes 589832 | tf_op jit(solution)/shard_map/ppermute | solution.py:395
  13.7 1.5 %collective-permute-start.4 = (f32[192,256]{1,0:T(8,128)S(1)}, f32[192,256]{1,0:T(8,128)S(1)}, u32[]{:S(2)}, u32[]{:S(2)}) collective-permute-start(f32[192,256]{1,0:T(8,128)S(1)} %get-tuple-element.41), channel_id=1, source_target_pairs={{0,1},{1,0},{2,3},{3,2},{4,5},{5,4},{6,7},{7,6},{8,9},{9,8},{10,11... | collective-permute-start | bytes 589832 | tf_op jit(solution)/shard_map/ppermute | solution.py:395
  13.8 1.7 %collective-permute-start.5 = (f32[192,256]{1,0:T(8,128)S(1)}, f32[192,256]{1,0:T(8,128)S(1)}, u32[]{:S(2)}, u32[]{:S(2)}) collective-permute-start(f32[192,256]{1,0:T(8,128)S(1)} %get-tuple-element.42), channel_id=1, source_target_pairs={{0,1},{1,0},{2,3},{3,2},{4,5},{5,4},{6,7},{7,6},{8,9},{9,8},{10,11... | collective-permute-start | bytes 589832 | tf_op jit(solution)/shard_map/ppermute | solution.py:395
  15.7 12.2 %collective-permute-start.9 = (s16[784,256]{1,0:T(8,128)(2,1)S(1)}, s16[784,256]{1,0:T(8,128)(2,1)S(1)}, u32[]{:S(2)}, u32[]{:S(2)}) collective-permute-start(s16[784,256]{1,0:T(8,128)(2,1)S(1)} %core_sum.6.refs_0_.code), channel_id=1, source_target_pairs={{0,2},{1,3},{2,0},{3,1},{4,6},{5,7},{6,4},{7,5},{8,10},{9,11},{10,... | collective-permute-start | bytes 1204232 | tf_op jit(solution)/shard_map/ppermute | solution.py:395
  18.7 4.7 %collective-permute-start.6 = (f32[384,256]{1,0:T(8,128)S(1)}, f32[384,256]{1,0:T(8,128)S(1)}, u32[]{:S(2)}, u32[]{:S(2)}) collective-permute-start(f32[384,256]{1,0:T(8,128)S(1)} %get-tuple-element.44), channel_id=1, source_target_pairs={{0,1},{1,0},{2,3},{3,2},{4,5},{5,4},{6,7},{7,6},{8,9},{9,8},{10,11... | collective-permute-start | bytes 1179656 | tf_op jit(solution)/shard_map/ppermute | solution.py:395
  18.9 4.5 %collective-permute-start.7 = (f32[384,256]{1,0:T(8,128)S(1)}, f32[384,256]{1,0:T(8,128)S(1)}, u32[]{:S(2)}, u32[]{:S(2)}) collective-permute-start(f32[384,256]{1,0:T(8,128)S(1)} %get-tuple-element.45), channel_id=1, source_target_pairs={{0,1},{1,0},{2,3},{3,2},{4,5},{5,4},{6,7},{7,6},{8,9},{9,8},{10,11... | collective-permute-start | bytes 1179656 | tf_op jit(solution)/shard_map/ppermute | solution.py:395
  19.3 2.1 %collective-permute-start.10 = (bf16[384,256]{1,0:T(8,128)(2,1)S(1)}, bf16[384,256]{1,0:T(8,128)(2,1)S(1)}, u32[]{:S(2)}, u32[]{:S(2)}) collective-permute-start(bf16[384,256]{1,0:T(8,128)(2,1)S(1)} %update_0.1.refs_0_.refs_3_), channel_id=1, source_target_pairs={{0,1},{1,0},{2,3},{3,2},{4,5},{5,4},{6,7},{7,6},{8,9},{9,8},{10,11... | collective-permute-start | bytes 589832 | tf_op jit(solution)/shard_map/ppermute | solution.py:395
  23.6 12.8 %collective-permute-start.8 = (s16[784,256]{1,0:T(8,128)(2,1)S(1)}, s16[784,256]{1,0:T(8,128)(2,1)S(1)}, u32[]{:S(2)}, u32[]{:S(2)}) collective-permute-start(s16[784,256]{1,0:T(8,128)(2,1)S(1)} %core_sum.7.refs_0_.code), channel_id=1, source_target_pairs={{0,2},{1,3},{2,0},{3,1},{4,6},{5,7},{6,4},{7,5},{8,10},{9,11},{10,... | collective-permute-start | bytes 1204232 | tf_op jit(solution)/shard_map/ppermute | solution.py:395
  30.8 1.8 %collective-permute-start.11 = (f32[384,256]{1,0:T(8,128)S(1)}, f32[384,256]{1,0:T(8,128)S(1)}, u32[]{:S(2)}, u32[]{:S(2)}) collective-permute-start(f32[384,256]{1,0:T(8,128)S(1)} %get-tuple-element.48), channel_id=1, source_target_pairs={{0,1},{1,0},{2,3},{3,2},{4,5},{5,4},{6,7},{7,6},{8,9},{9,8},{10,11... | collective-permute-start | bytes 1179656 | tf_op jit(solution)/shard_map/ppermute | solution.py:395
  30.9 2.3 %collective-permute-start.12 = (f32[384,256]{1,0:T(8,128)S(1)}, f32[384,256]{1,0:T(8,128)S(1)}, u32[]{:S(2)}, u32[]{:S(2)}) collective-permute-start(f32[384,256]{1,0:T(8,128)S(1)} %get-tuple-element.49), channel_id=1, source_target_pairs={{0,1},{1,0},{2,3},{3,2},{4,5},{5,4},{6,7},{7,6},{8,9},{9,8},{10,11... | collective-permute-start | bytes 1179656 | tf_op jit(solution)/shard_map/ppermute | solution.py:395
  31.4 2.3 %collective-permute-start.13 = (bf16[768,256]{1,0:T(8,128)(2,1)S(1)}, bf16[768,256]{1,0:T(8,128)(2,1)S(1)}, u32[]{:S(2)}, u32[]{:S(2)}) collective-permute-start(bf16[768,256]{1,0:T(8,128)(2,1)S(1)} %update_6.1.refs_0_.refs_3_), channel_id=1, source_target_pairs={{0,1},{1,0},{2,3},{3,2},{4,5},{5,4},{6,7},{7,6},{8,9},{9,8},{10,11... | collective-permute-start | bytes 1179656 | tf_op jit(solution)/shard_map/ppermute | solution.py:395
  33.3 11.4 %collective-permute-start.16 = (s16[784,256]{1,0:T(8,128)(2,1)S(1)}, s16[784,256]{1,0:T(8,128)(2,1)S(1)}, u32[]{:S(2)}, u32[]{:S(2)}) collective-permute-start(s16[784,256]{1,0:T(8,128)(2,1)S(1)} %core_sum.8.refs_0_.code), channel_id=1, source_target_pairs={{0,2},{1,3},{2,0},{3,1},{4,6},{5,7},{6,4},{7,5},{8,10},{9,11},{10,... | collective-permute-start | bytes 1204232 | tf_op jit(solution)/shard_map/ppermute | solution.py:395
  36.7 2.7 %collective-permute-start.17 = (bf16[768,256]{1,0:T(8,128)(2,1)S(1)}, bf16[768,256]{1,0:T(8,128)(2,1)S(1)}, u32[]{:S(2)}, u32[]{:S(2)}) collective-permute-start(bf16[768,256]{1,0:T(8,128)(2,1)S(1)} %update_18.1.refs_0_.refs_3_), channel_id=1, source_target_pairs={{0,1},{1,0},{2,3},{3,2},{4,5},{5,4},{6,7},{7,6},{8,9},{9,8},{10,11... | collective-permute-start | bytes 1179656 | tf_op jit(solution)/shard_map/ppermute | solution.py:395
  39.0 3.1 %collective-permute-start.14 = (f32[384,256]{1,0:T(8,128)S(1)}, f32[384,256]{1,0:T(8,128)S(1)}, u32[]{:S(2)}, u32[]{:S(2)}) collective-permute-start(f32[384,256]{1,0:T(8,128)S(1)} %get-tuple-element.53), channel_id=1, source_target_pairs={{0,1},{1,0},{2,3},{3,2},{4,5},{5,4},{6,7},{7,6},{8,9},{9,8},{10,11... | collective-permute-start | bytes 1179656 | tf_op jit(solution)/shard_map/ppermute | solution.py:395
  45.1 2.6 %collective-permute-start.18 = (bf16[768,256]{1,0:T(8,128)(2,1)S(1)}, bf16[768,256]{1,0:T(8,128)(2,1)S(1)}, u32[]{:S(2)}, u32[]{:S(2)}) collective-permute-start(bf16[768,256]{1,0:T(8,128)(2,1)S(1)} %update_30.1.refs_3_), channel_id=1, source_target_pairs={{0,1},{1,0},{2,3},{3,2},{4,5},{5,4},{6,7},{7,6},{8,9},{9,8},{10,11... | collective-permute-start | bytes 1179656 | tf_op jit(solution)/shard_map/ppermute | solution.py:395
  45.2 7.6 %collective-permute-start.15 = (s16[400,256]{1,0:T(8,128)(2,1)S(1)}, s16[400,256]{1,0:T(8,128)(2,1)S(1)}, u32[]{:S(2)}, u32[]{:S(2)}) collective-permute-start(s16[400,256]{1,0:T(8,128)(2,1)S(1)} %core_sum.9.refs_0_.code), channel_id=1, source_target_pairs={{0,2},{1,3},{2,0},{3,1},{4,6},{5,7},{6,4},{7,5},{8,10},{9,11},{10,... | collective-permute-start | bytes 614408 | tf_op jit(solution)/shard_map/ppermute | solution.py:395
  45.9 6.5 %collective-permute-start.19 = (bf16[16,256]{1,0:T(8,128)(2,1)S(1)}, bf16[16,256]{1,0:T(8,128)(2,1)S(1)}, u32[]{:S(2)}, u32[]{:S(2)}) collective-permute-start(bf16[16,256]{1,0:T(8,128)(2,1)S(1)} %get-tuple-element.69), channel_id=1, source_target_pairs={{0,1},{1,2},{2,3},{3,0},{4,5},{5,6},{6,7},{7,4},{8,9},{9,10},{10,1... | collective-permute-start | bytes 24584 | tf_op jit(solution)/shard_map/ppermute | solution.py:400
  46.1 6.3 %collective-permute-start.20 = (bf16[16,256]{1,0:T(8,128)(2,1)S(1)}, bf16[16,256]{1,0:T(8,128)(2,1)S(1)}, u32[]{:S(2)}, u32[]{:S(2)}) collective-permute-start(bf16[16,256]{1,0:T(8,128)(2,1)S(1)} %get-tuple-element.68), channel_id=1, source_target_pairs={{0,3},{1,0},{2,1},{3,2},{4,7},{5,4},{6,5},{7,6},{8,11},{9,8},{10,9... | collective-permute-start | bytes 24584 | tf_op jit(solution)/shard_map/ppermute | solution.py:400
  52.9 1.5 %collective-permute-start.21 = (bf16[384,256]{1,0:T(8,128)(2,1)S(1)}, bf16[384,256]{1,0:T(8,128)(2,1)S(1)}, u32[]{:S(2)}, u32[]{:S(2)}) collective-permute-start(bf16[384,256]{1,0:T(8,128)(2,1)S(1)} %update_42.1.refs_3_), channel_id=1, source_target_pairs={{0,1},{1,0},{2,3},{3,2},{4,5},{5,4},{6,7},{7,6},{8,9},{9,8},{10,11... | collective-permute-start | bytes 589832 | tf_op jit(solution)/shard_map/ppermute | solution.py:395
  56.9 9.8 %collective-permute-start.22 = (s16[144,256]{1,0:T(8,128)(2,1)S(1)}, s16[144,256]{1,0:T(8,128)(2,1)S(1)}, u32[]{:S(2)}, u32[]{:S(2)}) collective-permute-start(s16[144,256]{1,0:T(8,128)(2,1)S(1)} %get-tuple-element.61), channel_id=1, source_target_pairs={{0,28},{4,24},{8,20},{12,16},{16,12},{20,8},{24,4},{28,0},{1,29},{... | collective-permute-start | bytes 221192 | tf_op jit(solution)/shard_map/ppermute | solution.py:395
  61.4 6.8 %collective-permute-start.23 = (s16[144,256]{1,0:T(8,128)(2,1)S(1)}, s16[144,256]{1,0:T(8,128)(2,1)S(1)}, u32[]{:S(2)}, u32[]{:S(2)}) collective-permute-start(s16[144,256]{1,0:T(8,128)(2,1)S(1)} %get-tuple-element.62), channel_id=1, source_target_pairs={{0,24},{4,28},{8,16},{12,20},{16,8},{20,12},{24,0},{28,4},{1,25},{... | collective-permute-start | bytes 221192 | tf_op jit(solution)/shard_map/ppermute | solution.py:395
  61.7 11.6 %collective-permute-start.24 = (s16[144,256]{1,0:T(8,128)(2,1)S(1)}, s16[144,256]{1,0:T(8,128)(2,1)S(1)}, u32[]{:S(2)}, u32[]{:S(2)}) collective-permute-start(s16[144,256]{1,0:T(8,128)(2,1)S(1)} %get-tuple-element.63), channel_id=1, source_target_pairs={{0,20},{4,16},{8,28},{12,24},{16,4},{20,0},{24,12},{28,8},{1,21},{... | collective-permute-start | bytes 221192 | tf_op jit(solution)/shard_map/ppermute | solution.py:395
  62.6 11.3 %collective-permute-start.25 = (s16[144,256]{1,0:T(8,128)(2,1)S(1)}, s16[144,256]{1,0:T(8,128)(2,1)S(1)}, u32[]{:S(2)}, u32[]{:S(2)}) collective-permute-start(s16[144,256]{1,0:T(8,128)(2,1)S(1)} %get-tuple-element.64), channel_id=1, source_target_pairs={{0,16},{4,20},{8,24},{12,28},{16,0},{20,4},{24,8},{28,12},{1,17},{... | collective-permute-start | bytes 221192 | tf_op jit(solution)/shard_map/ppermute | solution.py:395
  64.6 9.3 %collective-permute-start.26 = (s16[144,256]{1,0:T(8,128)(2,1)S(1)}, s16[144,256]{1,0:T(8,128)(2,1)S(1)}, u32[]{:S(2)}, u32[]{:S(2)}) collective-permute-start(s16[144,256]{1,0:T(8,128)(2,1)S(1)} %get-tuple-element.65), channel_id=1, source_target_pairs={{0,12},{4,8},{8,4},{12,0},{16,28},{20,24},{24,20},{28,16},{1,13},{... | collective-permute-start | bytes 221192 | tf_op jit(solution)/shard_map/ppermute | solution.py:395
  66.7 7.3 %collective-permute-start.27 = (s16[144,256]{1,0:T(8,128)(2,1)S(1)}, s16[144,256]{1,0:T(8,128)(2,1)S(1)}, u32[]{:S(2)}, u32[]{:S(2)}) collective-permute-start(s16[144,256]{1,0:T(8,128)(2,1)S(1)} %get-tuple-element.66), channel_id=1, source_target_pairs={{0,8},{4,12},{8,0},{12,4},{16,24},{20,28},{24,16},{28,20},{1,9},{5... | collective-permute-start | bytes 221192 | tf_op jit(solution)/shard_map/ppermute | solution.py:395
  68.2 5.8 %collective-permute-start.28 = (s16[144,256]{1,0:T(8,128)(2,1)S(1)}, s16[144,256]{1,0:T(8,128)(2,1)S(1)}, u32[]{:S(2)}, u32[]{:S(2)}) collective-permute-start(s16[144,256]{1,0:T(8,128)(2,1)S(1)} %get-tuple-element.67), channel_id=1, source_target_pairs={{0,4},{4,0},{8,12},{12,8},{16,20},{20,16},{24,28},{28,24},{1,5},{5... | collective-permute-start | bytes 221192 | tf_op jit(solution)/shard_map/ppermute | solution.py:395
  74.3 6.0 %collective-permute-start.30 = (bf16[128,256]{1,0:T(8,128)(2,1)S(1)}, bf16[128,256]{1,0:T(8,128)(2,1)S(1)}, u32[]{:S(2)}, u32[]{:S(2)}) collective-permute-start(bf16[128,256]{1,0:T(8,128)(2,1)S(1)} %last_step.1.refs_0_), channel_id=1, source_target_pairs={{0,8},{4,12},{8,0},{12,4},{16,24},{20,28},{24,16},{28,20},{1,9},{5... | collective-permute-start | bytes 196616 | tf_op jit(solution)/shard_map/ppermute | solution.py:395
  76.0 5.8 %collective-permute-start.32 = (bf16[128,256]{1,0:T(8,128)(2,1)S(1)}, bf16[128,256]{1,0:T(8,128)(2,1)S(1)}, u32[]{:S(2)}, u32[]{:S(2)}) collective-permute-start(bf16[128,256]{1,0:T(8,128)(2,1)S(1)} %last_step.1.refs_0_), channel_id=1, source_target_pairs={{0,16},{4,20},{8,24},{12,28},{16,0},{20,4},{24,8},{28,12},{1,17},{... | collective-permute-start | bytes 196616 | tf_op jit(solution)/shard_map/ppermute | solution.py:395
  78.4 6.1 %collective-permute-start.34 = (bf16[128,256]{1,0:T(8,128)(2,1)S(1)}, bf16[128,256]{1,0:T(8,128)(2,1)S(1)}, u32[]{:S(2)}, u32[]{:S(2)}) collective-permute-start(bf16[128,256]{1,0:T(8,128)(2,1)S(1)} %last_step.1.refs_0_), channel_id=1, source_target_pairs={{0,24},{4,28},{8,16},{12,20},{16,8},{20,12},{24,0},{28,4},{1,25},{... | collective-permute-start | bytes 196616 | tf_op jit(solution)/shard_map/ppermute | solution.py:395
  79.0 6.0 %collective-permute-start.29 = (bf16[128,256]{1,0:T(8,128)(2,1)S(1)}, bf16[128,256]{1,0:T(8,128)(2,1)S(1)}, u32[]{:S(2)}, u32[]{:S(2)}) collective-permute-start(bf16[128,256]{1,0:T(8,128)(2,1)S(1)} %last_step.1.refs_0_), channel_id=1, source_target_pairs={{0,4},{4,0},{8,12},{12,8},{16,20},{20,16},{24,28},{28,24},{1,5},{5... | collective-permute-start | bytes 196616 | tf_op jit(solution)/shard_map/ppermute | solution.py:395
  80.3 4.8 %collective-permute-start.31 = (bf16[128,256]{1,0:T(8,128)(2,1)S(1)}, bf16[128,256]{1,0:T(8,128)(2,1)S(1)}, u32[]{:S(2)}, u32[]{:S(2)}) collective-permute-start(bf16[128,256]{1,0:T(8,128)(2,1)S(1)} %collective-permute-done.30.refs_2_), channel_id=1, source_target_pairs={{0,4},{4,0},{8,12},{12,8},{16,20},{20,16},{24,28},{28,24},{1,5},{5... | collective-permute-start | bytes 196616 | tf_op jit(solution)/shard_map/ppermute | solution.py:395
  81.8 4.3 %collective-permute-start.33 = (bf16[128,256]{1,0:T(8,128)(2,1)S(1)}, bf16[128,256]{1,0:T(8,128)(2,1)S(1)}, u32[]{:S(2)}, u32[]{:S(2)}) collective-permute-start(bf16[128,256]{1,0:T(8,128)(2,1)S(1)} %collective-permute-done.32.refs_4_), channel_id=1, source_target_pairs={{0,4},{4,0},{8,12},{12,8},{16,20},{20,16},{24,28},{28,24},{1,5},{5... | collective-permute-start | bytes 196616 | tf_op jit(solution)/shard_map/ppermute | solution.py:395
  84.5 4.3 %collective-permute-start.35 = (bf16[128,256]{1,0:T(8,128)(2,1)S(1)}, bf16[128,256]{1,0:T(8,128)(2,1)S(1)}, u32[]{:S(2)}, u32[]{:S(2)}) collective-permute-start(bf16[128,256]{1,0:T(8,128)(2,1)S(1)} %collective-permute-done.34.refs_6_), channel_id=1, source_target_pairs={{0,4},{4,0},{8,12},{12,8},{16,20},{20,16},{24,28},{28,24},{1,5},{5... | collective-permute-start | bytes 196616 | tf_op jit(solution)/shard_map/ppermute | solution.py:395

commit v4 on v3

--- a/solution.py
+++ b/solution.py
@@ -72,16 +72,20 @@
     return [pl.ds(pl.multiple_of(at * half, 16), half) for at in (core, 1 - core)]
 
 
-def residual(left, v_ref, block, err, slots, first, count, across):
-    wide = min(2, across)
-    for t in range(0, across, wide):
+def residual(left, v_ref, block, err, slots, first, count, across, base=0, ready=None):
+    columns = err.shape[1] // B
+    wide = min(2, columns)
+    for t in range(0, columns, wide):
+        start = t * B if isinstance(base, int) else pl.multiple_of((base + t) * B, B)
         predicted = lax.dot_general(
-            left, v_ref[t * B : (t + wide) * B, :], ROWS_BY_ROWS, preferred_element_type=f32
+            left, v_ref[pl.ds(start, wide * B), :], ROWS_BY_ROWS, preferred_element_type=f32
         )
+        if ready:
+            ready(t, wide)
         for r in range(count):
             rows = slice(r * B, (r + 1) * B)
             for c in range(t, t + wide):
-                slot = slots[(first + r) * across + c]
+                slot = slots[(first + r) * across + base + c]
                 gap = predicted[rows, (c - t) * B : (c - t + 1) * B] - block(slot, r, c).astype(f32)
                 err[rows, c * B : (c + 1) * B] = jnp.where(slot >= 0, gap, 0.0).astype(bf16)
 
@@ -95,8 +99,8 @@
 
 
 def first_u_body(
-    count, down, across, row_hbm, col_hbm, live_hbm, u_hbm, v_hbm, values,
-    keep, send, slots, row_ref, col_ref, live_ref, dense, err, left, v_ref, sems
+    count, down, across, row_hbm, col_hbm, live_ref, u_hbm, v_hbm, values,
+    keep, send, slots, row_ref, col_ref, dense, err, left, v_ref, sems
 ):
     loads = [
         pltpu.make_async_copy(src, dst, sems.at[i])
@@ -104,7 +108,6 @@
             (
                 (row_hbm, row_ref),
                 (col_hbm, col_ref),
-                (live_hbm, live_ref),
                 (u_hbm.at[pl.ds(0, count * B)], left),
                 (v_hbm, v_ref),
             )
@@ -118,40 +121,50 @@
         return c
 
     lax.fori_loop(0, down * across, clear, 0, unroll=8)
-    for load in loads[:3]:
+    for load in loads[:2]:
         load.wait()
     live = live_ref[0, 0]
 
-    def enter(k, c):
-        slots[row_ref[0, 0, k] * across + col_ref[0, 0, k]] = jnp.where(k < live, k, -1)
+    total = row_ref.shape[2]
+    batch = next(n for n in (14, 11, 8, 7, 4, 2, 1) if total % n == 0)
+
+    def enter(i, c):
+        at = [i * batch + j for j in range(batch)]
+        where = [row_ref[0, 0, k] * across + col_ref[0, 0, k] for k in at]
+        for k, place in zip(at, where):
+            slots[place] = jnp.where(k < live, k, -1)
         return c
 
-    lax.fori_loop(0, row_ref.shape[2], enter, 0, unroll=7)
+    lax.fori_loop(0, total // batch, enter, 0)
     sem = sems.at[len(loads)]
 
-    def fetch(i, started):
-        slot = slots[i]
-
-        @pl.when(slot >= 0)
-        def _():
-            row = pl.multiple_of((i // across) * B, B)
-            pltpu.make_async_copy(
-                values.at[slot], dense.at[lax.rem(i, across), pl.ds(row, B)], sem
-            ).start()
-
-        return started + (slot >= 0).astype(i32)
-
-    started = lax.fori_loop(0, count * across, fetch, jnp.int32(0), unroll=across)
-    for load in loads[3:]:
+    def fetch(c):
+        def go(r, started):
+            slot = slots[r * across + c]
+
+            @pl.when(slot >= 0)
+            def _():
+                row = pl.multiple_of(r * B, B)
+                pltpu.make_async_copy(values.at[slot], dense.at[c, pl.ds(row, B)], sem).start()
+
+            return started + (slot >= 0).astype(i32)
+
+        return lax.fori_loop(0, count, go, jnp.int32(0), unroll=True)
+
+    started = sum(fetch(c) for c in range(across))
+    for load in loads[2:]:
         load.wait()
 
     def wait(_, c):
         pltpu.make_async_copy(values.at[0], dense.at[0, pl.ds(0, B)], sem).wait()
         return c
 
-    lax.fori_loop(0, started, wait, 0)
+    def ready(t, wide):
+        if t == 0:
+            lax.fori_loop(0, started, wait, 0)
+
     block = lambda slot, r, c: dense[c, r * B : (r + 1) * B, :]
-    residual(left[...], v_ref, block, err, slots, 0, count, across)
+    residual(left[...], v_ref, block, err, slots, 0, count, across, 0, ready)
     split_product(err, v_ref, (keep, send))
 
 
@@ -166,15 +179,15 @@
     return pl.pallas_call(
         functools.partial(first_u_body, count, down, across),
         out_shape=[part, part, jax.ShapeDtypeStruct((down * across,), i32)],
-        in_specs=[hbm, hbm, ANY, hbm, hbm, hbm],
+        in_specs=[hbm, hbm, SMEM, hbm, hbm, hbm],
         out_specs=[VMEM, VMEM, SMEM],
         scratch_shapes=[
-            *(pltpu.SMEM(x.shape, i32) for x in index),
+            *(pltpu.SMEM(x.shape, i32) for x in index[:2]),
             pltpu.VMEM((across, rows, B), bf16),
             pltpu.VMEM((rows, across * B), bf16),
             pltpu.VMEM((rows, width), bf16),
             pltpu.VMEM(v.shape, bf16),
-            pltpu.SemaphoreType.DMA((6,)),
+            pltpu.SemaphoreType.DMA((5,)),
         ],
         compiler_params=params(),
         cost_estimate=SMALL,
@@ -264,20 +277,22 @@
     )(code, code_in, u, *after)
 
 
-def v_body(first, count, across, opening, shards, *refs):
-    slots, v_ref, values, own, other = refs[:5]
-    refs = refs[5:]
+def gather_left(left, own, others):
+    mine, theirs = two_halves(left.shape[0])
+    left[mine, :] = own[...]
+    size = others[0].shape[0]
+    for i, piece in enumerate(others):
+        left[pl.ds(pl.multiple_of(theirs.start + i * size, 16), size), :] = piece[...]
+
+
+def v_body(first, count, across, opening, pieces, *refs):
+    slots, v_ref, values, own = refs[:4]
+    others, refs = refs[4 : 4 + pieces], refs[4 + pieces :]
     if not opening:
         before = refs[0]
         refs = refs[2:]
-    new_out, refs = refs[0], refs[1:]
-    if shards:
-        own_out, sent, refs = refs[0], refs[1:shards], refs[shards:]
-    else:
-        total, refs = refs[0], refs[1:]
-    err, left, sem = refs[:3]
-    for src, rows in zip((own, other), two_halves(count * B)):
-        left[rows, :] = src[...]
+    new_out, total, err, left, sem = refs
+    gather_left(left, own, others)
     save = pltpu.make_async_copy(left, new_out.at[pl.ds(first * B, count * B)], sem)
     save.start()
     block = lambda slot, r, c: values[jnp.maximum(slot, 0)]
@@ -285,58 +300,124 @@
     part = lax.dot_general(left[...], err[...], COLS_BY_COLS, preferred_element_type=f32)
     if not opening:
         part = part + before[...]
-    if not shards:
-        total[...] = part
-    else:
-        turned = refs[3]
-        turned[...] = part.T
-        rows = turned.shape[0] // shards
-        here = lax.axis_index("svc")
-        own_out[...] = turned[pl.ds(pl.multiple_of(here * rows, 8), rows), :]
-        for d in range(1, shards):
-            there = jnp.bitwise_xor(here, d)
-            store_code(sent[d - 1], turned[pl.ds(pl.multiple_of(there * rows, 8), rows), :])
+    total[...] = part
     save.wait()
 
 
-def v_pass(first, count, across, slots, shape, v, values, halves, before, shards):
+def v_pass(first, count, across, slots, shape, v, values, halves, before):
     width = v.shape[1]
     times = v.shape[0]
     opening = before is None
     ins = [slots, v, values, *halves]
-    in_specs = [SMEM] + [VMEM] * 4
+    in_specs = [SMEM] + [VMEM] * (2 + len(halves))
     aliases = {}
-    out = [jax.ShapeDtypeStruct(shape, bf16)]
-    out_specs = [ANY]
     if not opening:
+        aliases = {len(ins) + 1: 0}
         ins += [before[1], before[0]]
         in_specs += [VMEM, ANY]
-        aliases = {6: 0}
-    scratch = [
-        pltpu.VMEM((count * B, across * B), bf16),
-        pltpu.VMEM((count * B, width), bf16),
-        pltpu.SemaphoreType.DMA,
-    ]
-    if shards:
-        rows = times // shards
-        out.append(jax.ShapeDtypeStruct((rows, width), f32))
-        out += [jax.ShapeDtypeStruct((rows + PAD, width), i16)] * (shards - 1)
-        out_specs += [VMEM] * shards
-        scratch.append(pltpu.VMEM((times, width), f32))
+    return pl.pallas_call(
+        functools.partial(v_body, first, count, across, opening, len(halves) - 1),
+        out_shape=[jax.ShapeDtypeStruct(shape, bf16), jax.ShapeDtypeStruct((width, times), f32)],
+        in_specs=in_specs,
+        out_specs=[ANY, VMEM],
+        input_output_aliases=aliases,
+        scratch_shapes=[
+            pltpu.VMEM((count * B, across * B), bf16),
+            pltpu.VMEM((count * B, width), bf16),
+            pltpu.SemaphoreType.DMA,
+        ],
+        compiler_params=params(),
+        cost_estimate=SMALL,
+        name=f"v_pass_{first}",
+    )(*ins)
+
+
+def v_end_body(first, count, across, peers, far, pieces, kinds, *refs):
+    slots, v_ref, values, own = refs[:4]
+    others, before, refs = refs[4 : 4 + pieces], refs[4 + pieces], refs[5 + pieces :]
+    if far:
+        new_out, outs = refs[1], refs[2 : 2 + len(kinds)]
     else:
-        out.append(jax.ShapeDtypeStruct((width, times), f32))
-        out_specs.append(VMEM)
-    return pl.pallas_call(
-        functools.partial(v_body, first, count, across, opening, shards),
+        outs = refs[1 : 1 + len(kinds)]
+    err, left, turned, sem = refs[-4:]
+    here = lax.axis_index("svc")
+    side = lax.div(here, peers // 2)
+    base = (1 - side if far else side) * (across // 2)
+    gather_left(left, own, others)
+    if far:
+        save = pltpu.make_async_copy(left, new_out.at[pl.ds(first * B, count * B)], sem)
+        save.start()
+    block = lambda slot, r, c: values[jnp.maximum(slot, 0)]
+    residual(left[...], v_ref, block, err, slots, first, count, across, base)
+    part = lax.dot_general(left[...], err[...], COLS_BY_COLS, preferred_element_type=f32)
+    part = part + before[:, pl.ds(pl.multiple_of(base * B, B), across // 2 * B)]
+    turned[...] = part.T
+    rows = turned.shape[0] // (peers // 2)
+    for (d, coded), out in zip(kinds, outs):
+        there = lax.rem(jnp.bitwise_xor(here, d), peers // 2)
+        part = turned[pl.ds(pl.multiple_of(there * rows, 8), rows), :]
+        if coded:
+            store_code(out, part)
+        else:
+            out[...] = part
+    if far:
+        save.wait()
+
+
+def v_end(first, count, across, peers, far, kinds, slots, v, values, halves, before, after):
+    times, width = v.shape
+    rows = times // peers
+    ins = [slots, v, values, *halves, before[1], after if after is not None else before[0]]
+    in_specs = [SMEM] + [VMEM] * (3 + len(halves)) + [ANY]
+    out = [jax.ShapeDtypeStruct((rows + PAD, width), i16) if coded else jax.ShapeDtypeStruct((rows, width), f32) for _, coded in kinds]
+    out_specs = [VMEM] * len(kinds)
+    if far:
+        out = [jax.ShapeDtypeStruct(before[0].shape, bf16)] + out
+        out_specs = [ANY] + out_specs
+    return pl.pallas_call(
+        functools.partial(v_end_body, first, count, across, peers, far, len(halves) - 1, kinds),
         out_shape=out,
         in_specs=in_specs,
         out_specs=out_specs,
-        input_output_aliases=aliases,
-        scratch_shapes=scratch,
-        compiler_params=params(),
-        cost_estimate=SMALL,
-        name=f"v_pass_{first}",
+        input_output_aliases={len(ins) - 1: 0} if far else {},
+        scratch_shapes=[
+            pltpu.VMEM((count * B, times // 2), bf16),
+            pltpu.VMEM((count * B, width), bf16),
+            pltpu.VMEM((times // 2, width), f32),
+            pltpu.SemaphoreType.DMA,
+        ],
+        compiler_params=params(),
+        cost_estimate=SMALL,
+        name="v_end_far" if far else "v_end_near",
     )(*ins)
+
+
+def combine_body(joined, *refs):
+    outs = refs[(len(refs) + joined) // 2 :]
+    owns, codes = refs[: len(outs)], refs[len(outs) : len(outs) + joined]
+    for i, (own, out) in enumerate(zip(owns, outs)):
+        if i < joined:
+            group = min(own.shape[0], B)
+            sums = [
+                own[g * group : (g + 1) * group, :] + decode(codes[i], g, group)
+                for g in range(own.shape[0] // group)
+            ]
+            store_code(out, jnp.concatenate(sums, axis=0))
+        else:
+            store_code(out, own[...])
+
+
+def combine(owns, codes):
+    rows, width = owns[0].shape
+    return pl.pallas_call(
+        functools.partial(combine_body, len(codes)),
+        out_shape=[jax.ShapeDtypeStruct((rows + PAD, width), i16)] * len(owns),
+        in_specs=[VMEM] * (len(owns) + len(codes)),
+        out_specs=[VMEM] * len(owns),
+        compiler_params=params(),
+        cost_estimate=SMALL,
+        name="combine",
+    )(*owns, *codes)
 
 
 def last_body(v_ref, low, high, own, *refs):
@@ -371,22 +452,24 @@
     )(v, low, high, own, *codes)
 
 
-def join_body(*refs):
+def join_body(order, *refs):
     out = refs[-1]
     rows = refs[0].shape[0]
-    for d, part in enumerate(refs[:-1]):
+    for d, part in zip(order, refs[:-1]):
         there = jnp.bitwise_xor(lax.axis_index("svc"), d)
         out[pl.ds(pl.multiple_of(there * rows, 16), rows), :] = part[...]
 
 
 def join(parts):
+    order, parts = zip(*parts.items())
     rows, width = parts[0].shape
     return pl.pallas_call(
-        join_body,
+        functools.partial(join_body, order),
         out_shape=jax.ShapeDtypeStruct((rows * len(parts), width), bf16),
         in_specs=[VMEM] * len(parts),
         out_specs=VMEM,
         compiler_params=params(),
+        cost_estimate=SMALL,
         name="join",
     )(*parts)
 
@@ -400,9 +483,12 @@
     return lax.ppermute(x, axis, [(i, (i + by) % n) for i in range(n)])
 
 
+SHARES = (3, 6, 6, 6, 3)
+
+
 def chunks_of(down):
-    unit = down // 8
-    sizes = [unit, 2 * unit, 2 * unit, 2 * unit]
+    unit = down // sum(SHARES)
+    sizes = [unit * share for share in SHARES[:-1]]
     sizes.append(down - sum(sizes))
     return [(sum(sizes[:i]), size) for i, size in enumerate(sizes)]
 
@@ -431,7 +517,11 @@
 
     def renew(k, after):
         half = update(chunks[k][0], *arrived[k], u, after)
-        halves.append((half, swap(half, "step", 1)))
+        pieces = 1 if k == last else pl.cdiv(chunks[k][1], chunks[k + 1][1])
+        while half.shape[0] % (PAD * pieces):
+            pieces += 1
+        size = half.shape[0] // pieces
+        halves.append((half, *(swap(half[i * size : (i + 1) * size], "step", 1) for i in range(pieces))))
 
     cross(0)
     token = codes[0]
@@ -446,21 +536,27 @@
             cross(k)
         if k >= 2:
             first, count = chunks[k - 2]
-            before = v_pass(first, count, across, slots, u.shape, v, values, halves[k - 2], before, 0)
+            before = v_pass(first, count, across, slots, u.shape, v, values, halves[k - 2], before)
         renew(k - 1, [codes[-1]] + ([before[1]] if before else []) + ([low, high] if k > last else []))
         token = halves[k - 1][0]
     first, count = chunks[last]
-    before = v_pass(first, count, across, slots, u.shape, v, values, halves[last], before, peers)
-    new_services, own, sent = before[0], before[1], before[2:]
-    far_first = sorted(range(1, peers), reverse=True)
-    part = last_step(v, low, high, own, [swap(sent[d - 1], "svc", d) for d in far_first])
-    column = {0: part}
-    for d in far_first:
-        if d % 2 == 0:
-            column[d] = swap(part, "svc", d)
-    for d in (0, *(x for x in far_first if x % 2 == 0)):
+    by_x = [d for d in range(peers * 3 // 4, peers) if d % 2]
+    far = [(d, d + 1 not in by_x) for d in range(peers // 2, peers)]
+    near = [(d, False) for d in range(peers // 2)]
+    new_services, *sent = v_end(first, count, across, peers, True, far, slots, v, values, halves[last], before, None)
+    sent = dict(zip((d for d, _ in far), sent))
+    arrived_x = {d: swap(sent.pop(d), "svc", 1) for d in by_x}
+    rest = v_end(first, count, across, peers, False, near, slots, v, values, halves[last], before, sent[peers // 2])
+    own = rest[0]
+    late = [d - 1 for d in by_x] + list(range(1, peers // 2))
+    coded = combine([sent[d - 1] for d in by_x] + list(rest[1:]), [arrived_x[d] for d in by_x])
+    sent = {d: x for d, x in sent.items() if d not in late} | dict(zip(late, coded))
+    part = last_step(v, low, high, own, [swap(x, "svc", d) for d, x in sent.items()])
+    column = {d: swap(part, "svc", d) for d in range(peers - 2, 0, -2)}
+    column[0] = part
+    for d in [x for x in column if x] + [0]:
         column[d + 1] = swap(column[d], "svc", 1)
-    return new_services, join([column[d] for d in range(peers)])
+    return new_services, join(column)
 
 
 def solution(mesh):

time: 89.8 us -> 87.2 us (0.971)
  waiting for transfers between devices: 26 us -> 21.3 us
  Pallas kernels: 30 us -> 31.2 us
  starting transfers between devices: 32.1 us -> 33 us
    ppermute x34 -> x35, waiting for transfers between devices: 23.9 us -> 21.3 us  [swap(): lax.ppermute(x, axis, [(i, i ^ mask) for i in range(lax.axis_size(axis))])]
    ppermute x2, waiting for transfers between devices: 2.11 us -> 0.01 us  [shift(): return lax.ppermute(x, axis, [(i, (i + by) % n) for i in range(n)])]
    ppermute x34 -> x35, starting transfers between devices: 30.3 us -> 31.3 us  [swap(): lax.ppermute(x, axis, [(i, i ^ mask) for i in range(lax.axis_size(axis))])]
    pallas_call x6 -> x8, Pallas kernels: 13.1 us -> 14.1 us  [the longest x4 9.84 us: v_pass(): pl.pallas_call(functools.partial(v_body, first, count, across, opening, l...]
  transfers between devices with their start and end apart: 36 -> 37, of which waited for: 23 -> 23; matrix products, arithmetic and copies ran while one was open for 0% -> 0% of each run, Pallas kernels for 24% -> 26%
where the time goes in v4:
time: 87.2 us; the launch traced here: 87.1 us
  starting transfers between devices  33 us (38%)
  Pallas kernels  31.2 us (36%)
  waiting for transfers between devices  21.3 us (24%)
  between operations  1.57 us (2%)
    ppermute x35, starting transfers between devices, swap(): lax.ppermute(x, axis, [(i, i ^ mask) for i in range(lax.axis_size(axis))])  31.3 us
    ppermute x35, waiting for transfers between devices, swap(): lax.ppermute(x, axis, [(i, i ^ mask) for i in range(lax.axis_size(axis))])  21.3 us
    pallas_call x4, Pallas kernels, v_pass(): pl.pallas_call(functools.partial(v_body, first, count, across, opening, l...  9.84 us
    pallas_call x4, Pallas kernels, u_pass(): pl.pallas_call(functools.partial(u_body, first, count, across, len(after)...  9.8 us
    pallas_call x1, Pallas kernels, first_u_pass(): pl.pallas_call(functools.partial(first_u_body, count, down, across), out_...  5 us
    pallas_call x2, Pallas kernels, v_end(): pl.pallas_call(functools.partial(v_end_body, first, count, across, peers,...  3.28 us
    ppermute x2, starting transfers between devices, shift(): return lax.ppermute(x, axis, [(i, (i + by) % n) for i in range(n)])  1.75 us
  transfers between devices with their start and end apart: 37, of which 23 were waited for; matrix products, arithmetic and copies ran while one was open for 0% of the time, Pallas kernels for 26%

profile of v4, /device:TPU:0, one launch (start us, length us, event | category | flops | bytes accessed | tf_op | source)
XLA Modules:
  0.0 87.1 jit_solution(7878926926999018693)
XLA Ops:
  1.3 5.0 %u_pass_0.1 = (f32[384,256]{1,0:T(8,128)S(1)}, f32[384,256]{1,0:T(8,128)S(1)}, s32[384]{0:T(512)S(1)}) custom-call(s32[1,1,154]{2,1,0:T(1,128)} %row_hbm.1, s32[1,1,154]{2,1,0:T(1,128)} %col_hbm.1, s32[1,1]{1,0:T(1,128)S(6)} %copy.16.live_ref, bf16[6144,256]{1,0:T(8,128)(2,1)} %u_ref.17, bf16[1024,256]{1,0:T(8,128)(2,1)} %v_ref.9, bf16[154,128,128]{2,1,0:T(8,128)(2,1)} %bitcast.1), custom_call_target="tpu_custom_call" | custom-call | flops 1 | bytes 1 | tf_op jit(solution)/shard_map/u_pass_0/pallas_call | solution.py:179
  6.3 0.5 collective-permute-start
  6.8 1.3 %collective-permute-done.refs_0_ = f32[384,256]{1,0:T(8,128)S(1)} collective-permute-done((f32[384,256]{1,0:T(8,128)S(1)}, f32[384,256]{1,0:T(8,128)S(1)}, u32[]{:S(2)}, u32[]{:S(2)}) %collective-permute-start) | collective-permute-done | bytes 393248 | tf_op jit(solution)/shard_map/ppermute | solution.py:478
  8.3 2.9 %collective-permute-start.1 = (s16[400,256]{1,0:T(8,128)(2,1)S(1)}, s16[400,256]{1,0:T(8,128)(2,1)S(1)}, u32[]{:S(2)}, u32[]{:S(2)}) collective-permute-start(s16[400,256]{1,0:T(8,128)(2,1)S(1)} %core_sum.5.refs_0_.code), channel_id=1, source_target_pairs={{0,2},{1,3},{2,0},{3,1},{4,6},{5,7},{6,4},{7,5},{8,10},{9,11},{10,... | collective-permute-start | bytes 614408 | tf_op jit(solution)/shard_map/ppermute | solution.py:478
  11.2 2.6 %u_pass_6.1 = (f32[768,256]{1,0:T(8,128)S(1)}, f32[192,256]{1,0:T(8,128)S(1)}, f32[192,256]{1,0:T(8,128)S(1)}, f32[192,256]{1,0:T(8,128)S(1)}, f32[192,256]{1,0:T(8,128)S(1)}) custom-call(s32[384]{0:T(512)S(1)} %get-tuple-element.39.slots.refs_0_, bf16[6144,256]{1,0:T(8,128)(2,1)S(1)} %copy-done, bf16[1024,256]{1,0:T(8,128)(2,1)S(1)} %copy-done.1, ...), custom_call_target="tpu_custom_call" | custom-call | flops 1 | bytes 1 | tf_op jit(solution)/shard_map/u_pass_6/pallas_call | solution.py:209
  13.9 0.5 collective-permute-start.3
  16.7 2.6 %u_pass_18.1 = (f32[768,256]{1,0:T(8,128)S(1)}, f32[384,256]{1,0:T(8,128)S(1)}, f32[384,256]{1,0:T(8,128)S(1)}) custom-call(s32[384]{0:T(512)S(1)} %get-tuple-element.39.slots.refs_0_, bf16[6144,256]{1,0:T(8,128)(2,1)S(1)} %copy-done, bf16[1024,256]{1,0:T(8,128)(2,1)S(1)} %copy-done.1, bf16[154,128,128]{2,1,0:T(8,128)(2,1)S(1)} %bitcast.5, ...), custom_call_target="tpu_custom_call" | custom-call | flops 1 | bytes 1 | tf_op jit(solution)/shard_map/u_pass_18/pallas_call | solution.py:209
  20.0 1.1 %collective-permute-done.6.refs_0_ = f32[384,256]{1,0:T(8,128)S(1)} collective-permute-done((f32[384,256]{1,0:T(8,128)S(1)}, f32[384,256]{1,0:T(8,128)S(1)}, u32[]{:S(2)}, u32[]{:S(2)}) %collective-permute-start.6) | collective-permute-done | bytes 393248 | tf_op jit(solution)/shard_map/ppermute | solution.py:478
  21.1 0.6 collective-permute-done.7.refs_1_
  21.8 1.9 %collective-permute-start.8 = (s16[784,256]{1,0:T(8,128)(2,1)S(1)}, s16[784,256]{1,0:T(8,128)(2,1)S(1)}, u32[]{:S(2)}, u32[]{:S(2)}) collective-permute-start(s16[784,256]{1,0:T(8,128)(2,1)S(1)} %core_sum.7.refs_0_.code), channel_id=1, source_target_pairs={{0,2},{1,3},{2,0},{3,1},{4,6},{5,7},{6,4},{7,5},{8,10},{9,11},{10,... | collective-permute-start | bytes 1204232 | tf_op jit(solution)/shard_map/ppermute | solution.py:478
  23.8 2.0 %v_pass_0.1 = (bf16[6144,256]{1,0:T(8,128)(2,1)}, f32[256,1024]{1,0:T(8,128)S(1)}) custom-call(s32[384]{0:T(512)S(1)} %get-tuple-element.39.slots.refs_0_, bf16[1024,256]{1,0:T(8,128)(2,1)S(1)} %copy-done.1, bf16[154,128,128]{2,1,0:T(8,128)(2,1)S(1)} %bitcast.6, bf16[384,256]{1,0:T(8,128)(2,1)S(1)} %update_0.1.refs_0_.refs_3_, ...), custom_call_target="tpu_custom_call" | custom-call | flops 1 | bytes 1 | tf_op jit(solution)/shard_map/v_pass_0/pallas_call | solution.py:318
  25.8 2.7 %collective-permute-done.9.code_in = s16[784,256]{1,0:T(8,128)(2,1)S(1)} collective-permute-done((s16[784,256]{1,0:T(8,128)(2,1)S(1)}, s16[784,256]{1,0:T(8,128)(2,1)S(1)}, u32[]{:S(2)}, u32[]{:S(2)}) %collective-permute-start.9) | collective-permute-done | bytes 401440 | tf_op jit(solution)/shard_map/ppermute | solution.py:478
  28.8 2.6 %u_pass_30.1 = (f32[768,256]{1,0:T(8,128)S(1)}, f32[384,256]{1,0:T(8,128)S(1)}, f32[384,256]{1,0:T(8,128)S(1)}) custom-call(s32[384]{0:T(512)S(1)} %get-tuple-element.39.slots.refs_0_, bf16[6144,256]{1,0:T(8,128)(2,1)S(1)} %copy-done, bf16[1024,256]{1,0:T(8,128)(2,1)S(1)} %copy-done.1, bf16[154,128,128]{2,1,0:T(8,128)(2,1)S(1)} %bitcast.7, ...), custom_call_target="tpu_custom_call" | custom-call | flops 1 | bytes 1 | tf_op jit(solution)/shard_map/u_pass_30/pallas_call | solution.py:209
  31.5 0.5 collective-permute-start.12
  32.1 1.1 %collective-permute-done.11.refs_0_ = f32[384,256]{1,0:T(8,128)S(1)} collective-permute-done((f32[384,256]{1,0:T(8,128)S(1)}, f32[384,256]{1,0:T(8,128)S(1)}, u32[]{:S(2)}, u32[]{:S(2)}) %collective-permute-start.11) | collective-permute-done | bytes 393248 | tf_op jit(solution)/shard_map/ppermute | solution.py:478
  33.2 0.6 collective-permute-done.12.refs_1_
  34.3 2.6 %v_pass_6.1 = (bf16[6144,256]{1,0:T(8,128)(2,1)}, f32[256,1024]{1,0:T(8,128)S(1)}) custom-call(s32[384]{0:T(512)S(1)} %get-tuple-element.39.slots.refs_0_, bf16[1024,256]{1,0:T(8,128)(2,1)S(1)} %copy-done.1, bf16[154,128,128]{2,1,0:T(8,128)(2,1)S(1)} %bitcast.8, bf16[768,256]{1,0:T(8,128)(2,1)S(1)} %update_6.1.refs_0_.refs_3_, ...), custom_call_target="tpu_custom_call", output_to_operand_aliasing={{0}: (6, {})} | custom-call | flops 1 | bytes 1 | tf_op jit(solution)/shard_map/v_pass_6/pallas_call | solution.py:318
  37.3 2.0 %u_pass_42.1 = (f32[384,256]{1,0:T(8,128)S(1)}, f32[384,256]{1,0:T(8,128)S(1)}) custom-call(s32[384]{0:T(512)S(1)} %get-tuple-element.39.slots.refs_0_, bf16[6144,256]{1,0:T(8,128)(2,1)S(1)} %copy-done, bf16[1024,256]{1,0:T(8,128)(2,1)S(1)} %copy-done.1, bf16[154,128,128]{2,1,0:T(8,128)(2,1)S(1)} %bitcast.9, bf16[768,256]{1,0:T(8,128)(2,1)S(1)} %update_18.1.refs_0_.refs_3_), custom_call_target="tpu_custom_call" | custom-call | flops 1 | bytes 1 | tf_op jit(solution)/shard_map/u_pass_42/pallas_call | solution.py:209
  39.9 1.2 %collective-permute-done.14.refs_0_ = f32[384,256]{1,0:T(8,128)S(1)} collective-permute-done((f32[384,256]{1,0:T(8,128)S(1)}, f32[384,256]{1,0:T(8,128)S(1)}, u32[]{:S(2)}, u32[]{:S(2)}) %collective-permute-start.14) | collective-permute-done | bytes 393248 | tf_op jit(solution)/shard_map/ppermute | solution.py:478
  41.3 1.8 %collective-permute-start.15 = (s16[400,256]{1,0:T(8,128)(2,1)S(1)}, s16[400,256]{1,0:T(8,128)(2,1)S(1)}, u32[]{:S(2)}, u32[]{:S(2)}) collective-permute-start(s16[400,256]{1,0:T(8,128)(2,1)S(1)} %core_sum.9.refs_0_.code), channel_id=1, source_target_pairs={{0,2},{1,3},{2,0},{3,1},{4,6},{5,7},{6,4},{7,5},{8,10},{9,11},{10,... | collective-permute-start | bytes 614408 | tf_op jit(solution)/shard_map/ppermute | solution.py:478
  43.0 2.6 %v_pass_18.1 = (bf16[6144,256]{1,0:T(8,128)(2,1)}, f32[256,1024]{1,0:T(8,128)S(1)}) custom-call(s32[384]{0:T(512)S(1)} %get-tuple-element.39.slots.refs_0_, bf16[1024,256]{1,0:T(8,128)(2,1)S(1)} %copy-done.1, bf16[154,128,128]{2,1,0:T(8,128)(2,1)S(1)} %bitcast.10, bf16[768,256]{1,0:T(8,128)(2,1)S(1)} %update_18.1.refs_0_.refs_3_, ...), custom_call_target="tpu_custom_call", output_to_operand_aliasing={{0}: (6, {})} | custom-call | flops 1 | bytes 1 | tf_op jit(solution)/shard_map/v_pass_18/pallas_call | solution.py:318
  45.7 0.5 collective-permute-done.16.code_in
  46.6 0.5 collective-permute-start.19
  47.2 1.7 %collective-permute-start.21 = (bf16[16,256]{1,0:T(8,128)(2,1)S(1)}, bf16[16,256]{1,0:T(8,128)(2,1)S(1)}, u32[]{:S(2)}, u32[]{:S(2)}) collective-permute-start(bf16[16,256]{1,0:T(8,128)(2,1)S(1)} %get-tuple-element.76), channel_id=1, source_target_pairs={{0,3},{1,0},{2,1},{3,2},{4,7},{5,4},{6,5},{7,6},{8,11},{9,8},{10,9... | collective-permute-start | bytes 24584 | tf_op jit(solution)/shard_map/ppermute | solution.py:483
  48.9 2.6 %v_pass_30.1 = (bf16[6144,256]{1,0:T(8,128)(2,1)}, f32[256,1024]{1,0:T(8,128)S(1)}) custom-call(s32[384]{0:T(512)S(1)} %get-tuple-element.39.slots.refs_0_, bf16[1024,256]{1,0:T(8,128)(2,1)S(1)} %copy-done.1, bf16[154,128,128]{2,1,0:T(8,128)(2,1)S(1)} %bitcast.11, bf16[768,256]{1,0:T(8,128)(2,1)S(1)} %update_30.1.refs_3_, ...), custom_call_target="tpu_custom_call", output_to_operand_aliasing={{0}: (7, {})} | custom-call | flops 1 | bytes 1 | tf_op jit(solution)/shard_map/v_pass_30/pallas_call | solution.py:318
  51.8 1.4 %collective-permute-done.22.refs_4_ = bf16[384,256]{1,0:T(8,128)(2,1)S(1)} collective-permute-done((bf16[384,256]{1,0:T(8,128)(2,1)S(1)}, bf16[384,256]{1,0:T(8,128)(2,1)S(1)}, u32[]{:S(2)}, u32[]{:S(2)}) %collective-permute-start.22) | collective-permute-done | bytes 196640 | tf_op jit(solution)/shard_map/ppermute | solution.py:478
  53.2 1.8 %v_end_far.1 = (bf16[6144,256]{1,0:T(8,128)(2,1)}, s16[144,256]{1,0:T(8,128)(2,1)S(1)}, s16[144,256]{1,0:T(8,128)(2,1)S(1)}, f32[128,256]{1,0:T(8,128)S(1)}, s16[144,256]{1,0:T(8,128)(2,1)S(1)}) custom-call(s32[384]{0:T(512)S(1)} %get-tuple-element.39.slots.refs_0_, bf16[1024,256]{1,0:T(8,128)(2,1)S(1)} %copy-done.1, ...), custom_call_target="tpu_custom_call", output_to_operand_aliasing={{0}: (6, {})} | custom-call | flops 1 | bytes 1 | tf_op jit(solution)/shard_map/v_end_far/pallas_call | solution.py:377
  55.0 1.6 %collective-permute-start.25 = (s16[144,256]{1,0:T(8,128)(2,1)S(1)}, s16[144,256]{1,0:T(8,128)(2,1)S(1)}, u32[]{:S(2)}, u32[]{:S(2)}) collective-permute-start(s16[144,256]{1,0:T(8,128)(2,1)S(1)} %get-tuple-element.71), channel_id=1, source_target_pairs={{0,4},{4,0},{8,12},{12,8},{16,20},{20,16},{24,28},{28,24},{1,5},{5... | collective-permute-start | bytes 221192 | tf_op jit(solution)/shard_map/ppermute | solution.py:478
  56.6 2.5 %collective-permute-start.23 = (s16[144,256]{1,0:T(8,128)(2,1)S(1)}, s16[144,256]{1,0:T(8,128)(2,1)S(1)}, u32[]{:S(2)}, u32[]{:S(2)}) collective-permute-start(s16[144,256]{1,0:T(8,128)(2,1)S(1)} %get-tuple-element.64.refs_6_), channel_id=1, source_target_pairs={{0,16},{4,20},{8,24},{12,28},{16,0},{20,4},{24,8},{28,12},{1,17},{... | collective-permute-start | bytes 221192 | tf_op jit(solution)/shard_map/ppermute | solution.py:478
  59.5 1.5 %v_end_near.1 = (f32[128,256]{1,0:T(8,128)S(1)}, f32[128,256]{1,0:T(8,128)S(1)}, f32[128,256]{1,0:T(8,128)S(1)}, f32[128,256]{1,0:T(8,128)S(1)}) custom-call(s32[384]{0:T(512)S(1)} %get-tuple-element.39.slots.refs_0_, bf16[1024,256]{1,0:T(8,128)(2,1)S(1)} %copy-done.1, bf16[154,128,128]{2,1,0:T(8,128)(2,1)S(1)} %bitcast.13, ...), custom_call_target="tpu_custom_call" | custom-call | flops 1 | bytes 1 | tf_op jit(solution)/shard_map/v_end_near/pallas_call | solution.py:377
  61.1 3.7 %collective-permute-start.26 = (s16[144,256]{1,0:T(8,128)(2,1)S(1)}, s16[144,256]{1,0:T(8,128)(2,1)S(1)}, u32[]{:S(2)}, u32[]{:S(2)}) collective-permute-start(s16[144,256]{1,0:T(8,128)(2,1)S(1)} %get-tuple-element.72), channel_id=1, source_target_pairs={{0,24},{4,28},{8,16},{12,20},{16,8},{20,12},{24,0},{28,4},{1,25},{... | collective-permute-start | bytes 221192 | tf_op jit(solution)/shard_map/ppermute | solution.py:478
  64.8 1.5 %collective-permute-start.27 = (s16[144,256]{1,0:T(8,128)(2,1)S(1)}, s16[144,256]{1,0:T(8,128)(2,1)S(1)}, u32[]{:S(2)}, u32[]{:S(2)}) collective-permute-start(s16[144,256]{1,0:T(8,128)(2,1)S(1)} %get-tuple-element.73), channel_id=1, source_target_pairs={{0,4},{4,0},{8,12},{12,8},{16,20},{20,16},{24,28},{28,24},{1,5},{5... | collective-permute-start | bytes 221192 | tf_op jit(solution)/shard_map/ppermute | solution.py:478
  66.3 2.0 %collective-permute-start.29 = (s16[144,256]{1,0:T(8,128)(2,1)S(1)}, s16[144,256]{1,0:T(8,128)(2,1)S(1)}, u32[]{:S(2)}, u32[]{:S(2)}) collective-permute-start(s16[144,256]{1,0:T(8,128)(2,1)S(1)} %get-tuple-element.75), channel_id=1, source_target_pairs={{0,12},{4,8},{8,4},{12,0},{16,28},{20,24},{24,20},{28,16},{1,13},{... | collective-permute-start | bytes 221192 | tf_op jit(solution)/shard_map/ppermute | solution.py:478
  68.3 0.7 collective-permute-done.24.refs_1_
  69.3 1.4 %collective-permute-done.28.refs_4_ = s16[144,256]{1,0:T(8,128)(2,1)S(1)} collective-permute-done((s16[144,256]{1,0:T(8,128)(2,1)S(1)}, s16[144,256]{1,0:T(8,128)(2,1)S(1)}, u32[]{:S(2)}, u32[]{:S(2)}) %collective-permute-start.28) | collective-permute-done | bytes 73760 | tf_op jit(solution)/shard_map/ppermute | solution.py:478
  70.7 1.1 %collective-permute-done.29.refs_5_ = s16[144,256]{1,0:T(8,128)(2,1)S(1)} collective-permute-done((s16[144,256]{1,0:T(8,128)(2,1)S(1)}, s16[144,256]{1,0:T(8,128)(2,1)S(1)}, u32[]{:S(2)}, u32[]{:S(2)}) %collective-permute-start.29) | collective-permute-done | bytes 73760 | tf_op jit(solution)/shard_map/ppermute | solution.py:478
  72.0 2.7 %collective-permute-start.30 = (bf16[128,256]{1,0:T(8,128)(2,1)S(1)}, bf16[128,256]{1,0:T(8,128)(2,1)S(1)}, u32[]{:S(2)}, u32[]{:S(2)}) collective-permute-start(bf16[128,256]{1,0:T(8,128)(2,1)S(1)} %last_step.1.refs_3_), channel_id=1, source_target_pairs={{0,24},{4,28},{8,16},{12,20},{16,8},{20,12},{24,0},{28,4},{1,25},{... | collective-permute-start | bytes 196616 | tf_op jit(solution)/shard_map/ppermute | solution.py:478
  74.7 0.6 collective-permute-start.31
  75.4 1.1 %collective-permute-start.32 = (bf16[128,256]{1,0:T(8,128)(2,1)S(1)}, bf16[128,256]{1,0:T(8,128)(2,1)S(1)}, u32[]{:S(2)}, u32[]{:S(2)}) collective-permute-start(bf16[128,256]{1,0:T(8,128)(2,1)S(1)} %last_step.1.refs_3_), channel_id=1, source_target_pairs={{0,8},{4,12},{8,0},{12,4},{16,24},{20,28},{24,16},{28,20},{1,9},{5... | collective-permute-start | bytes 196616 | tf_op jit(solution)/shard_map/ppermute | solution.py:478
  76.5 1.1 %collective-permute-start.36 = (bf16[128,256]{1,0:T(8,128)(2,1)S(1)}, bf16[128,256]{1,0:T(8,128)(2,1)S(1)}, u32[]{:S(2)}, u32[]{:S(2)}) collective-permute-start(bf16[128,256]{1,0:T(8,128)(2,1)S(1)} %last_step.1.refs_3_), channel_id=1, source_target_pairs={{0,4},{4,0},{8,12},{12,8},{16,20},{20,16},{24,28},{28,24},{1,5},{5... | collective-permute-start | bytes 196616 | tf_op jit(solution)/shard_map/ppermute | solution.py:478
  77.6 0.6 collective-permute-done.30.refs_0_
  78.3 1.1 %collective-permute-start.33 = (bf16[128,256]{1,0:T(8,128)(2,1)S(1)}, bf16[128,256]{1,0:T(8,128)(2,1)S(1)}, u32[]{:S(2)}, u32[]{:S(2)}) collective-permute-start(bf16[128,256]{1,0:T(8,128)(2,1)S(1)} %collective-permute-done.30.refs_0_), channel_id=1, source_target_pairs={{0,4},{4,0},{8,12},{12,8},{16,20},{20,16},{24,28},{28,24},{1,5},{5... | collective-permute-start | bytes 196616 | tf_op jit(solution)/shard_map/ppermute | solution.py:478
  79.4 1.2 %collective-permute-done.31.refs_1_ = bf16[128,256]{1,0:T(8,128)(2,1)S(1)} collective-permute-done((bf16[128,256]{1,0:T(8,128)(2,1)S(1)}, bf16[128,256]{1,0:T(8,128)(2,1)S(1)}, u32[]{:S(2)}, u32[]{:S(2)}) %collective-permute-start.31) | collective-permute-done | bytes 65568 | tf_op jit(solution)/shard_map/ppermute | solution.py:478
  80.6 1.4 %collective-permute-start.34 = (bf16[128,256]{1,0:T(8,128)(2,1)S(1)}, bf16[128,256]{1,0:T(8,128)(2,1)S(1)}, u32[]{:S(2)}, u32[]{:S(2)}) collective-permute-start(bf16[128,256]{1,0:T(8,128)(2,1)S(1)} %collective-permute-done.31.refs_1_), channel_id=1, source_target_pairs={{0,4},{4,0},{8,12},{12,8},{16,20},{20,16},{24,28},{28,24},{1,5},{5... | collective-permute-start | bytes 196616 | tf_op jit(solution)/shard_map/ppermute | solution.py:478
  82.0 0.6 collective-permute-start.35
  82.7 2.6 %collective-permute-done.34.refs_5_ = bf16[128,256]{1,0:T(8,128)(2,1)S(1)} collective-permute-done((bf16[128,256]{1,0:T(8,128)(2,1)S(1)}, bf16[128,256]{1,0:T(8,128)(2,1)S(1)}, u32[]{:S(2)}, u32[]{:S(2)}) %collective-permute-start.34) | collective-permute-done | bytes 65568 | tf_op jit(solution)/shard_map/ppermute | solution.py:478
  85.3 1.0 %collective-permute-done.35.refs_6_ = bf16[128,256]{1,0:T(8,128)(2,1)S(1)} collective-permute-done((bf16[128,256]{1,0:T(8,128)(2,1)S(1)}, bf16[128,256]{1,0:T(8,128)(2,1)S(1)}, u32[]{:S(2)}, u32[]{:S(2)}) %collective-permute-start.35) | collective-permute-done | bytes 65568 | tf_op jit(solution)/shard_map/ppermute | solution.py:478
  86.3 0.8 join.1
  (61 shorter events, 7.2 us)
Async XLA Ops:
  1.3 9.9 %slice-start = ((s8[5046272]{0:T(1024)(128)(4,1)}), s8[4194304]{0:T(1024)(128)(4,1)S(1)}, s32[]{:S(2)}) async-start(s8[5046272]{0:T(1024)(128)(4,1)} %bitcast.2), calls=%async_computation | async-start | bytes 8388608
  1.3 9.9 %slice-start.1 = ((s8[5046272]{0:T(1024)(128)(4,1)}), s8[851968]{0:T(1024)(128)(4,1)S(1)}, s32[]{:S(2)}) async-start(s8[5046272]{0:T(1024)(128)(4,1)} %bitcast.2), calls=%async_computation.1 | async-start | bytes 1703936
  1.3 9.9 %copy-start = (bf16[6144,256]{1,0:T(8,128)(2,1)S(1)}, bf16[6144,256]{1,0:T(8,128)(2,1)}, u32[]{:S(2)}) copy-start(bf16[6144,256]{1,0:T(8,128)(2,1)} %u_ref.17) | copy-start | bytes 9437188
  1.3 9.9 %copy-start.1 = (bf16[1024,256]{1,0:T(8,128)(2,1)S(1)}, bf16[1024,256]{1,0:T(8,128)(2,1)}, u32[]{:S(2)}) copy-start(bf16[1024,256]{1,0:T(8,128)(2,1)} %v_ref.9) | copy-start | bytes 1572868
  6.3 1.9 %collective-permute-start = (f32[384,256]{1,0:T(8,128)S(1)}, f32[384,256]{1,0:T(8,128)S(1)}, u32[]{:S(2)}, u32[]{:S(2)}) collective-permute-start(f32[384,256]{1,0:T(8,128)S(1)} %get-tuple-element.41), channel_id=1, source_target_pairs={{0,1},{1,0},{2,3},{3,2},{4,5},{5,4},{6,7},{7,6},{8,9},{9,8},{10,11... | collective-permute-start | bytes 1179656 | tf_op jit(solution)/shard_map/ppermute | solution.py:478
  8.3 8.2 %collective-permute-start.1 = (s16[400,256]{1,0:T(8,128)(2,1)S(1)}, s16[400,256]{1,0:T(8,128)(2,1)S(1)}, u32[]{:S(2)}, u32[]{:S(2)}) collective-permute-start(s16[400,256]{1,0:T(8,128)(2,1)S(1)} %core_sum.5.refs_0_.code), channel_id=1, source_target_pairs={{0,2},{1,3},{2,0},{3,1},{4,6},{5,7},{6,4},{7,5},{8,10},{9,11},{10,... | collective-permute-start | bytes 614408 | tf_op jit(solution)/shard_map/ppermute | solution.py:478
  13.8 1.5 %collective-permute-start.2 = (f32[192,256]{1,0:T(8,128)S(1)}, f32[192,256]{1,0:T(8,128)S(1)}, u32[]{:S(2)}, u32[]{:S(2)}) collective-permute-start(f32[192,256]{1,0:T(8,128)S(1)} %get-tuple-element.43), channel_id=1, source_target_pairs={{0,1},{1,0},{2,3},{3,2},{4,5},{5,4},{6,7},{7,6},{8,9},{9,8},{10,11... | collective-permute-start | bytes 589832 | tf_op jit(solution)/shard_map/ppermute | solution.py:478
  13.9 1.7 %collective-permute-start.3 = (f32[192,256]{1,0:T(8,128)S(1)}, f32[192,256]{1,0:T(8,128)S(1)}, u32[]{:S(2)}, u32[]{:S(2)}) collective-permute-start(f32[192,256]{1,0:T(8,128)S(1)} %get-tuple-element.44), channel_id=1, source_target_pairs={{0,1},{1,0},{2,3},{3,2},{4,5},{5,4},{6,7},{7,6},{8,9},{9,8},{10,11... | collective-permute-start | bytes 589832 | tf_op jit(solution)/shard_map/ppermute | solution.py:478
  14.3 1.5 %collective-permute-start.4 = (f32[192,256]{1,0:T(8,128)S(1)}, f32[192,256]{1,0:T(8,128)S(1)}, u32[]{:S(2)}, u32[]{:S(2)}) collective-permute-start(f32[192,256]{1,0:T(8,128)S(1)} %get-tuple-element.45), channel_id=1, source_target_pairs={{0,1},{1,0},{2,3},{3,2},{4,5},{5,4},{6,7},{7,6},{8,9},{9,8},{10,11... | collective-permute-start | bytes 589832 | tf_op jit(solution)/shard_map/ppermute | solution.py:478
  14.4 1.7 %collective-permute-start.5 = (f32[192,256]{1,0:T(8,128)S(1)}, f32[192,256]{1,0:T(8,128)S(1)}, u32[]{:S(2)}, u32[]{:S(2)}) collective-permute-start(f32[192,256]{1,0:T(8,128)S(1)} %get-tuple-element.46), channel_id=1, source_target_pairs={{0,1},{1,0},{2,3},{3,2},{4,5},{5,4},{6,7},{7,6},{8,9},{9,8},{10,11... | collective-permute-start | bytes 589832 | tf_op jit(solution)/shard_map/ppermute | solution.py:478
  16.3 12.2 %collective-permute-start.9 = (s16[784,256]{1,0:T(8,128)(2,1)S(1)}, s16[784,256]{1,0:T(8,128)(2,1)S(1)}, u32[]{:S(2)}, u32[]{:S(2)}) collective-permute-start(s16[784,256]{1,0:T(8,128)(2,1)S(1)} %core_sum.6.refs_0_.code), channel_id=1, source_target_pairs={{0,2},{1,3},{2,0},{3,1},{4,6},{5,7},{6,4},{7,5},{8,10},{9,11},{10,... | collective-permute-start | bytes 1204232 | tf_op jit(solution)/shard_map/ppermute | solution.py:478
  19.3 1.8 %collective-permute-start.6 = (f32[384,256]{1,0:T(8,128)S(1)}, f32[384,256]{1,0:T(8,128)S(1)}, u32[]{:S(2)}, u32[]{:S(2)}) collective-permute-start(f32[384,256]{1,0:T(8,128)S(1)} %get-tuple-element.48), channel_id=1, source_target_pairs={{0,1},{1,0},{2,3},{3,2},{4,5},{5,4},{6,7},{7,6},{8,9},{9,8},{10,11... | collective-permute-start | bytes 1179656 | tf_op jit(solution)/shard_map/ppermute | solution.py:478
  19.5 2.2 %collective-permute-start.7 = (f32[384,256]{1,0:T(8,128)S(1)}, f32[384,256]{1,0:T(8,128)S(1)}, u32[]{:S(2)}, u32[]{:S(2)}) collective-permute-start(f32[384,256]{1,0:T(8,128)S(1)} %get-tuple-element.49), channel_id=1, source_target_pairs={{0,1},{1,0},{2,3},{3,2},{4,5},{5,4},{6,7},{7,6},{8,9},{9,8},{10,11... | collective-permute-start | bytes 1179656 | tf_op jit(solution)/shard_map/ppermute | solution.py:478
  19.9 3.9 %collective-permute-start.10 = (bf16[384,256]{1,0:T(8,128)(2,1)S(1)}, bf16[384,256]{1,0:T(8,128)(2,1)S(1)}, u32[]{:S(2)}, u32[]{:S(2)}) collective-permute-start(bf16[384,256]{1,0:T(8,128)(2,1)S(1)} %update_0.1.refs_0_.refs_3_), channel_id=1, source_target_pairs={{0,1},{1,0},{2,3},{3,2},{4,5},{5,4},{6,7},{7,6},{8,9},{9,8},{10,11... | collective-permute-start | bytes 589832 | tf_op jit(solution)/shard_map/ppermute | solution.py:478
  21.8 15.1 %collective-permute-start.8 = (s16[784,256]{1,0:T(8,128)(2,1)S(1)}, s16[784,256]{1,0:T(8,128)(2,1)S(1)}, u32[]{:S(2)}, u32[]{:S(2)}) collective-permute-start(s16[784,256]{1,0:T(8,128)(2,1)S(1)} %core_sum.7.refs_0_.code), channel_id=1, source_target_pairs={{0,2},{1,3},{2,0},{3,1},{4,6},{5,7},{6,4},{7,5},{8,10},{9,11},{10,... | collective-permute-start | bytes 1204232 | tf_op jit(solution)/shard_map/ppermute | solution.py:478
  31.4 1.8 %collective-permute-start.11 = (f32[384,256]{1,0:T(8,128)S(1)}, f32[384,256]{1,0:T(8,128)S(1)}, u32[]{:S(2)}, u32[]{:S(2)}) collective-permute-start(f32[384,256]{1,0:T(8,128)S(1)} %get-tuple-element.52), channel_id=1, source_target_pairs={{0,1},{1,0},{2,3},{3,2},{4,5},{5,4},{6,7},{7,6},{8,9},{9,8},{10,11... | collective-permute-start | bytes 1179656 | tf_op jit(solution)/shard_map/ppermute | solution.py:478
  31.5 2.3 %collective-permute-start.12 = (f32[384,256]{1,0:T(8,128)S(1)}, f32[384,256]{1,0:T(8,128)S(1)}, u32[]{:S(2)}, u32[]{:S(2)}) collective-permute-start(f32[384,256]{1,0:T(8,128)S(1)} %get-tuple-element.53), channel_id=1, source_target_pairs={{0,1},{1,0},{2,3},{3,2},{4,5},{5,4},{6,7},{7,6},{8,9},{9,8},{10,11... | collective-permute-start | bytes 1179656 | tf_op jit(solution)/shard_map/ppermute | solution.py:478
  32.0 2.3 %collective-permute-start.13 = (bf16[768,256]{1,0:T(8,128)(2,1)S(1)}, bf16[768,256]{1,0:T(8,128)(2,1)S(1)}, u32[]{:S(2)}, u32[]{:S(2)}) collective-permute-start(bf16[768,256]{1,0:T(8,128)(2,1)S(1)} %update_6.1.refs_0_.refs_3_), channel_id=1, source_target_pairs={{0,1},{1,0},{2,3},{3,2},{4,5},{5,4},{6,7},{7,6},{8,9},{9,8},{10,11... | collective-permute-start | bytes 1179656 | tf_op jit(solution)/shard_map/ppermute | solution.py:478
  34.0 12.2 %collective-permute-start.16 = (s16[784,256]{1,0:T(8,128)(2,1)S(1)}, s16[784,256]{1,0:T(8,128)(2,1)S(1)}, u32[]{:S(2)}, u32[]{:S(2)}) collective-permute-start(s16[784,256]{1,0:T(8,128)(2,1)S(1)} %core_sum.8.refs_0_.code), channel_id=1, source_target_pairs={{0,2},{1,3},{2,0},{3,1},{4,6},{5,7},{6,4},{7,5},{8,10},{9,11},{10,... | collective-permute-start | bytes 1204232 | tf_op jit(solution)/shard_map/ppermute | solution.py:478
  39.4 1.8 %collective-permute-start.14 = (f32[384,256]{1,0:T(8,128)S(1)}, f32[384,256]{1,0:T(8,128)S(1)}, u32[]{:S(2)}, u32[]{:S(2)}) collective-permute-start(f32[384,256]{1,0:T(8,128)S(1)} %get-tuple-element.57), channel_id=1, source_target_pairs={{0,1},{1,0},{2,3},{3,2},{4,5},{5,4},{6,7},{7,6},{8,9},{9,8},{10,11... | collective-permute-start | bytes 1179656 | tf_op jit(solution)/shard_map/ppermute | solution.py:478
  39.6 3.5 %collective-permute-start.17 = (bf16[768,256]{1,0:T(8,128)(2,1)S(1)}, bf16[768,256]{1,0:T(8,128)(2,1)S(1)}, u32[]{:S(2)}, u32[]{:S(2)}) collective-permute-start(bf16[768,256]{1,0:T(8,128)(2,1)S(1)} %update_18.1.refs_0_.refs_3_), channel_id=1, source_target_pairs={{0,1},{1,0},{2,3},{3,2},{4,5},{5,4},{6,7},{7,6},{8,9},{9,8},{10,11... | collective-permute-start | bytes 1179656 | tf_op jit(solution)/shard_map/ppermute | solution.py:478
  41.3 10.2 %collective-permute-start.15 = (s16[400,256]{1,0:T(8,128)(2,1)S(1)}, s16[400,256]{1,0:T(8,128)(2,1)S(1)}, u32[]{:S(2)}, u32[]{:S(2)}) collective-permute-start(s16[400,256]{1,0:T(8,128)(2,1)S(1)} %core_sum.9.refs_0_.code), channel_id=1, source_target_pairs={{0,2},{1,3},{2,0},{3,1},{4,6},{5,7},{6,4},{7,5},{8,10},{9,11},{10,... | collective-permute-start | bytes 614408 | tf_op jit(solution)/shard_map/ppermute | solution.py:478
  46.5 2.3 %collective-permute-start.18 = (bf16[384,256]{1,0:T(8,128)(2,1)S(1)}, bf16[384,256]{1,0:T(8,128)(2,1)S(1)}, u32[]{:S(2)}, u32[]{:S(2)}) collective-permute-start(bf16[384,256]{1,0:T(8,128)(2,1)S(1)} %get-tuple-element.79), channel_id=1, source_target_pairs={{0,1},{1,0},{2,3},{3,2},{4,5},{5,4},{6,7},{7,6},{8,9},{9,8},{10,11... | collective-permute-start | bytes 589832 | tf_op jit(solution)/shard_map/ppermute | solution.py:478
  46.6 2.3 %collective-permute-start.19 = (bf16[384,256]{1,0:T(8,128)(2,1)S(1)}, bf16[384,256]{1,0:T(8,128)(2,1)S(1)}, u32[]{:S(2)}, u32[]{:S(2)}) collective-permute-start(bf16[384,256]{1,0:T(8,128)(2,1)S(1)} %get-tuple-element.78), channel_id=1, source_target_pairs={{0,1},{1,0},{2,3},{3,2},{4,5},{5,4},{6,7},{7,6},{8,9},{9,8},{10,11... | collective-permute-start | bytes 589832 | tf_op jit(solution)/shard_map/ppermute | solution.py:478
  47.1 4.4 %collective-permute-start.20 = (bf16[16,256]{1,0:T(8,128)(2,1)S(1)}, bf16[16,256]{1,0:T(8,128)(2,1)S(1)}, u32[]{:S(2)}, u32[]{:S(2)}) collective-permute-start(bf16[16,256]{1,0:T(8,128)(2,1)S(1)} %get-tuple-element.77), channel_id=1, source_target_pairs={{0,1},{1,2},{2,3},{3,0},{4,5},{5,6},{6,7},{7,4},{8,9},{9,10},{10,1... | collective-permute-start | bytes 24584 | tf_op jit(solution)/shard_map/ppermute | solution.py:483
  47.2 4.3 %collective-permute-start.21 = (bf16[16,256]{1,0:T(8,128)(2,1)S(1)}, bf16[16,256]{1,0:T(8,128)(2,1)S(1)}, u32[]{:S(2)}, u32[]{:S(2)}) collective-permute-start(bf16[16,256]{1,0:T(8,128)(2,1)S(1)} %get-tuple-element.76), channel_id=1, source_target_pairs={{0,3},{1,0},{2,1},{3,2},{4,7},{5,4},{6,5},{7,6},{8,11},{9,8},{10,9... | collective-permute-start | bytes 24584 | tf_op jit(solution)/shard_map/ppermute | solution.py:483
  51.7 1.5 %collective-permute-start.22 = (bf16[384,256]{1,0:T(8,128)(2,1)S(1)}, bf16[384,256]{1,0:T(8,128)(2,1)S(1)}, u32[]{:S(2)}, u32[]{:S(2)}) collective-permute-start(bf16[384,256]{1,0:T(8,128)(2,1)S(1)} %update_42.1.refs_3_), channel_id=1, source_target_pairs={{0,1},{1,0},{2,3},{3,2},{4,5},{5,4},{6,7},{7,6},{8,9},{9,8},{10,11... | collective-permute-start | bytes 589832 | tf_op jit(solution)/shard_map/ppermute | solution.py:478
  55.0 5.9 %collective-permute-start.25 = (s16[144,256]{1,0:T(8,128)(2,1)S(1)}, s16[144,256]{1,0:T(8,128)(2,1)S(1)}, u32[]{:S(2)}, u32[]{:S(2)}) collective-permute-start(s16[144,256]{1,0:T(8,128)(2,1)S(1)} %get-tuple-element.71), channel_id=1, source_target_pairs={{0,4},{4,0},{8,12},{12,8},{16,20},{20,16},{24,28},{28,24},{1,5},{5... | collective-permute-start | bytes 221192 | tf_op jit(solution)/shard_map/ppermute | solution.py:478
  56.6 9.8 %collective-permute-start.23 = (s16[144,256]{1,0:T(8,128)(2,1)S(1)}, s16[144,256]{1,0:T(8,128)(2,1)S(1)}, u32[]{:S(2)}, u32[]{:S(2)}) collective-permute-start(s16[144,256]{1,0:T(8,128)(2,1)S(1)} %get-tuple-element.64.refs_6_), channel_id=1, source_target_pairs={{0,16},{4,20},{8,24},{12,28},{16,0},{20,4},{24,8},{28,12},{1,17},{... | collective-permute-start | bytes 221192 | tf_op jit(solution)/shard_map/ppermute | solution.py:478
  59.1 9.9 %collective-permute-start.24 = (s16[144,256]{1,0:T(8,128)(2,1)S(1)}, s16[144,256]{1,0:T(8,128)(2,1)S(1)}, u32[]{:S(2)}, u32[]{:S(2)}) collective-permute-start(s16[144,256]{1,0:T(8,128)(2,1)S(1)} %get-tuple-element.66), channel_id=1, source_target_pairs={{0,20},{4,16},{8,28},{12,24},{16,4},{20,0},{24,12},{28,8},{1,21},{... | collective-permute-start | bytes 221192 | tf_op jit(solution)/shard_map/ppermute | solution.py:478
  61.1 7.9 %collective-permute-start.26 = (s16[144,256]{1,0:T(8,128)(2,1)S(1)}, s16[144,256]{1,0:T(8,128)(2,1)S(1)}, u32[]{:S(2)}, u32[]{:S(2)}) collective-permute-start(s16[144,256]{1,0:T(8,128)(2,1)S(1)} %get-tuple-element.72), channel_id=1, source_target_pairs={{0,24},{4,28},{8,16},{12,20},{16,8},{20,12},{24,0},{28,4},{1,25},{... | collective-permute-start | bytes 221192 | tf_op jit(solution)/shard_map/ppermute | solution.py:478
  64.8 4.4 %collective-permute-start.27 = (s16[144,256]{1,0:T(8,128)(2,1)S(1)}, s16[144,256]{1,0:T(8,128)(2,1)S(1)}, u32[]{:S(2)}, u32[]{:S(2)}) collective-permute-start(s16[144,256]{1,0:T(8,128)(2,1)S(1)} %get-tuple-element.73), channel_id=1, source_target_pairs={{0,4},{4,0},{8,12},{12,8},{16,20},{20,16},{24,28},{28,24},{1,5},{5... | collective-permute-start | bytes 221192 | tf_op jit(solution)/shard_map/ppermute | solution.py:478
  66.3 4.4 %collective-permute-start.28 = (s16[144,256]{1,0:T(8,128)(2,1)S(1)}, s16[144,256]{1,0:T(8,128)(2,1)S(1)}, u32[]{:S(2)}, u32[]{:S(2)}) collective-permute-start(s16[144,256]{1,0:T(8,128)(2,1)S(1)} %get-tuple-element.74), channel_id=1, source_target_pairs={{0,8},{4,12},{8,0},{12,4},{16,24},{20,28},{24,16},{28,20},{1,9},{5... | collective-permute-start | bytes 221192 | tf_op jit(solution)/shard_map/ppermute | solution.py:478
  66.3 5.5 %collective-permute-start.29 = (s16[144,256]{1,0:T(8,128)(2,1)S(1)}, s16[144,256]{1,0:T(8,128)(2,1)S(1)}, u32[]{:S(2)}, u32[]{:S(2)}) collective-permute-start(s16[144,256]{1,0:T(8,128)(2,1)S(1)} %get-tuple-element.75), channel_id=1, source_target_pairs={{0,12},{4,8},{8,4},{12,0},{16,28},{20,24},{24,20},{28,16},{1,13},{... | collective-permute-start | bytes 221192 | tf_op jit(solution)/shard_map/ppermute | solution.py:478
  72.0 6.2 %collective-permute-start.30 = (bf16[128,256]{1,0:T(8,128)(2,1)S(1)}, bf16[128,256]{1,0:T(8,128)(2,1)S(1)}, u32[]{:S(2)}, u32[]{:S(2)}) collective-permute-start(bf16[128,256]{1,0:T(8,128)(2,1)S(1)} %last_step.1.refs_3_), channel_id=1, source_target_pairs={{0,24},{4,28},{8,16},{12,20},{16,8},{20,12},{24,0},{28,4},{1,25},{... | collective-permute-start | bytes 196616 | tf_op jit(solution)/shard_map/ppermute | solution.py:478
  74.7 5.9 %collective-permute-start.31 = (bf16[128,256]{1,0:T(8,128)(2,1)S(1)}, bf16[128,256]{1,0:T(8,128)(2,1)S(1)}, u32[]{:S(2)}, u32[]{:S(2)}) collective-permute-start(bf16[128,256]{1,0:T(8,128)(2,1)S(1)} %last_step.1.refs_3_), channel_id=1, source_target_pairs={{0,16},{4,20},{8,24},{12,28},{16,0},{20,4},{24,8},{28,12},{1,17},{... | collective-permute-start | bytes 196616 | tf_op jit(solution)/shard_map/ppermute | solution.py:478
  75.4 6.6 %collective-permute-start.32 = (bf16[128,256]{1,0:T(8,128)(2,1)S(1)}, bf16[128,256]{1,0:T(8,128)(2,1)S(1)}, u32[]{:S(2)}, u32[]{:S(2)}) collective-permute-start(bf16[128,256]{1,0:T(8,128)(2,1)S(1)} %last_step.1.refs_3_), channel_id=1, source_target_pairs={{0,8},{4,12},{8,0},{12,4},{16,24},{20,28},{24,16},{28,20},{1,9},{5... | collective-permute-start | bytes 196616 | tf_op jit(solution)/shard_map/ppermute | solution.py:478
  76.5 6.2 %collective-permute-start.36 = (bf16[128,256]{1,0:T(8,128)(2,1)S(1)}, bf16[128,256]{1,0:T(8,128)(2,1)S(1)}, u32[]{:S(2)}, u32[]{:S(2)}) collective-permute-start(bf16[128,256]{1,0:T(8,128)(2,1)S(1)} %last_step.1.refs_3_), channel_id=1, source_target_pairs={{0,4},{4,0},{8,12},{12,8},{16,20},{20,16},{24,28},{28,24},{1,5},{5... | collective-permute-start | bytes 196616 | tf_op jit(solution)/shard_map/ppermute | solution.py:478
  78.3 4.4 %collective-permute-start.33 = (bf16[128,256]{1,0:T(8,128)(2,1)S(1)}, bf16[128,256]{1,0:T(8,128)(2,1)S(1)}, u32[]{:S(2)}, u32[]{:S(2)}) collective-permute-start(bf16[128,256]{1,0:T(8,128)(2,1)S(1)} %collective-permute-done.30.refs_0_), channel_id=1, source_target_pairs={{0,4},{4,0},{8,12},{12,8},{16,20},{20,16},{24,28},{28,24},{1,5},{5... | collective-permute-start | bytes 196616 | tf_op jit(solution)/shard_map/ppermute | solution.py:478
  80.6 4.7 %collective-permute-start.34 = (bf16[128,256]{1,0:T(8,128)(2,1)S(1)}, bf16[128,256]{1,0:T(8,128)(2,1)S(1)}, u32[]{:S(2)}, u32[]{:S(2)}) collective-permute-start(bf16[128,256]{1,0:T(8,128)(2,1)S(1)} %collective-permute-done.31.refs_1_), channel_id=1, source_target_pairs={{0,4},{4,0},{8,12},{12,8},{16,20},{20,16},{24,28},{28,24},{1,5},{5... | collective-permute-start | bytes 196616 | tf_op jit(solution)/shard_map/ppermute | solution.py:478
  82.0 4.3 %collective-permute-start.35 = (bf16[128,256]{1,0:T(8,128)(2,1)S(1)}, bf16[128,256]{1,0:T(8,128)(2,1)S(1)}, u32[]{:S(2)}, u32[]{:S(2)}) collective-permute-start(bf16[128,256]{1,0:T(8,128)(2,1)S(1)} %collective-permute-done.32.refs_2_), channel_id=1, source_target_pairs={{0,4},{4,0},{8,12},{12,8},{16,20},{20,16},{24,28},{28,24},{1,5},{5... | collective-permute-start | bytes 196616 | tf_op jit(solution)/shard_map/ppermute | solution.py:478

commit v5 on v4

--- a/solution.py
+++ b/solution.py
@@ -90,12 +90,13 @@
                 err[rows, c * B : (c + 1) * B] = jnp.where(slot >= 0, gap, 0.0).astype(bf16)
 
 
-def split_product(err, v_ref, outs):
-    for out, rows in zip((outs[:1], outs[1:]), two_halves(err.shape[0])):
-        whole = jnp.dot(err[rows, :], v_ref[...], preferred_element_type=f32)
-        size = out[0].shape[0]
-        for i, piece in enumerate(out):
-            piece[...] = whole[i * size : (i + 1) * size]
+def split_product(err, v_ref, keep, sends):
+    mine, theirs = two_halves(err.shape[0])
+    whole = jnp.dot(err[theirs, :], v_ref[...], preferred_element_type=f32)
+    size = whole.shape[0] // len(sends)
+    for i, send in enumerate(sends):
+        store_code(send, whole[i * size : (i + 1) * size])
+    keep[...] = jnp.dot(err[mine, :], v_ref[...], preferred_element_type=f32)
 
 
 def first_u_body(
@@ -165,7 +166,7 @@
 
     block = lambda slot, r, c: dense[c, r * B : (r + 1) * B, :]
     residual(left[...], v_ref, block, err, slots, 0, count, across, 0, ready)
-    split_product(err, v_ref, (keep, send))
+    split_product(err, v_ref, keep, [send])
 
 
 def in_hbm(x):
@@ -178,7 +179,7 @@
     part = jax.ShapeDtypeStruct((rows // 2, width), f32)
     return pl.pallas_call(
         functools.partial(first_u_body, count, down, across),
-        out_shape=[part, part, jax.ShapeDtypeStruct((down * across,), i32)],
+        out_shape=[part, jax.ShapeDtypeStruct((rows // 2 + PAD, width), i16), jax.ShapeDtypeStruct((down * across,), i32)],
         in_specs=[hbm, hbm, SMEM, hbm, hbm, hbm],
         out_specs=[VMEM, VMEM, SMEM],
         scratch_shapes=[
@@ -199,13 +200,13 @@
     outs, err = refs[waits:-1], refs[-1]
     block = lambda slot, r, c: values[jnp.maximum(slot, 0)]
     residual(u_ref[first * B : (first + count) * B, :], v_ref, block, err, slots, first, count, across)
-    split_product(err, v_ref, outs)
+    split_product(err, v_ref, outs[0], outs[1:])
 
 
 def u_pass(first, count, across, pieces, slots, u, v, values, after):
     rows, width = count * B, u.shape[1]
     part = jax.ShapeDtypeStruct((rows // 2, width), f32)
-    piece = jax.ShapeDtypeStruct((rows // 2 // pieces, width), f32)
+    piece = jax.ShapeDtypeStruct((rows // 2 // pieces + PAD, width), i16)
     return pl.pallas_call(
         functools.partial(u_body, first, count, across, len(after)),
         out_shape=[part] + [piece] * pieces,
@@ -219,7 +220,14 @@
 
 
 def sum_body(own, *refs):
-    store_code(refs[-1], own[...] + jnp.concatenate([x[...] for x in refs[:-1]], axis=0))
+    sums, at = [], 0
+    for piece in refs[:-1]:
+        rows = piece.shape[0] - PAD
+        group = min(rows, B)
+        for g in range(rows // group):
+            sums.append(own[at : at + group, :] + decode(piece, g, group))
+            at += group
+    store_code(refs[-1], jnp.concatenate(sums, axis=0))
 
 
 def core_sum(own, others):
@@ -483,7 +491,7 @@
     return lax.ppermute(x, axis, [(i, (i + by) % n) for i in range(n)])
 
 
-SHARES = (3, 6, 6, 6, 3)
+SHARES = (4, 6, 8, 6)
 
 
 def chunks_of(down):
@@ -528,8 +536,9 @@
     for k in range(1, last + 2):
         if k <= last:
             first, count = chunks[k]
-            pieces = pl.cdiv(2 * count, chunks[k - 1][1])
-            while count * B // 2 % (8 * pieces):
+            groups = count // 2
+            pieces = min(count // chunks[k - 1][1] + 1, groups)
+            while groups % pieces:
                 pieces += 1
             keep, *send = u_pass(first, count, across, pieces, slots, u, v, values, [token])
             codes.append(core_sum(keep, [swap(x, "step", 1) for x in send]))

time: 87.2 us -> 84.6 us (0.970)
  Pallas kernels: 31.2 us -> 29 us
  starting transfers between devices: 33 us -> 30.9 us
  waiting for transfers between devices: 21.3 us -> 22.9 us
    ppermute x2, waiting for transfers between devices: 0.01 us -> 2.71 us  [shift(): return lax.ppermute(x, axis, [(i, (i + by) % n) for i in range(n)])]
    ppermute x35 -> x29, starting transfers between devices: 31.3 us -> 29.2 us  [swap(): lax.ppermute(x, axis, [(i, i ^ mask) for i in range(lax.axis_size(axis))])]
    pallas_call x4 -> x3, Pallas kernels: 9.84 us -> 8.08 us  [v_pass(): pl.pallas_call(functools.partial(v_body, first, count, across, opening, l...]
    pallas_call x4 -> x3, Pallas kernels: 9.8 us -> 8.38 us  [u_pass(): pl.pallas_call(functools.partial(u_body, first, count, across, len(after)...]
    ppermute x35 -> x29, waiting for transfers between devices: 21.3 us -> 20.2 us  [swap(): lax.ppermute(x, axis, [(i, i ^ mask) for i in range(lax.axis_size(axis))])]
  transfers between devices with their start and end apart: 37 -> 31, of which waited for: 23 -> 18; matrix products, arithmetic and copies ran while one was open for 0% -> 0% of each run, Pallas kernels for 26% -> 24%
where the time goes in v5:
time: 84.6 us; the launch traced here: 84.4 us
  starting transfers between devices  30.9 us (37%)
  Pallas kernels  29 us (34%)
  waiting for transfers between devices  22.9 us (27%)
  between operations  1.52 us (2%)
    ppermute x29, starting transfers between devices, swap(): lax.ppermute(x, axis, [(i, i ^ mask) for i in range(lax.axis_size(axis))])  29.2 us
    ppermute x29, waiting for transfers between devices, swap(): lax.ppermute(x, axis, [(i, i ^ mask) for i in range(lax.axis_size(axis))])  20.2 us
    pallas_call x3, Pallas kernels, u_pass(): pl.pallas_call(functools.partial(u_body, first, count, across, len(after)...  8.38 us
    pallas_call x3, Pallas kernels, v_pass(): pl.pallas_call(functools.partial(v_body, first, count, across, opening, l...  8.08 us
    pallas_call x1, Pallas kernels, first_u_pass(): pl.pallas_call(functools.partial(first_u_body, count, down, across), out_...  4.97 us
    pallas_call x2, Pallas kernels, v_end(): pl.pallas_call(functools.partial(v_end_body, first, count, across, peers,...  4.09 us
    ppermute x2, waiting for transfers between devices, shift(): return lax.ppermute(x, axis, [(i, (i + by) % n) for i in range(n)])  2.71 us
    ppermute x2, starting transfers between devices, shift(): return lax.ppermute(x, axis, [(i, (i + by) % n) for i in range(n)])  1.75 us
  transfers between devices with their start and end apart: 31, of which 18 were waited for; matrix products, arithmetic and copies ran while one was open for 0% of the time, Pallas kernels for 24%

profile of v5, /device:TPU:0, one launch (start us, length us, event | category | flops | bytes accessed | tf_op | source)
XLA Modules:
  0.0 84.4 jit_solution(14579882891408036920)
XLA Ops:
  1.3 5.0 %u_pass_0.1 = (f32[512,256]{1,0:T(8,128)S(1)}, s16[528,256]{1,0:T(8,128)(2,1)S(1)}, s32[384]{0:T(512)S(1)}) custom-call(s32[1,1,154]{2,1,0:T(1,128)} %row_hbm.1, s32[1,1,154]{2,1,0:T(1,128)} %col_hbm.1, s32[1,1]{1,0:T(1,128)S(6)} %copy.14.live_ref, bf16[6144,256]{1,0:T(8,128)(2,1)} %u_ref.13, bf16[1024,256]{1,0:T(8,128)(2,1)} %v_ref.7, ...), custom_call_target="tpu_custom_call" | custom-call | flops 1 | bytes 1 | tf_op jit(solution)/shard_map/u_pass_0/pallas_call | solution.py:180
  6.3 0.5 collective-permute-start
  6.8 1.2 %collective-permute-done.refs_0_ = s16[528,256]{1,0:T(8,128)(2,1)S(1)} collective-permute-done((s16[528,256]{1,0:T(8,128)(2,1)S(1)}, s16[528,256]{1,0:T(8,128)(2,1)S(1)}, u32[]{:S(2)}, u32[]{:S(2)}) %collective-permute-start) | collective-permute-done | bytes 270368 | tf_op jit(solution)/shard_map/ppermute | solution.py:486
  8.1 2.9 %collective-permute-start.4 = (s16[528,256]{1,0:T(8,128)(2,1)S(1)}, s16[528,256]{1,0:T(8,128)(2,1)S(1)}, u32[]{:S(2)}, u32[]{:S(2)}) collective-permute-start(s16[528,256]{1,0:T(8,128)(2,1)S(1)} %core_sum.4.refs_0_.code), channel_id=1, source_target_pairs={{0,2},{1,3},{2,0},{3,1},{4,6},{5,7},{6,4},{7,5},{8,10},{9,11},{10,... | collective-permute-start | bytes 811016 | tf_op jit(solution)/shard_map/ppermute | solution.py:486
  11.1 2.6 %u_pass_8.1 = (f32[768,256]{1,0:T(8,128)S(1)}, s16[400,256]{1,0:T(8,128)(2,1)S(1)}, s16[400,256]{1,0:T(8,128)(2,1)S(1)}) custom-call(s32[384]{0:T(512)S(1)} %get-tuple-element.32.slots.refs_0_, bf16[6144,256]{1,0:T(8,128)(2,1)S(1)} %copy-done, bf16[1024,256]{1,0:T(8,128)(2,1)S(1)} %copy-done.1, bf16[154,128,128]{2,1,0:T(8,128)(2,1)S(1)} %bitcast.4, ...), custom_call_target="tpu_custom_call" | custom-call | flops 1 | bytes 1 | tf_op jit(solution)/shard_map/u_pass_8/pallas_call | solution.py:210
  13.7 0.5 collective-permute-start.2
  14.2 0.9 %collective-permute-done.1.refs_0_ = s16[400,256]{1,0:T(8,128)(2,1)S(1)} collective-permute-done((s16[400,256]{1,0:T(8,128)(2,1)S(1)}, s16[400,256]{1,0:T(8,128)(2,1)S(1)}, u32[]{:S(2)}, u32[]{:S(2)}) %collective-permute-start.1) | collective-permute-done | bytes 204832 | tf_op jit(solution)/shard_map/ppermute | solution.py:486
  15.8 2.0 %collective-permute-done.4.code_in = s16[528,256]{1,0:T(8,128)(2,1)S(1)} collective-permute-done((s16[528,256]{1,0:T(8,128)(2,1)S(1)}, s16[528,256]{1,0:T(8,128)(2,1)S(1)}, u32[]{:S(2)}, u32[]{:S(2)}) %collective-permute-start.4) | collective-permute-done | bytes 270368 | tf_op jit(solution)/shard_map/ppermute | solution.py:486
  18.0 3.2 %u_pass_20.1 = (f32[1024,256]{1,0:T(8,128)S(1)}, s16[528,256]{1,0:T(8,128)(2,1)S(1)}, s16[528,256]{1,0:T(8,128)(2,1)S(1)}) custom-call(s32[384]{0:T(512)S(1)} %get-tuple-element.32.slots.refs_0_, bf16[6144,256]{1,0:T(8,128)(2,1)S(1)} %copy-done, bf16[1024,256]{1,0:T(8,128)(2,1)S(1)} %copy-done.1, bf16[154,128,128]{2,1,0:T(8,128)(2,1)S(1)} %bitcast.5, ...), custom_call_target="tpu_custom_call" | custom-call | flops 1 | bytes 1 | tf_op jit(solution)/shard_map/u_pass_20/pallas_call | solution.py:210
  21.3 0.5 collective-permute-start.6
  21.9 1.0 %collective-permute-done.5.refs_0_ = s16[528,256]{1,0:T(8,128)(2,1)S(1)} collective-permute-done((s16[528,256]{1,0:T(8,128)(2,1)S(1)}, s16[528,256]{1,0:T(8,128)(2,1)S(1)}, u32[]{:S(2)}, u32[]{:S(2)}) %collective-permute-start.5) | collective-permute-done | bytes 270368 | tf_op jit(solution)/shard_map/ppermute | solution.py:486
  23.5 2.4 %collective-permute-start.10 = (s16[1040,256]{1,0:T(8,128)(2,1)S(1)}, s16[1040,256]{1,0:T(8,128)(2,1)S(1)}, u32[]{:S(2)}, u32[]{:S(2)}) collective-permute-start(s16[1040,256]{1,0:T(8,128)(2,1)S(1)} %core_sum.6.refs_0_.code), channel_id=1, source_target_pairs={{0,2},{1,3},{2,0},{3,1},{4,6},{5,7},{6,4},{7,5},{8,10},{9,11},{10,... | collective-permute-start | bytes 1597448 | tf_op jit(solution)/shard_map/ppermute | solution.py:486
  26.0 2.2 %v_pass_0.1 = (bf16[6144,256]{1,0:T(8,128)(2,1)}, f32[256,1024]{1,0:T(8,128)S(1)}) custom-call(s32[384]{0:T(512)S(1)} %get-tuple-element.32.slots.refs_0_, bf16[1024,256]{1,0:T(8,128)(2,1)S(1)} %copy-done.1, bf16[154,128,128]{2,1,0:T(8,128)(2,1)S(1)} %bitcast.6, bf16[512,256]{1,0:T(8,128)(2,1)S(1)} %update_0.1.refs_0_.refs_3_, ...), custom_call_target="tpu_custom_call" | custom-call | flops 1 | bytes 1 | tf_op jit(solution)/shard_map/v_pass_0/pallas_call | solution.py:326
  28.5 2.6 %u_pass_36.1 = (f32[768,256]{1,0:T(8,128)S(1)}, s16[784,256]{1,0:T(8,128)(2,1)S(1)}) custom-call(s32[384]{0:T(512)S(1)} %get-tuple-element.32.slots.refs_0_, bf16[6144,256]{1,0:T(8,128)(2,1)S(1)} %copy-done, bf16[1024,256]{1,0:T(8,128)(2,1)S(1)} %copy-done.1, bf16[154,128,128]{2,1,0:T(8,128)(2,1)S(1)} %bitcast.7, bf16[768,256]{1,0:T(8,128)(2,1)S(1)} %update_8.1.refs_0_.refs_3_), custom_call_target="tpu_custom_call" | custom-call | flops 1 | bytes 1 | tf_op jit(solution)/shard_map/u_pass_36/pallas_call | solution.py:210
  31.2 0.5 collective-permute-start.11
  31.7 1.8 %collective-permute-done.11.refs_4_ = bf16[768,256]{1,0:T(8,128)(2,1)S(1)} collective-permute-done((bf16[768,256]{1,0:T(8,128)(2,1)S(1)}, bf16[768,256]{1,0:T(8,128)(2,1)S(1)}, u32[]{:S(2)}, u32[]{:S(2)}) %collective-permute-start.11) | collective-permute-done | bytes 393248 | tf_op jit(solution)/shard_map/ppermute | solution.py:486
  33.5 2.7 %v_pass_8.1 = (bf16[6144,256]{1,0:T(8,128)(2,1)}, f32[256,1024]{1,0:T(8,128)S(1)}) custom-call(s32[384]{0:T(512)S(1)} %get-tuple-element.32.slots.refs_0_, bf16[1024,256]{1,0:T(8,128)(2,1)S(1)} %copy-done.1, bf16[154,128,128]{2,1,0:T(8,128)(2,1)S(1)} %bitcast.8, bf16[768,256]{1,0:T(8,128)(2,1)S(1)} %update_8.1.refs_0_.refs_3_, ...), custom_call_target="tpu_custom_call", output_to_operand_aliasing={{0}: (6, {})} | custom-call | flops 1 | bytes 1 | tf_op jit(solution)/shard_map/v_pass_8/pallas_call | solution.py:326
  36.6 2.0 %collective-permute-done.10.code_in = s16[1040,256]{1,0:T(8,128)(2,1)S(1)} collective-permute-done((s16[1040,256]{1,0:T(8,128)(2,1)S(1)}, s16[1040,256]{1,0:T(8,128)(2,1)S(1)}, u32[]{:S(2)}, u32[]{:S(2)}) %collective-permute-start.10) | collective-permute-done | bytes 532512 | tf_op jit(solution)/shard_map/ppermute | solution.py:486
  38.6 0.4 update_20.1.refs_3_
  39.2 0.5 collective-permute-start.13
  39.8 1.7 %collective-permute-start.15 = (bf16[16,256]{1,0:T(8,128)(2,1)S(1)}, bf16[16,256]{1,0:T(8,128)(2,1)S(1)}, u32[]{:S(2)}, u32[]{:S(2)}) collective-permute-start(bf16[16,256]{1,0:T(8,128)(2,1)S(1)} %get-tuple-element.62), channel_id=1, source_target_pairs={{0,3},{1,0},{2,1},{3,2},{4,7},{5,4},{6,5},{7,6},{8,11},{9,8},{10,9... | collective-permute-start | bytes 24584 | tf_op jit(solution)/shard_map/ppermute | solution.py:491
  41.4 3.1 %v_pass_20.1 = (bf16[6144,256]{1,0:T(8,128)(2,1)}, f32[256,1024]{1,0:T(8,128)S(1)}) custom-call(s32[384]{0:T(512)S(1)} %get-tuple-element.32.slots.refs_0_, bf16[1024,256]{1,0:T(8,128)(2,1)S(1)} %copy-done.1, bf16[154,128,128]{2,1,0:T(8,128)(2,1)S(1)} %bitcast.9, bf16[1024,256]{1,0:T(8,128)(2,1)S(1)} %update_20.1.refs_3_, ...), custom_call_target="tpu_custom_call", output_to_operand_aliasing={{0}: (7, {})} | custom-call | flops 1 | bytes 1 | tf_op jit(solution)/shard_map/v_pass_20/pallas_call | solution.py:326
  44.6 2.7 %collective-permute-done.14.refs_2_.low = bf16[16,256]{1,0:T(8,128)(2,1)S(1)} collective-permute-done((bf16[16,256]{1,0:T(8,128)(2,1)S(1)}, bf16[16,256]{1,0:T(8,128)(2,1)S(1)}, u32[]{:S(2)}, u32[]{:S(2)}) %collective-permute-start.14) | collective-permute-done | bytes 8224 | tf_op jit(solution)/shard_map/ppermute | solution.py:491
  47.3 0.7 collective-permute-done.9.code_in
  48.5 1.6 %collective-permute-done.16.refs_4_ = bf16[768,256]{1,0:T(8,128)(2,1)S(1)} collective-permute-done((bf16[768,256]{1,0:T(8,128)(2,1)S(1)}, bf16[768,256]{1,0:T(8,128)(2,1)S(1)}, u32[]{:S(2)}, u32[]{:S(2)}) %collective-permute-start.16) | collective-permute-done | bytes 393248 | tf_op jit(solution)/shard_map/ppermute | solution.py:486
  50.1 2.2 %v_end_far.1 = (bf16[6144,256]{1,0:T(8,128)(2,1)}, s16[144,256]{1,0:T(8,128)(2,1)S(1)}, s16[144,256]{1,0:T(8,128)(2,1)S(1)}, f32[128,256]{1,0:T(8,128)S(1)}, s16[144,256]{1,0:T(8,128)(2,1)S(1)}) custom-call(s32[384]{0:T(512)S(1)} %get-tuple-element.32.slots.refs_0_, bf16[1024,256]{1,0:T(8,128)(2,1)S(1)} %copy-done.1, ...), custom_call_target="tpu_custom_call", output_to_operand_aliasing={{0}: (6, {})} | custom-call | flops 1 | bytes 1 | tf_op jit(solution)/shard_map/v_end_far/pallas_call | solution.py:385
  52.3 1.7 %collective-permute-start.19 = (s16[144,256]{1,0:T(8,128)(2,1)S(1)}, s16[144,256]{1,0:T(8,128)(2,1)S(1)}, u32[]{:S(2)}, u32[]{:S(2)}) collective-permute-start(s16[144,256]{1,0:T(8,128)(2,1)S(1)} %get-tuple-element.57), channel_id=1, source_target_pairs={{0,4},{4,0},{8,12},{12,8},{16,20},{20,16},{24,28},{28,24},{1,5},{5... | collective-permute-start | bytes 221192 | tf_op jit(solution)/shard_map/ppermute | solution.py:486
  54.0 2.3 %collective-permute-start.17 = (s16[144,256]{1,0:T(8,128)(2,1)S(1)}, s16[144,256]{1,0:T(8,128)(2,1)S(1)}, u32[]{:S(2)}, u32[]{:S(2)}) collective-permute-start(s16[144,256]{1,0:T(8,128)(2,1)S(1)} %get-tuple-element.50.refs_6_), channel_id=1, source_target_pairs={{0,16},{4,20},{8,24},{12,28},{16,0},{20,4},{24,8},{28,12},{1,17},{... | collective-permute-start | bytes 221192 | tf_op jit(solution)/shard_map/ppermute | solution.py:486
  56.3 0.4 collective-permute-start.18
  56.8 1.9 %v_end_near.1 = (f32[128,256]{1,0:T(8,128)S(1)}, f32[128,256]{1,0:T(8,128)S(1)}, f32[128,256]{1,0:T(8,128)S(1)}, f32[128,256]{1,0:T(8,128)S(1)}) custom-call(s32[384]{0:T(512)S(1)} %get-tuple-element.32.slots.refs_0_, bf16[1024,256]{1,0:T(8,128)(2,1)S(1)} %copy-done.1, bf16[154,128,128]{2,1,0:T(8,128)(2,1)S(1)} %bitcast.11, ...), custom_call_target="tpu_custom_call" | custom-call | flops 1 | bytes 1 | tf_op jit(solution)/shard_map/v_end_near/pallas_call | solution.py:385
  58.8 3.5 %collective-permute-start.20 = (s16[144,256]{1,0:T(8,128)(2,1)S(1)}, s16[144,256]{1,0:T(8,128)(2,1)S(1)}, u32[]{:S(2)}, u32[]{:S(2)}) collective-permute-start(s16[144,256]{1,0:T(8,128)(2,1)S(1)} %get-tuple-element.58), channel_id=1, source_target_pairs={{0,24},{4,28},{8,16},{12,20},{16,8},{20,12},{24,0},{28,4},{1,25},{... | collective-permute-start | bytes 221192 | tf_op jit(solution)/shard_map/ppermute | solution.py:486
  62.4 1.5 %collective-permute-start.21 = (s16[144,256]{1,0:T(8,128)(2,1)S(1)}, s16[144,256]{1,0:T(8,128)(2,1)S(1)}, u32[]{:S(2)}, u32[]{:S(2)}) collective-permute-start(s16[144,256]{1,0:T(8,128)(2,1)S(1)} %get-tuple-element.59), channel_id=1, source_target_pairs={{0,4},{4,0},{8,12},{12,8},{16,20},{20,16},{24,28},{28,24},{1,5},{5... | collective-permute-start | bytes 221192 | tf_op jit(solution)/shard_map/ppermute | solution.py:486
  63.8 2.0 %collective-permute-start.23 = (s16[144,256]{1,0:T(8,128)(2,1)S(1)}, s16[144,256]{1,0:T(8,128)(2,1)S(1)}, u32[]{:S(2)}, u32[]{:S(2)}) collective-permute-start(s16[144,256]{1,0:T(8,128)(2,1)S(1)} %get-tuple-element.61), channel_id=1, source_target_pairs={{0,12},{4,8},{8,4},{12,0},{16,28},{20,24},{24,20},{28,16},{1,13},{... | collective-permute-start | bytes 221192 | tf_op jit(solution)/shard_map/ppermute | solution.py:486
  65.9 0.9 %collective-permute-done.21.refs_3_ = s16[144,256]{1,0:T(8,128)(2,1)S(1)} collective-permute-done((s16[144,256]{1,0:T(8,128)(2,1)S(1)}, s16[144,256]{1,0:T(8,128)(2,1)S(1)}, u32[]{:S(2)}, u32[]{:S(2)}) %collective-permute-start.21) | collective-permute-done | bytes 73760 | tf_op jit(solution)/shard_map/ppermute | solution.py:486
  66.7 1.5 %collective-permute-done.22.refs_4_ = s16[144,256]{1,0:T(8,128)(2,1)S(1)} collective-permute-done((s16[144,256]{1,0:T(8,128)(2,1)S(1)}, s16[144,256]{1,0:T(8,128)(2,1)S(1)}, u32[]{:S(2)}, u32[]{:S(2)}) %collective-permute-start.22) | collective-permute-done | bytes 73760 | tf_op jit(solution)/shard_map/ppermute | solution.py:486
  68.2 0.9 %collective-permute-done.23.refs_5_ = s16[144,256]{1,0:T(8,128)(2,1)S(1)} collective-permute-done((s16[144,256]{1,0:T(8,128)(2,1)S(1)}, s16[144,256]{1,0:T(8,128)(2,1)S(1)}, u32[]{:S(2)}, u32[]{:S(2)}) %collective-permute-start.23) | collective-permute-done | bytes 73760 | tf_op jit(solution)/shard_map/ppermute | solution.py:486
  69.3 2.6 %collective-permute-start.24 = (bf16[128,256]{1,0:T(8,128)(2,1)S(1)}, bf16[128,256]{1,0:T(8,128)(2,1)S(1)}, u32[]{:S(2)}, u32[]{:S(2)}) collective-permute-start(bf16[128,256]{1,0:T(8,128)(2,1)S(1)} %last_step.1.refs_3_), channel_id=1, source_target_pairs={{0,24},{4,28},{8,16},{12,20},{16,8},{20,12},{24,0},{28,4},{1,25},{... | collective-permute-start | bytes 196616 | tf_op jit(solution)/shard_map/ppermute | solution.py:486
  72.0 0.9 %collective-permute-start.25 = (bf16[128,256]{1,0:T(8,128)(2,1)S(1)}, bf16[128,256]{1,0:T(8,128)(2,1)S(1)}, u32[]{:S(2)}, u32[]{:S(2)}) collective-permute-start(bf16[128,256]{1,0:T(8,128)(2,1)S(1)} %last_step.1.refs_3_), channel_id=1, source_target_pairs={{0,16},{4,20},{8,24},{12,28},{16,0},{20,4},{24,8},{28,12},{1,17},{... | collective-permute-start | bytes 196616 | tf_op jit(solution)/shard_map/ppermute | solution.py:486
  72.9 0.9 %collective-permute-start.26 = (bf16[128,256]{1,0:T(8,128)(2,1)S(1)}, bf16[128,256]{1,0:T(8,128)(2,1)S(1)}, u32[]{:S(2)}, u32[]{:S(2)}) collective-permute-start(bf16[128,256]{1,0:T(8,128)(2,1)S(1)} %last_step.1.refs_3_), channel_id=1, source_target_pairs={{0,8},{4,12},{8,0},{12,4},{16,24},{20,28},{24,16},{28,20},{1,9},{5... | collective-permute-start | bytes 196616 | tf_op jit(solution)/shard_map/ppermute | solution.py:486
  73.8 1.3 %collective-permute-start.30 = (bf16[128,256]{1,0:T(8,128)(2,1)S(1)}, bf16[128,256]{1,0:T(8,128)(2,1)S(1)}, u32[]{:S(2)}, u32[]{:S(2)}) collective-permute-start(bf16[128,256]{1,0:T(8,128)(2,1)S(1)} %last_step.1.refs_3_), channel_id=1, source_target_pairs={{0,4},{4,0},{8,12},{12,8},{16,20},{20,16},{24,28},{28,24},{1,5},{5... | collective-permute-start | bytes 196616 | tf_op jit(solution)/shard_map/ppermute | solution.py:486
  75.1 0.4 collective-permute-done.24.refs_0_
  75.6 1.4 %collective-permute-start.27 = (bf16[128,256]{1,0:T(8,128)(2,1)S(1)}, bf16[128,256]{1,0:T(8,128)(2,1)S(1)}, u32[]{:S(2)}, u32[]{:S(2)}) collective-permute-start(bf16[128,256]{1,0:T(8,128)(2,1)S(1)} %collective-permute-done.24.refs_0_), channel_id=1, source_target_pairs={{0,4},{4,0},{8,12},{12,8},{16,20},{20,16},{24,28},{28,24},{1,5},{5... | collective-permute-start | bytes 196616 | tf_op jit(solution)/shard_map/ppermute | solution.py:486
  76.9 1.1 %collective-permute-done.25.refs_1_ = bf16[128,256]{1,0:T(8,128)(2,1)S(1)} collective-permute-done((bf16[128,256]{1,0:T(8,128)(2,1)S(1)}, bf16[128,256]{1,0:T(8,128)(2,1)S(1)}, u32[]{:S(2)}, u32[]{:S(2)}) %collective-permute-start.25) | collective-permute-done | bytes 65568 | tf_op jit(solution)/shard_map/ppermute | solution.py:486
  78.0 1.2 %collective-permute-start.28 = (bf16[128,256]{1,0:T(8,128)(2,1)S(1)}, bf16[128,256]{1,0:T(8,128)(2,1)S(1)}, u32[]{:S(2)}, u32[]{:S(2)}) collective-permute-start(bf16[128,256]{1,0:T(8,128)(2,1)S(1)} %collective-permute-done.25.refs_1_), channel_id=1, source_target_pairs={{0,4},{4,0},{8,12},{12,8},{16,20},{20,16},{24,28},{28,24},{1,5},{5... | collective-permute-start | bytes 196616 | tf_op jit(solution)/shard_map/ppermute | solution.py:486
  79.2 0.9 %collective-permute-start.29 = (bf16[128,256]{1,0:T(8,128)(2,1)S(1)}, bf16[128,256]{1,0:T(8,128)(2,1)S(1)}, u32[]{:S(2)}, u32[]{:S(2)}) collective-permute-start(bf16[128,256]{1,0:T(8,128)(2,1)S(1)} %collective-permute-done.26.refs_2_), channel_id=1, source_target_pairs={{0,4},{4,0},{8,12},{12,8},{16,20},{20,16},{24,28},{28,24},{1,5},{5... | collective-permute-start | bytes 196616 | tf_op jit(solution)/shard_map/ppermute | solution.py:486
  80.1 2.8 %collective-permute-done.28.refs_5_ = bf16[128,256]{1,0:T(8,128)(2,1)S(1)} collective-permute-done((bf16[128,256]{1,0:T(8,128)(2,1)S(1)}, bf16[128,256]{1,0:T(8,128)(2,1)S(1)}, u32[]{:S(2)}, u32[]{:S(2)}) %collective-permute-start.28) | collective-permute-done | bytes 65568 | tf_op jit(solution)/shard_map/ppermute | solution.py:486
  82.9 0.7 collective-permute-done.29.refs_6_
  83.6 0.8 join.1
  (45 shorter events, 3.8 us)
Async XLA Ops:
  1.3 9.8 %slice-start = ((s8[5046272]{0:T(1024)(128)(4,1)}), s8[4194304]{0:T(1024)(128)(4,1)S(1)}, s32[]{:S(2)}) async-start(s8[5046272]{0:T(1024)(128)(4,1)} %bitcast.2), calls=%async_computation | async-start | bytes 8388608
  1.3 9.8 %slice-start.1 = ((s8[5046272]{0:T(1024)(128)(4,1)}), s8[851968]{0:T(1024)(128)(4,1)S(1)}, s32[]{:S(2)}) async-start(s8[5046272]{0:T(1024)(128)(4,1)} %bitcast.2), calls=%async_computation.1 | async-start | bytes 1703936
  1.3 9.7 %copy-start = (bf16[6144,256]{1,0:T(8,128)(2,1)S(1)}, bf16[6144,256]{1,0:T(8,128)(2,1)}, u32[]{:S(2)}) copy-start(bf16[6144,256]{1,0:T(8,128)(2,1)} %u_ref.13) | copy-start | bytes 9437188
  1.3 9.7 %copy-start.1 = (bf16[1024,256]{1,0:T(8,128)(2,1)S(1)}, bf16[1024,256]{1,0:T(8,128)(2,1)}, u32[]{:S(2)}) copy-start(bf16[1024,256]{1,0:T(8,128)(2,1)} %v_ref.7) | copy-start | bytes 1572868
  6.3 1.7 %collective-permute-start = (s16[528,256]{1,0:T(8,128)(2,1)S(1)}, s16[528,256]{1,0:T(8,128)(2,1)S(1)}, u32[]{:S(2)}, u32[]{:S(2)}) collective-permute-start(s16[528,256]{1,0:T(8,128)(2,1)S(1)} %get-tuple-element.34), channel_id=1, source_target_pairs={{0,1},{1,0},{2,3},{3,2},{4,5},{5,4},{6,7},{7,6},{8,9},{9,8},{10,11... | collective-permute-start | bytes 811016 | tf_op jit(solution)/shard_map/ppermute | solution.py:486
  8.1 9.7 %collective-permute-start.4 = (s16[528,256]{1,0:T(8,128)(2,1)S(1)}, s16[528,256]{1,0:T(8,128)(2,1)S(1)}, u32[]{:S(2)}, u32[]{:S(2)}) collective-permute-start(s16[528,256]{1,0:T(8,128)(2,1)S(1)} %core_sum.4.refs_0_.code), channel_id=1, source_target_pairs={{0,2},{1,3},{2,0},{3,1},{4,6},{5,7},{6,4},{7,5},{8,10},{9,11},{10,... | collective-permute-start | bytes 811016 | tf_op jit(solution)/shard_map/ppermute | solution.py:486
  13.7 1.5 %collective-permute-start.1 = (s16[400,256]{1,0:T(8,128)(2,1)S(1)}, s16[400,256]{1,0:T(8,128)(2,1)S(1)}, u32[]{:S(2)}, u32[]{:S(2)}) collective-permute-start(s16[400,256]{1,0:T(8,128)(2,1)S(1)} %get-tuple-element.36), channel_id=1, source_target_pairs={{0,1},{1,0},{2,3},{3,2},{4,5},{5,4},{6,7},{7,6},{8,9},{9,8},{10,11... | collective-permute-start | bytes 614408 | tf_op jit(solution)/shard_map/ppermute | solution.py:486
  13.7 1.7 %collective-permute-start.2 = (s16[400,256]{1,0:T(8,128)(2,1)S(1)}, s16[400,256]{1,0:T(8,128)(2,1)S(1)}, u32[]{:S(2)}, u32[]{:S(2)}) collective-permute-start(s16[400,256]{1,0:T(8,128)(2,1)S(1)} %get-tuple-element.37), channel_id=1, source_target_pairs={{0,1},{1,0},{2,3},{3,2},{4,5},{5,4},{6,7},{7,6},{8,9},{9,8},{10,11... | collective-permute-start | bytes 614408 | tf_op jit(solution)/shard_map/ppermute | solution.py:486
  15.7 12.5 %collective-permute-start.3 = (s16[784,256]{1,0:T(8,128)(2,1)S(1)}, s16[784,256]{1,0:T(8,128)(2,1)S(1)}, u32[]{:S(2)}, u32[]{:S(2)}) collective-permute-start(s16[784,256]{1,0:T(8,128)(2,1)S(1)} %core_sum.5.refs_0_.code), channel_id=1, source_target_pairs={{0,2},{1,3},{2,0},{3,1},{4,6},{5,7},{6,4},{7,5},{8,10},{9,11},{10,... | collective-permute-start | bytes 1204232 | tf_op jit(solution)/shard_map/ppermute | solution.py:486
  21.2 1.6 %collective-permute-start.5 = (s16[528,256]{1,0:T(8,128)(2,1)S(1)}, s16[528,256]{1,0:T(8,128)(2,1)S(1)}, u32[]{:S(2)}, u32[]{:S(2)}) collective-permute-start(s16[528,256]{1,0:T(8,128)(2,1)S(1)} %get-tuple-element.39), channel_id=1, source_target_pairs={{0,1},{1,0},{2,3},{3,2},{4,5},{5,4},{6,7},{7,6},{8,9},{9,8},{10,11... | collective-permute-start | bytes 811016 | tf_op jit(solution)/shard_map/ppermute | solution.py:486
  21.3 1.9 %collective-permute-start.6 = (s16[528,256]{1,0:T(8,128)(2,1)S(1)}, s16[528,256]{1,0:T(8,128)(2,1)S(1)}, u32[]{:S(2)}, u32[]{:S(2)}) collective-permute-start(s16[528,256]{1,0:T(8,128)(2,1)S(1)} %get-tuple-element.40), channel_id=1, source_target_pairs={{0,1},{1,0},{2,3},{3,2},{4,5},{5,4},{6,7},{7,6},{8,9},{9,8},{10,11... | collective-permute-start | bytes 811016 | tf_op jit(solution)/shard_map/ppermute | solution.py:486
  21.8 4.2 %collective-permute-start.7 = (bf16[512,256]{1,0:T(8,128)(2,1)S(1)}, bf16[512,256]{1,0:T(8,128)(2,1)S(1)}, u32[]{:S(2)}, u32[]{:S(2)}) collective-permute-start(bf16[512,256]{1,0:T(8,128)(2,1)S(1)} %update_0.1.refs_0_.refs_3_), channel_id=1, source_target_pairs={{0,1},{1,0},{2,3},{3,2},{4,5},{5,4},{6,7},{7,6},{8,9},{9,8},{10,11... | collective-permute-start | bytes 786440 | tf_op jit(solution)/shard_map/ppermute | solution.py:486
  23.5 15.1 %collective-permute-start.10 = (s16[1040,256]{1,0:T(8,128)(2,1)S(1)}, s16[1040,256]{1,0:T(8,128)(2,1)S(1)}, u32[]{:S(2)}, u32[]{:S(2)}) collective-permute-start(s16[1040,256]{1,0:T(8,128)(2,1)S(1)} %core_sum.6.refs_0_.code), channel_id=1, source_target_pairs={{0,2},{1,3},{2,0},{3,1},{4,6},{5,7},{6,4},{7,5},{8,10},{9,11},{10,... | collective-permute-start | bytes 1597448 | tf_op jit(solution)/shard_map/ppermute | solution.py:486
  31.1 5.1 %collective-permute-start.8 = (s16[784,256]{1,0:T(8,128)(2,1)S(1)}, s16[784,256]{1,0:T(8,128)(2,1)S(1)}, u32[]{:S(2)}, u32[]{:S(2)}) collective-permute-start(s16[784,256]{1,0:T(8,128)(2,1)S(1)} %get-tuple-element.43), channel_id=1, source_target_pairs={{0,1},{1,0},{2,3},{3,2},{4,5},{5,4},{6,7},{7,6},{8,9},{9,8},{10,11... | collective-permute-start | bytes 1204232 | tf_op jit(solution)/shard_map/ppermute | solution.py:486
  31.2 2.3 %collective-permute-start.11 = (bf16[768,256]{1,0:T(8,128)(2,1)S(1)}, bf16[768,256]{1,0:T(8,128)(2,1)S(1)}, u32[]{:S(2)}, u32[]{:S(2)}) collective-permute-start(bf16[768,256]{1,0:T(8,128)(2,1)S(1)} %update_8.1.refs_0_.refs_3_), channel_id=1, source_target_pairs={{0,1},{1,0},{2,3},{3,2},{4,5},{5,4},{6,7},{7,6},{8,9},{9,8},{10,11... | collective-permute-start | bytes 1179656 | tf_op jit(solution)/shard_map/ppermute | solution.py:486
  36.5 11.5 %collective-permute-start.9 = (s16[784,256]{1,0:T(8,128)(2,1)S(1)}, s16[784,256]{1,0:T(8,128)(2,1)S(1)}, u32[]{:S(2)}, u32[]{:S(2)}) collective-permute-start(s16[784,256]{1,0:T(8,128)(2,1)S(1)} %core_sum.7.refs_0_.code), channel_id=1, source_target_pairs={{0,2},{1,3},{2,0},{3,1},{4,6},{5,7},{6,4},{7,5},{8,10},{9,11},{10,... | collective-permute-start | bytes 1204232 | tf_op jit(solution)/shard_map/ppermute | solution.py:486
  39.1 2.3 %collective-permute-start.12 = (bf16[512,256]{1,0:T(8,128)(2,1)S(1)}, bf16[512,256]{1,0:T(8,128)(2,1)S(1)}, u32[]{:S(2)}, u32[]{:S(2)}) collective-permute-start(bf16[512,256]{1,0:T(8,128)(2,1)S(1)} %get-tuple-element.65), channel_id=1, source_target_pairs={{0,1},{1,0},{2,3},{3,2},{4,5},{5,4},{6,7},{7,6},{8,9},{9,8},{10,11... | collective-permute-start | bytes 786440 | tf_op jit(solution)/shard_map/ppermute | solution.py:486
  39.2 2.3 %collective-permute-start.13 = (bf16[512,256]{1,0:T(8,128)(2,1)S(1)}, bf16[512,256]{1,0:T(8,128)(2,1)S(1)}, u32[]{:S(2)}, u32[]{:S(2)}) collective-permute-start(bf16[512,256]{1,0:T(8,128)(2,1)S(1)} %get-tuple-element.64), channel_id=1, source_target_pairs={{0,1},{1,0},{2,3},{3,2},{4,5},{5,4},{6,7},{7,6},{8,9},{9,8},{10,11... | collective-permute-start | bytes 786440 | tf_op jit(solution)/shard_map/ppermute | solution.py:486
  39.7 7.6 %collective-permute-start.14 = (bf16[16,256]{1,0:T(8,128)(2,1)S(1)}, bf16[16,256]{1,0:T(8,128)(2,1)S(1)}, u32[]{:S(2)}, u32[]{:S(2)}) collective-permute-start(bf16[16,256]{1,0:T(8,128)(2,1)S(1)} %get-tuple-element.63), channel_id=1, source_target_pairs={{0,1},{1,2},{2,3},{3,0},{4,5},{5,6},{6,7},{7,4},{8,9},{9,10},{10,1... | collective-permute-start | bytes 24584 | tf_op jit(solution)/shard_map/ppermute | solution.py:491
  39.8 7.5 %collective-permute-start.15 = (bf16[16,256]{1,0:T(8,128)(2,1)S(1)}, bf16[16,256]{1,0:T(8,128)(2,1)S(1)}, u32[]{:S(2)}, u32[]{:S(2)}) collective-permute-start(bf16[16,256]{1,0:T(8,128)(2,1)S(1)} %get-tuple-element.62), channel_id=1, source_target_pairs={{0,3},{1,0},{2,1},{3,2},{4,7},{5,4},{6,5},{7,6},{8,11},{9,8},{10,9... | collective-permute-start | bytes 24584 | tf_op jit(solution)/shard_map/ppermute | solution.py:491
  48.3 1.8 %collective-permute-start.16 = (bf16[768,256]{1,0:T(8,128)(2,1)S(1)}, bf16[768,256]{1,0:T(8,128)(2,1)S(1)}, u32[]{:S(2)}, u32[]{:S(2)}) collective-permute-start(bf16[768,256]{1,0:T(8,128)(2,1)S(1)} %update_36.1.refs_3_), channel_id=1, source_target_pairs={{0,1},{1,0},{2,3},{3,2},{4,5},{5,4},{6,7},{7,6},{8,9},{9,8},{10,11... | collective-permute-start | bytes 1179656 | tf_op jit(solution)/shard_map/ppermute | solution.py:486
  52.3 6.4 %collective-permute-start.19 = (s16[144,256]{1,0:T(8,128)(2,1)S(1)}, s16[144,256]{1,0:T(8,128)(2,1)S(1)}, u32[]{:S(2)}, u32[]{:S(2)}) collective-permute-start(s16[144,256]{1,0:T(8,128)(2,1)S(1)} %get-tuple-element.57), channel_id=1, source_target_pairs={{0,4},{4,0},{8,12},{12,8},{16,20},{20,16},{24,28},{28,24},{1,5},{5... | collective-permute-start | bytes 221192 | tf_op jit(solution)/shard_map/ppermute | solution.py:486
  54.0 9.9 %collective-permute-start.17 = (s16[144,256]{1,0:T(8,128)(2,1)S(1)}, s16[144,256]{1,0:T(8,128)(2,1)S(1)}, u32[]{:S(2)}, u32[]{:S(2)}) collective-permute-start(s16[144,256]{1,0:T(8,128)(2,1)S(1)} %get-tuple-element.50.refs_6_), channel_id=1, source_target_pairs={{0,16},{4,20},{8,24},{12,28},{16,0},{20,4},{24,8},{28,12},{1,17},{... | collective-permute-start | bytes 221192 | tf_op jit(solution)/shard_map/ppermute | solution.py:486
  56.3 9.5 %collective-permute-start.18 = (s16[144,256]{1,0:T(8,128)(2,1)S(1)}, s16[144,256]{1,0:T(8,128)(2,1)S(1)}, u32[]{:S(2)}, u32[]{:S(2)}) collective-permute-start(s16[144,256]{1,0:T(8,128)(2,1)S(1)} %get-tuple-element.52), channel_id=1, source_target_pairs={{0,20},{4,16},{8,28},{12,24},{16,4},{20,0},{24,12},{28,8},{1,21},{... | collective-permute-start | bytes 221192 | tf_op jit(solution)/shard_map/ppermute | solution.py:486
  58.8 7.0 %collective-permute-start.20 = (s16[144,256]{1,0:T(8,128)(2,1)S(1)}, s16[144,256]{1,0:T(8,128)(2,1)S(1)}, u32[]{:S(2)}, u32[]{:S(2)}) collective-permute-start(s16[144,256]{1,0:T(8,128)(2,1)S(1)} %get-tuple-element.58), channel_id=1, source_target_pairs={{0,24},{4,28},{8,16},{12,20},{16,8},{20,12},{24,0},{28,4},{1,25},{... | collective-permute-start | bytes 221192 | tf_op jit(solution)/shard_map/ppermute | solution.py:486
  62.4 4.4 %collective-permute-start.21 = (s16[144,256]{1,0:T(8,128)(2,1)S(1)}, s16[144,256]{1,0:T(8,128)(2,1)S(1)}, u32[]{:S(2)}, u32[]{:S(2)}) collective-permute-start(s16[144,256]{1,0:T(8,128)(2,1)S(1)} %get-tuple-element.59), channel_id=1, source_target_pairs={{0,4},{4,0},{8,12},{12,8},{16,20},{20,16},{24,28},{28,24},{1,5},{5... | collective-permute-start | bytes 221192 | tf_op jit(solution)/shard_map/ppermute | solution.py:486
  63.8 4.4 %collective-permute-start.22 = (s16[144,256]{1,0:T(8,128)(2,1)S(1)}, s16[144,256]{1,0:T(8,128)(2,1)S(1)}, u32[]{:S(2)}, u32[]{:S(2)}) collective-permute-start(s16[144,256]{1,0:T(8,128)(2,1)S(1)} %get-tuple-element.60), channel_id=1, source_target_pairs={{0,8},{4,12},{8,0},{12,4},{16,24},{20,28},{24,16},{28,20},{1,9},{5... | collective-permute-start | bytes 221192 | tf_op jit(solution)/shard_map/ppermute | solution.py:486
  63.8 5.3 %collective-permute-start.23 = (s16[144,256]{1,0:T(8,128)(2,1)S(1)}, s16[144,256]{1,0:T(8,128)(2,1)S(1)}, u32[]{:S(2)}, u32[]{:S(2)}) collective-permute-start(s16[144,256]{1,0:T(8,128)(2,1)S(1)} %get-tuple-element.61), channel_id=1, source_target_pairs={{0,12},{4,8},{8,4},{12,0},{16,28},{20,24},{24,20},{28,16},{1,13},{... | collective-permute-start | bytes 221192 | tf_op jit(solution)/shard_map/ppermute | solution.py:486
  69.3 6.2 %collective-permute-start.24 = (bf16[128,256]{1,0:T(8,128)(2,1)S(1)}, bf16[128,256]{1,0:T(8,128)(2,1)S(1)}, u32[]{:S(2)}, u32[]{:S(2)}) collective-permute-start(bf16[128,256]{1,0:T(8,128)(2,1)S(1)} %last_step.1.refs_3_), channel_id=1, source_target_pairs={{0,24},{4,28},{8,16},{12,20},{16,8},{20,12},{24,0},{28,4},{1,25},{... | collective-permute-start | bytes 196616 | tf_op jit(solution)/shard_map/ppermute | solution.py:486
  72.0 6.1 %collective-permute-start.25 = (bf16[128,256]{1,0:T(8,128)(2,1)S(1)}, bf16[128,256]{1,0:T(8,128)(2,1)S(1)}, u32[]{:S(2)}, u32[]{:S(2)}) collective-permute-start(bf16[128,256]{1,0:T(8,128)(2,1)S(1)} %last_step.1.refs_3_), channel_id=1, source_target_pairs={{0,16},{4,20},{8,24},{12,28},{16,0},{20,4},{24,8},{28,12},{1,17},{... | collective-permute-start | bytes 196616 | tf_op jit(solution)/shard_map/ppermute | solution.py:486
  72.9 6.3 %collective-permute-start.26 = (bf16[128,256]{1,0:T(8,128)(2,1)S(1)}, bf16[128,256]{1,0:T(8,128)(2,1)S(1)}, u32[]{:S(2)}, u32[]{:S(2)}) collective-permute-start(bf16[128,256]{1,0:T(8,128)(2,1)S(1)} %last_step.1.refs_3_), channel_id=1, source_target_pairs={{0,8},{4,12},{8,0},{12,4},{16,24},{20,28},{24,16},{28,20},{1,9},{5... | collective-permute-start | bytes 196616 | tf_op jit(solution)/shard_map/ppermute | solution.py:486
  73.8 6.3 %collective-permute-start.30 = (bf16[128,256]{1,0:T(8,128)(2,1)S(1)}, bf16[128,256]{1,0:T(8,128)(2,1)S(1)}, u32[]{:S(2)}, u32[]{:S(2)}) collective-permute-start(bf16[128,256]{1,0:T(8,128)(2,1)S(1)} %last_step.1.refs_3_), channel_id=1, source_target_pairs={{0,4},{4,0},{8,12},{12,8},{16,20},{20,16},{24,28},{28,24},{1,5},{5... | collective-permute-start | bytes 196616 | tf_op jit(solution)/shard_map/ppermute | solution.py:486
  75.6 4.5 %collective-permute-start.27 = (bf16[128,256]{1,0:T(8,128)(2,1)S(1)}, bf16[128,256]{1,0:T(8,128)(2,1)S(1)}, u32[]{:S(2)}, u32[]{:S(2)}) collective-permute-start(bf16[128,256]{1,0:T(8,128)(2,1)S(1)} %collective-permute-done.24.refs_0_), channel_id=1, source_target_pairs={{0,4},{4,0},{8,12},{12,8},{16,20},{20,16},{24,28},{28,24},{1,5},{5... | collective-permute-start | bytes 196616 | tf_op jit(solution)/shard_map/ppermute | solution.py:486
  78.0 4.8 %collective-permute-start.28 = (bf16[128,256]{1,0:T(8,128)(2,1)S(1)}, bf16[128,256]{1,0:T(8,128)(2,1)S(1)}, u32[]{:S(2)}, u32[]{:S(2)}) collective-permute-start(bf16[128,256]{1,0:T(8,128)(2,1)S(1)} %collective-permute-done.25.refs_1_), channel_id=1, source_target_pairs={{0,4},{4,0},{8,12},{12,8},{16,20},{20,16},{24,28},{28,24},{1,5},{5... | collective-permute-start | bytes 196616 | tf_op jit(solution)/shard_map/ppermute | solution.py:486
  79.2 4.4 %collective-permute-start.29 = (bf16[128,256]{1,0:T(8,128)(2,1)S(1)}, bf16[128,256]{1,0:T(8,128)(2,1)S(1)}, u32[]{:S(2)}, u32[]{:S(2)}) collective-permute-start(bf16[128,256]{1,0:T(8,128)(2,1)S(1)} %collective-permute-done.26.refs_2_), channel_id=1, source_target_pairs={{0,4},{4,0},{8,12},{12,8},{16,20},{20,16},{24,28},{28,24},{1,5},{5... | collective-permute-start | bytes 196616 | tf_op jit(solution)/shard_map/ppermute | solution.py:486

commit v6 on v5

--- a/solution.py
+++ b/solution.py
@@ -559,7 +559,8 @@
     own = rest[0]
     late = [d - 1 for d in by_x] + list(range(1, peers // 2))
     coded = combine([sent[d - 1] for d in by_x] + list(rest[1:]), [arrived_x[d] for d in by_x])
-    sent = {d: x for d, x in sent.items() if d not in late} | dict(zip(late, coded))
+    coded = dict(zip(late, coded))
+    sent = {d: x for d, x in sent.items() if d not in late} | {d: coded[d] for d in sorted(late)}
     part = last_step(v, low, high, own, [swap(x, "svc", d) for d, x in sent.items()])
     column = {d: swap(part, "svc", d) for d in range(peers - 2, 0, -2)}
     column[0] = part

time: 84.6 us -> 84.3 us (level)
  transfers between devices with their start and end apart: 31 -> 31, of which waited for: 18 -> 19; matrix products, arithmetic and copies ran while one was open for 0% -> 0% of each run, Pallas kernels for 24% -> 24%
where the time goes in v6:
time: 84.3 us; the launch traced here: 84.2 us
  starting transfers between devices  30.7 us (36%)
  Pallas kernels  29.1 us (35%)
  waiting for transfers between devices  22.9 us (27%)
  between operations  1.53 us (2%)
    ppermute x29, starting transfers between devices, swap(): lax.ppermute(x, axis, [(i, i ^ mask) for i in range(lax.axis_size(axis))])  28.9 us
    ppermute x29, waiting for transfers between devices, swap(): lax.ppermute(x, axis, [(i, i ^ mask) for i in range(lax.axis_size(axis))])  20.2 us
    pallas_call x3, Pallas kernels, u_pass(): pl.pallas_call(functools.partial(u_body, first, count, across, len(after)...  8.38 us
    pallas_call x3, Pallas kernels, v_pass(): pl.pallas_call(functools.partial(v_body, first, count, across, opening, l...  8.08 us
    pallas_call x1, Pallas kernels, first_u_pass(): pl.pallas_call(functools.partial(first_u_body, count, down, across), out_...  5.04 us
    pallas_call x2, Pallas kernels, v_end(): pl.pallas_call(functools.partial(v_end_body, first, count, across, peers,...  4.08 us
    ppermute x2, waiting for transfers between devices, shift(): return lax.ppermute(x, axis, [(i, (i + by) % n) for i in range(n)])  2.72 us
    ppermute x2, starting transfers between devices, shift(): return lax.ppermute(x, axis, [(i, (i + by) % n) for i in range(n)])  1.75 us
  transfers between devices with their start and end apart: 31, of which 19 were waited for; matrix products, arithmetic and copies ran while one was open for 0% of the time, Pallas kernels for 24%

profile of v6, /device:TPU:0, one launch (start us, length us, event | category | flops | bytes accessed | tf_op | source)
XLA Modules:
  0.0 84.2 jit_solution(12096722065409288402)
XLA Ops:
  1.3 5.0 %u_pass_0.1 = (f32[512,256]{1,0:T(8,128)S(1)}, s16[528,256]{1,0:T(8,128)(2,1)S(1)}, s32[384]{0:T(512)S(1)}) custom-call(s32[1,1,154]{2,1,0:T(1,128)} %row_hbm.1, s32[1,1,154]{2,1,0:T(1,128)} %col_hbm.1, s32[1,1]{1,0:T(1,128)S(6)} %copy.14.live_ref, bf16[6144,256]{1,0:T(8,128)(2,1)} %u_ref.13, bf16[1024,256]{1,0:T(8,128)(2,1)} %v_ref.7, ...), custom_call_target="tpu_custom_call" | custom-call | flops 1 | bytes 1 | tf_op jit(solution)/shard_map/u_pass_0/pallas_call | solution.py:180
  6.4 0.5 collective-permute-start
  6.8 1.2 %collective-permute-done.refs_0_ = s16[528,256]{1,0:T(8,128)(2,1)S(1)} collective-permute-done((s16[528,256]{1,0:T(8,128)(2,1)S(1)}, s16[528,256]{1,0:T(8,128)(2,1)S(1)}, u32[]{:S(2)}, u32[]{:S(2)}) %collective-permute-start) | collective-permute-done | bytes 270368 | tf_op jit(solution)/shard_map/ppermute | solution.py:486
  8.2 3.0 %collective-permute-start.4 = (s16[528,256]{1,0:T(8,128)(2,1)S(1)}, s16[528,256]{1,0:T(8,128)(2,1)S(1)}, u32[]{:S(2)}, u32[]{:S(2)}) collective-permute-start(s16[528,256]{1,0:T(8,128)(2,1)S(1)} %core_sum.4.refs_0_.code), channel_id=1, source_target_pairs={{0,2},{1,3},{2,0},{3,1},{4,6},{5,7},{6,4},{7,5},{8,10},{9,11},{10,... | collective-permute-start | bytes 811016 | tf_op jit(solution)/shard_map/ppermute | solution.py:486
  11.2 2.6 %u_pass_8.1 = (f32[768,256]{1,0:T(8,128)S(1)}, s16[400,256]{1,0:T(8,128)(2,1)S(1)}, s16[400,256]{1,0:T(8,128)(2,1)S(1)}) custom-call(s32[384]{0:T(512)S(1)} %get-tuple-element.32.slots.refs_0_, bf16[6144,256]{1,0:T(8,128)(2,1)S(1)} %copy-done, bf16[1024,256]{1,0:T(8,128)(2,1)S(1)} %copy-done.1, bf16[154,128,128]{2,1,0:T(8,128)(2,1)S(1)} %bitcast.4, ...), custom_call_target="tpu_custom_call" | custom-call | flops 1 | bytes 1 | tf_op jit(solution)/shard_map/u_pass_8/pallas_call | solution.py:210
  13.8 0.5 collective-permute-start.2
  14.3 0.9 %collective-permute-done.1.refs_0_ = s16[400,256]{1,0:T(8,128)(2,1)S(1)} collective-permute-done((s16[400,256]{1,0:T(8,128)(2,1)S(1)}, s16[400,256]{1,0:T(8,128)(2,1)S(1)}, u32[]{:S(2)}, u32[]{:S(2)}) %collective-permute-start.1) | collective-permute-done | bytes 204832 | tf_op jit(solution)/shard_map/ppermute | solution.py:486
  15.9 2.0 %collective-permute-done.4.code_in = s16[528,256]{1,0:T(8,128)(2,1)S(1)} collective-permute-done((s16[528,256]{1,0:T(8,128)(2,1)S(1)}, s16[528,256]{1,0:T(8,128)(2,1)S(1)}, u32[]{:S(2)}, u32[]{:S(2)}) %collective-permute-start.4) | collective-permute-done | bytes 270368 | tf_op jit(solution)/shard_map/ppermute | solution.py:486
  18.2 3.2 %u_pass_20.1 = (f32[1024,256]{1,0:T(8,128)S(1)}, s16[528,256]{1,0:T(8,128)(2,1)S(1)}, s16[528,256]{1,0:T(8,128)(2,1)S(1)}) custom-call(s32[384]{0:T(512)S(1)} %get-tuple-element.32.slots.refs_0_, bf16[6144,256]{1,0:T(8,128)(2,1)S(1)} %copy-done, bf16[1024,256]{1,0:T(8,128)(2,1)S(1)} %copy-done.1, bf16[154,128,128]{2,1,0:T(8,128)(2,1)S(1)} %bitcast.5, ...), custom_call_target="tpu_custom_call" | custom-call | flops 1 | bytes 1 | tf_op jit(solution)/shard_map/u_pass_20/pallas_call | solution.py:210
  21.4 0.5 collective-permute-start.6
  22.0 1.0 %collective-permute-done.5.refs_0_ = s16[528,256]{1,0:T(8,128)(2,1)S(1)} collective-permute-done((s16[528,256]{1,0:T(8,128)(2,1)S(1)}, s16[528,256]{1,0:T(8,128)(2,1)S(1)}, u32[]{:S(2)}, u32[]{:S(2)}) %collective-permute-start.5) | collective-permute-done | bytes 270368 | tf_op jit(solution)/shard_map/ppermute | solution.py:486
  23.0 0.4 collective-permute-done.6.refs_1_
  23.7 2.4 %collective-permute-start.10 = (s16[1040,256]{1,0:T(8,128)(2,1)S(1)}, s16[1040,256]{1,0:T(8,128)(2,1)S(1)}, u32[]{:S(2)}, u32[]{:S(2)}) collective-permute-start(s16[1040,256]{1,0:T(8,128)(2,1)S(1)} %core_sum.6.refs_0_.code), channel_id=1, source_target_pairs={{0,2},{1,3},{2,0},{3,1},{4,6},{5,7},{6,4},{7,5},{8,10},{9,11},{10,... | collective-permute-start | bytes 1597448 | tf_op jit(solution)/shard_map/ppermute | solution.py:486
  26.1 2.2 %v_pass_0.1 = (bf16[6144,256]{1,0:T(8,128)(2,1)}, f32[256,1024]{1,0:T(8,128)S(1)}) custom-call(s32[384]{0:T(512)S(1)} %get-tuple-element.32.slots.refs_0_, bf16[1024,256]{1,0:T(8,128)(2,1)S(1)} %copy-done.1, bf16[154,128,128]{2,1,0:T(8,128)(2,1)S(1)} %bitcast.6, bf16[512,256]{1,0:T(8,128)(2,1)S(1)} %update_0.1.refs_0_.refs_3_, ...), custom_call_target="tpu_custom_call" | custom-call | flops 1 | bytes 1 | tf_op jit(solution)/shard_map/v_pass_0/pallas_call | solution.py:326
  28.6 2.6 %u_pass_36.1 = (f32[768,256]{1,0:T(8,128)S(1)}, s16[784,256]{1,0:T(8,128)(2,1)S(1)}) custom-call(s32[384]{0:T(512)S(1)} %get-tuple-element.32.slots.refs_0_, bf16[6144,256]{1,0:T(8,128)(2,1)S(1)} %copy-done, bf16[1024,256]{1,0:T(8,128)(2,1)S(1)} %copy-done.1, bf16[154,128,128]{2,1,0:T(8,128)(2,1)S(1)} %bitcast.7, bf16[768,256]{1,0:T(8,128)(2,1)S(1)} %update_8.1.refs_0_.refs_3_), custom_call_target="tpu_custom_call" | custom-call | flops 1 | bytes 1 | tf_op jit(solution)/shard_map/u_pass_36/pallas_call | solution.py:210
  31.3 0.5 collective-permute-start.11
  31.8 1.8 %collective-permute-done.11.refs_4_ = bf16[768,256]{1,0:T(8,128)(2,1)S(1)} collective-permute-done((bf16[768,256]{1,0:T(8,128)(2,1)S(1)}, bf16[768,256]{1,0:T(8,128)(2,1)S(1)}, u32[]{:S(2)}, u32[]{:S(2)}) %collective-permute-start.11) | collective-permute-done | bytes 393248 | tf_op jit(solution)/shard_map/ppermute | solution.py:486
  33.6 2.7 %v_pass_8.1 = (bf16[6144,256]{1,0:T(8,128)(2,1)}, f32[256,1024]{1,0:T(8,128)S(1)}) custom-call(s32[384]{0:T(512)S(1)} %get-tuple-element.32.slots.refs_0_, bf16[1024,256]{1,0:T(8,128)(2,1)S(1)} %copy-done.1, bf16[154,128,128]{2,1,0:T(8,128)(2,1)S(1)} %bitcast.8, bf16[768,256]{1,0:T(8,128)(2,1)S(1)} %update_8.1.refs_0_.refs_3_, ...), custom_call_target="tpu_custom_call", output_to_operand_aliasing={{0}: (6, {})} | custom-call | flops 1 | bytes 1 | tf_op jit(solution)/shard_map/v_pass_8/pallas_call | solution.py:326
  36.7 2.0 %collective-permute-done.10.code_in = s16[1040,256]{1,0:T(8,128)(2,1)S(1)} collective-permute-done((s16[1040,256]{1,0:T(8,128)(2,1)S(1)}, s16[1040,256]{1,0:T(8,128)(2,1)S(1)}, u32[]{:S(2)}, u32[]{:S(2)}) %collective-permute-start.10) | collective-permute-done | bytes 532512 | tf_op jit(solution)/shard_map/ppermute | solution.py:486
  38.7 0.4 update_20.1.refs_3_
  39.3 0.5 collective-permute-start.13
  39.9 1.7 %collective-permute-start.15 = (bf16[16,256]{1,0:T(8,128)(2,1)S(1)}, bf16[16,256]{1,0:T(8,128)(2,1)S(1)}, u32[]{:S(2)}, u32[]{:S(2)}) collective-permute-start(bf16[16,256]{1,0:T(8,128)(2,1)S(1)} %get-tuple-element.62), channel_id=1, source_target_pairs={{0,3},{1,0},{2,1},{3,2},{4,7},{5,4},{6,5},{7,6},{8,11},{9,8},{10,9... | collective-permute-start | bytes 24584 | tf_op jit(solution)/shard_map/ppermute | solution.py:491
  41.5 3.1 %v_pass_20.1 = (bf16[6144,256]{1,0:T(8,128)(2,1)}, f32[256,1024]{1,0:T(8,128)S(1)}) custom-call(s32[384]{0:T(512)S(1)} %get-tuple-element.32.slots.refs_0_, bf16[1024,256]{1,0:T(8,128)(2,1)S(1)} %copy-done.1, bf16[154,128,128]{2,1,0:T(8,128)(2,1)S(1)} %bitcast.9, bf16[1024,256]{1,0:T(8,128)(2,1)S(1)} %update_20.1.refs_3_, ...), custom_call_target="tpu_custom_call", output_to_operand_aliasing={{0}: (7, {})} | custom-call | flops 1 | bytes 1 | tf_op jit(solution)/shard_map/v_pass_20/pallas_call | solution.py:326
  44.7 2.7 %collective-permute-done.14.refs_2_.low = bf16[16,256]{1,0:T(8,128)(2,1)S(1)} collective-permute-done((bf16[16,256]{1,0:T(8,128)(2,1)S(1)}, bf16[16,256]{1,0:T(8,128)(2,1)S(1)}, u32[]{:S(2)}, u32[]{:S(2)}) %collective-permute-start.14) | collective-permute-done | bytes 8224 | tf_op jit(solution)/shard_map/ppermute | solution.py:491
  47.4 0.7 collective-permute-done.9.code_in
  48.6 1.6 %collective-permute-done.16.refs_4_ = bf16[768,256]{1,0:T(8,128)(2,1)S(1)} collective-permute-done((bf16[768,256]{1,0:T(8,128)(2,1)S(1)}, bf16[768,256]{1,0:T(8,128)(2,1)S(1)}, u32[]{:S(2)}, u32[]{:S(2)}) %collective-permute-start.16) | collective-permute-done | bytes 393248 | tf_op jit(solution)/shard_map/ppermute | solution.py:486
  50.2 2.2 %v_end_far.1 = (bf16[6144,256]{1,0:T(8,128)(2,1)}, s16[144,256]{1,0:T(8,128)(2,1)S(1)}, s16[144,256]{1,0:T(8,128)(2,1)S(1)}, f32[128,256]{1,0:T(8,128)S(1)}, s16[144,256]{1,0:T(8,128)(2,1)S(1)}) custom-call(s32[384]{0:T(512)S(1)} %get-tuple-element.32.slots.refs_0_, bf16[1024,256]{1,0:T(8,128)(2,1)S(1)} %copy-done.1, ...), custom_call_target="tpu_custom_call", output_to_operand_aliasing={{0}: (6, {})} | custom-call | flops 1 | bytes 1 | tf_op jit(solution)/shard_map/v_end_far/pallas_call | solution.py:385
  52.4 1.3 %collective-permute-start.19 = (s16[144,256]{1,0:T(8,128)(2,1)S(1)}, s16[144,256]{1,0:T(8,128)(2,1)S(1)}, u32[]{:S(2)}, u32[]{:S(2)}) collective-permute-start(s16[144,256]{1,0:T(8,128)(2,1)S(1)} %get-tuple-element.57), channel_id=1, source_target_pairs={{0,4},{4,0},{8,12},{12,8},{16,20},{20,16},{24,28},{28,24},{1,5},{5... | collective-permute-start | bytes 221192 | tf_op jit(solution)/shard_map/ppermute | solution.py:486
  53.8 2.6 %collective-permute-start.17 = (s16[144,256]{1,0:T(8,128)(2,1)S(1)}, s16[144,256]{1,0:T(8,128)(2,1)S(1)}, u32[]{:S(2)}, u32[]{:S(2)}) collective-permute-start(s16[144,256]{1,0:T(8,128)(2,1)S(1)} %get-tuple-element.50.refs_6_), channel_id=1, source_target_pairs={{0,16},{4,20},{8,24},{12,28},{16,0},{20,4},{24,8},{28,12},{1,17},{... | collective-permute-start | bytes 221192 | tf_op jit(solution)/shard_map/ppermute | solution.py:486
  56.4 0.5 collective-permute-start.18
  56.9 1.9 %v_end_near.1 = (f32[128,256]{1,0:T(8,128)S(1)}, f32[128,256]{1,0:T(8,128)S(1)}, f32[128,256]{1,0:T(8,128)S(1)}, f32[128,256]{1,0:T(8,128)S(1)}) custom-call(s32[384]{0:T(512)S(1)} %get-tuple-element.32.slots.refs_0_, bf16[1024,256]{1,0:T(8,128)(2,1)S(1)} %copy-done.1, bf16[154,128,128]{2,1,0:T(8,128)(2,1)S(1)} %bitcast.11, ...), custom_call_target="tpu_custom_call" | custom-call | flops 1 | bytes 1 | tf_op jit(solution)/shard_map/v_end_near/pallas_call | solution.py:385
  58.9 1.3 %collective-permute-start.20 = (s16[144,256]{1,0:T(8,128)(2,1)S(1)}, s16[144,256]{1,0:T(8,128)(2,1)S(1)}, u32[]{:S(2)}, u32[]{:S(2)}) collective-permute-start(s16[144,256]{1,0:T(8,128)(2,1)S(1)} %get-tuple-element.58), channel_id=1, source_target_pairs={{0,4},{4,0},{8,12},{12,8},{16,20},{20,16},{24,28},{28,24},{1,5},{5... | collective-permute-start | bytes 221192 | tf_op jit(solution)/shard_map/ppermute | solution.py:486
  60.3 1.7 %collective-permute-start.21 = (s16[144,256]{1,0:T(8,128)(2,1)S(1)}, s16[144,256]{1,0:T(8,128)(2,1)S(1)}, u32[]{:S(2)}, u32[]{:S(2)}) collective-permute-start(s16[144,256]{1,0:T(8,128)(2,1)S(1)} %get-tuple-element.59), channel_id=1, source_target_pairs={{0,8},{4,12},{8,0},{12,4},{16,24},{20,28},{24,16},{28,20},{1,9},{5... | collective-permute-start | bytes 221192 | tf_op jit(solution)/shard_map/ppermute | solution.py:486
  62.0 0.5 collective-permute-start.22
  62.9 2.9 %collective-permute-start.23 = (s16[144,256]{1,0:T(8,128)(2,1)S(1)}, s16[144,256]{1,0:T(8,128)(2,1)S(1)}, u32[]{:S(2)}, u32[]{:S(2)}) collective-permute-start(s16[144,256]{1,0:T(8,128)(2,1)S(1)} %get-tuple-element.61), channel_id=1, source_target_pairs={{0,24},{4,28},{8,16},{12,20},{16,8},{20,12},{24,0},{28,4},{1,25},{... | collective-permute-start | bytes 221192 | tf_op jit(solution)/shard_map/ppermute | solution.py:486
  65.7 1.5 %collective-permute-done.22.refs_4_ = s16[144,256]{1,0:T(8,128)(2,1)S(1)} collective-permute-done((s16[144,256]{1,0:T(8,128)(2,1)S(1)}, s16[144,256]{1,0:T(8,128)(2,1)S(1)}, u32[]{:S(2)}, u32[]{:S(2)}) %collective-permute-start.22) | collective-permute-done | bytes 73760 | tf_op jit(solution)/shard_map/ppermute | solution.py:486
  67.2 1.8 %collective-permute-done.23.refs_5_ = s16[144,256]{1,0:T(8,128)(2,1)S(1)} collective-permute-done((s16[144,256]{1,0:T(8,128)(2,1)S(1)}, s16[144,256]{1,0:T(8,128)(2,1)S(1)}, u32[]{:S(2)}, u32[]{:S(2)}) %collective-permute-start.23) | collective-permute-done | bytes 73760 | tf_op jit(solution)/shard_map/ppermute | solution.py:486
  69.3 2.9 %collective-permute-start.24 = (bf16[128,256]{1,0:T(8,128)(2,1)S(1)}, bf16[128,256]{1,0:T(8,128)(2,1)S(1)}, u32[]{:S(2)}, u32[]{:S(2)}) collective-permute-start(bf16[128,256]{1,0:T(8,128)(2,1)S(1)} %last_step.1.refs_3_), channel_id=1, source_target_pairs={{0,24},{4,28},{8,16},{12,20},{16,8},{20,12},{24,0},{28,4},{1,25},{... | collective-permute-start | bytes 196616 | tf_op jit(solution)/shard_map/ppermute | solution.py:486
  72.2 1.5 %collective-permute-start.26 = (bf16[128,256]{1,0:T(8,128)(2,1)S(1)}, bf16[128,256]{1,0:T(8,128)(2,1)S(1)}, u32[]{:S(2)}, u32[]{:S(2)}) collective-permute-start(bf16[128,256]{1,0:T(8,128)(2,1)S(1)} %last_step.1.refs_3_), channel_id=1, source_target_pairs={{0,8},{4,12},{8,0},{12,4},{16,24},{20,28},{24,16},{28,20},{1,9},{5... | collective-permute-start | bytes 196616 | tf_op jit(solution)/shard_map/ppermute | solution.py:486
  73.7 1.6 %collective-permute-start.30 = (bf16[128,256]{1,0:T(8,128)(2,1)S(1)}, bf16[128,256]{1,0:T(8,128)(2,1)S(1)}, u32[]{:S(2)}, u32[]{:S(2)}) collective-permute-start(bf16[128,256]{1,0:T(8,128)(2,1)S(1)} %last_step.1.refs_3_), channel_id=1, source_target_pairs={{0,4},{4,0},{8,12},{12,8},{16,20},{20,16},{24,28},{28,24},{1,5},{5... | collective-permute-start | bytes 196616 | tf_op jit(solution)/shard_map/ppermute | solution.py:486
  75.7 1.4 %collective-permute-start.27 = (bf16[128,256]{1,0:T(8,128)(2,1)S(1)}, bf16[128,256]{1,0:T(8,128)(2,1)S(1)}, u32[]{:S(2)}, u32[]{:S(2)}) collective-permute-start(bf16[128,256]{1,0:T(8,128)(2,1)S(1)} %collective-permute-done.24.refs_0_), channel_id=1, source_target_pairs={{0,4},{4,0},{8,12},{12,8},{16,20},{20,16},{24,28},{28,24},{1,5},{5... | collective-permute-start | bytes 196616 | tf_op jit(solution)/shard_map/ppermute | solution.py:486
  77.1 0.4 collective-permute-done.25.refs_1_
  77.5 1.5 %collective-permute-start.28 = (bf16[128,256]{1,0:T(8,128)(2,1)S(1)}, bf16[128,256]{1,0:T(8,128)(2,1)S(1)}, u32[]{:S(2)}, u32[]{:S(2)}) collective-permute-start(bf16[128,256]{1,0:T(8,128)(2,1)S(1)} %collective-permute-done.25.refs_1_), channel_id=1, source_target_pairs={{0,4},{4,0},{8,12},{12,8},{16,20},{20,16},{24,28},{28,24},{1,5},{5... | collective-permute-start | bytes 196616 | tf_op jit(solution)/shard_map/ppermute | solution.py:486
  79.1 0.5 collective-permute-start.29
  79.6 0.6 collective-permute-done.27.refs_4_
  80.1 1.7 %collective-permute-done.28.refs_5_ = bf16[128,256]{1,0:T(8,128)(2,1)S(1)} collective-permute-done((bf16[128,256]{1,0:T(8,128)(2,1)S(1)}, bf16[128,256]{1,0:T(8,128)(2,1)S(1)}, u32[]{:S(2)}, u32[]{:S(2)}) %collective-permute-start.28) | collective-permute-done | bytes 65568 | tf_op jit(solution)/shard_map/ppermute | solution.py:486
  81.8 1.5 %collective-permute-done.29.refs_6_ = bf16[128,256]{1,0:T(8,128)(2,1)S(1)} collective-permute-done((bf16[128,256]{1,0:T(8,128)(2,1)S(1)}, bf16[128,256]{1,0:T(8,128)(2,1)S(1)}, u32[]{:S(2)}, u32[]{:S(2)}) %collective-permute-start.29) | collective-permute-done | bytes 65568 | tf_op jit(solution)/shard_map/ppermute | solution.py:486
  83.3 0.8 join.1
  (45 shorter events, 4.2 us)
Async XLA Ops:
  1.3 9.9 %slice-start = ((s8[5046272]{0:T(1024)(128)(4,1)}), s8[4194304]{0:T(1024)(128)(4,1)S(1)}, s32[]{:S(2)}) async-start(s8[5046272]{0:T(1024)(128)(4,1)} %bitcast.2), calls=%async_computation | async-start | bytes 8388608
  1.3 9.9 %slice-start.1 = ((s8[5046272]{0:T(1024)(128)(4,1)}), s8[851968]{0:T(1024)(128)(4,1)S(1)}, s32[]{:S(2)}) async-start(s8[5046272]{0:T(1024)(128)(4,1)} %bitcast.2), calls=%async_computation.1 | async-start | bytes 1703936
  1.3 9.9 %copy-start = (bf16[6144,256]{1,0:T(8,128)(2,1)S(1)}, bf16[6144,256]{1,0:T(8,128)(2,1)}, u32[]{:S(2)}) copy-start(bf16[6144,256]{1,0:T(8,128)(2,1)} %u_ref.13) | copy-start | bytes 9437188
  1.3 9.8 %copy-start.1 = (bf16[1024,256]{1,0:T(8,128)(2,1)S(1)}, bf16[1024,256]{1,0:T(8,128)(2,1)}, u32[]{:S(2)}) copy-start(bf16[1024,256]{1,0:T(8,128)(2,1)} %v_ref.7) | copy-start | bytes 1572868
  6.4 1.6 %collective-permute-start = (s16[528,256]{1,0:T(8,128)(2,1)S(1)}, s16[528,256]{1,0:T(8,128)(2,1)S(1)}, u32[]{:S(2)}, u32[]{:S(2)}) collective-permute-start(s16[528,256]{1,0:T(8,128)(2,1)S(1)} %get-tuple-element.34), channel_id=1, source_target_pairs={{0,1},{1,0},{2,3},{3,2},{4,5},{5,4},{6,7},{7,6},{8,9},{9,8},{10,11... | collective-permute-start | bytes 811016 | tf_op jit(solution)/shard_map/ppermute | solution.py:486
  8.2 9.8 %collective-permute-start.4 = (s16[528,256]{1,0:T(8,128)(2,1)S(1)}, s16[528,256]{1,0:T(8,128)(2,1)S(1)}, u32[]{:S(2)}, u32[]{:S(2)}) collective-permute-start(s16[528,256]{1,0:T(8,128)(2,1)S(1)} %core_sum.4.refs_0_.code), channel_id=1, source_target_pairs={{0,2},{1,3},{2,0},{3,1},{4,6},{5,7},{6,4},{7,5},{8,10},{9,11},{10,... | collective-permute-start | bytes 811016 | tf_op jit(solution)/shard_map/ppermute | solution.py:486
  13.8 1.5 %collective-permute-start.1 = (s16[400,256]{1,0:T(8,128)(2,1)S(1)}, s16[400,256]{1,0:T(8,128)(2,1)S(1)}, u32[]{:S(2)}, u32[]{:S(2)}) collective-permute-start(s16[400,256]{1,0:T(8,128)(2,1)S(1)} %get-tuple-element.36), channel_id=1, source_target_pairs={{0,1},{1,0},{2,3},{3,2},{4,5},{5,4},{6,7},{7,6},{8,9},{9,8},{10,11... | collective-permute-start | bytes 614408 | tf_op jit(solution)/shard_map/ppermute | solution.py:486
  13.8 1.7 %collective-permute-start.2 = (s16[400,256]{1,0:T(8,128)(2,1)S(1)}, s16[400,256]{1,0:T(8,128)(2,1)S(1)}, u32[]{:S(2)}, u32[]{:S(2)}) collective-permute-start(s16[400,256]{1,0:T(8,128)(2,1)S(1)} %get-tuple-element.37), channel_id=1, source_target_pairs={{0,1},{1,0},{2,3},{3,2},{4,5},{5,4},{6,7},{7,6},{8,9},{9,8},{10,11... | collective-permute-start | bytes 614408 | tf_op jit(solution)/shard_map/ppermute | solution.py:486
  15.8 12.5 %collective-permute-start.3 = (s16[784,256]{1,0:T(8,128)(2,1)S(1)}, s16[784,256]{1,0:T(8,128)(2,1)S(1)}, u32[]{:S(2)}, u32[]{:S(2)}) collective-permute-start(s16[784,256]{1,0:T(8,128)(2,1)S(1)} %core_sum.5.refs_0_.code), channel_id=1, source_target_pairs={{0,2},{1,3},{2,0},{3,1},{4,6},{5,7},{6,4},{7,5},{8,10},{9,11},{10,... | collective-permute-start | bytes 1204232 | tf_op jit(solution)/shard_map/ppermute | solution.py:486
  21.3 1.6 %collective-permute-start.5 = (s16[528,256]{1,0:T(8,128)(2,1)S(1)}, s16[528,256]{1,0:T(8,128)(2,1)S(1)}, u32[]{:S(2)}, u32[]{:S(2)}) collective-permute-start(s16[528,256]{1,0:T(8,128)(2,1)S(1)} %get-tuple-element.39), channel_id=1, source_target_pairs={{0,1},{1,0},{2,3},{3,2},{4,5},{5,4},{6,7},{7,6},{8,9},{9,8},{10,11... | collective-permute-start | bytes 811016 | tf_op jit(solution)/shard_map/ppermute | solution.py:486
  21.4 1.9 %collective-permute-start.6 = (s16[528,256]{1,0:T(8,128)(2,1)S(1)}, s16[528,256]{1,0:T(8,128)(2,1)S(1)}, u32[]{:S(2)}, u32[]{:S(2)}) collective-permute-start(s16[528,256]{1,0:T(8,128)(2,1)S(1)} %get-tuple-element.40), channel_id=1, source_target_pairs={{0,1},{1,0},{2,3},{3,2},{4,5},{5,4},{6,7},{7,6},{8,9},{9,8},{10,11... | collective-permute-start | bytes 811016 | tf_op jit(solution)/shard_map/ppermute | solution.py:486
  21.9 4.2 %collective-permute-start.7 = (bf16[512,256]{1,0:T(8,128)(2,1)S(1)}, bf16[512,256]{1,0:T(8,128)(2,1)S(1)}, u32[]{:S(2)}, u32[]{:S(2)}) collective-permute-start(bf16[512,256]{1,0:T(8,128)(2,1)S(1)} %update_0.1.refs_0_.refs_3_), channel_id=1, source_target_pairs={{0,1},{1,0},{2,3},{3,2},{4,5},{5,4},{6,7},{7,6},{8,9},{9,8},{10,11... | collective-permute-start | bytes 786440 | tf_op jit(solution)/shard_map/ppermute | solution.py:486
  23.7 15.1 %collective-permute-start.10 = (s16[1040,256]{1,0:T(8,128)(2,1)S(1)}, s16[1040,256]{1,0:T(8,128)(2,1)S(1)}, u32[]{:S(2)}, u32[]{:S(2)}) collective-permute-start(s16[1040,256]{1,0:T(8,128)(2,1)S(1)} %core_sum.6.refs_0_.code), channel_id=1, source_target_pairs={{0,2},{1,3},{2,0},{3,1},{4,6},{5,7},{6,4},{7,5},{8,10},{9,11},{10,... | collective-permute-start | bytes 1597448 | tf_op jit(solution)/shard_map/ppermute | solution.py:486
  31.3 5.1 %collective-permute-start.8 = (s16[784,256]{1,0:T(8,128)(2,1)S(1)}, s16[784,256]{1,0:T(8,128)(2,1)S(1)}, u32[]{:S(2)}, u32[]{:S(2)}) collective-permute-start(s16[784,256]{1,0:T(8,128)(2,1)S(1)} %get-tuple-element.43), channel_id=1, source_target_pairs={{0,1},{1,0},{2,3},{3,2},{4,5},{5,4},{6,7},{7,6},{8,9},{9,8},{10,11... | collective-permute-start | bytes 1204232 | tf_op jit(solution)/shard_map/ppermute | solution.py:486
  31.3 2.3 %collective-permute-start.11 = (bf16[768,256]{1,0:T(8,128)(2,1)S(1)}, bf16[768,256]{1,0:T(8,128)(2,1)S(1)}, u32[]{:S(2)}, u32[]{:S(2)}) collective-permute-start(bf16[768,256]{1,0:T(8,128)(2,1)S(1)} %update_8.1.refs_0_.refs_3_), channel_id=1, source_target_pairs={{0,1},{1,0},{2,3},{3,2},{4,5},{5,4},{6,7},{7,6},{8,9},{9,8},{10,11... | collective-permute-start | bytes 1179656 | tf_op jit(solution)/shard_map/ppermute | solution.py:486
  36.6 11.5 %collective-permute-start.9 = (s16[784,256]{1,0:T(8,128)(2,1)S(1)}, s16[784,256]{1,0:T(8,128)(2,1)S(1)}, u32[]{:S(2)}, u32[]{:S(2)}) collective-permute-start(s16[784,256]{1,0:T(8,128)(2,1)S(1)} %core_sum.7.refs_0_.code), channel_id=1, source_target_pairs={{0,2},{1,3},{2,0},{3,1},{4,6},{5,7},{6,4},{7,5},{8,10},{9,11},{10,... | collective-permute-start | bytes 1204232 | tf_op jit(solution)/shard_map/ppermute | solution.py:486
  39.2 2.3 %collective-permute-start.12 = (bf16[512,256]{1,0:T(8,128)(2,1)S(1)}, bf16[512,256]{1,0:T(8,128)(2,1)S(1)}, u32[]{:S(2)}, u32[]{:S(2)}) collective-permute-start(bf16[512,256]{1,0:T(8,128)(2,1)S(1)} %get-tuple-element.65), channel_id=1, source_target_pairs={{0,1},{1,0},{2,3},{3,2},{4,5},{5,4},{6,7},{7,6},{8,9},{9,8},{10,11... | collective-permute-start | bytes 786440 | tf_op jit(solution)/shard_map/ppermute | solution.py:486
  39.3 2.3 %collective-permute-start.13 = (bf16[512,256]{1,0:T(8,128)(2,1)S(1)}, bf16[512,256]{1,0:T(8,128)(2,1)S(1)}, u32[]{:S(2)}, u32[]{:S(2)}) collective-permute-start(bf16[512,256]{1,0:T(8,128)(2,1)S(1)} %get-tuple-element.64), channel_id=1, source_target_pairs={{0,1},{1,0},{2,3},{3,2},{4,5},{5,4},{6,7},{7,6},{8,9},{9,8},{10,11... | collective-permute-start | bytes 786440 | tf_op jit(solution)/shard_map/ppermute | solution.py:486
  39.8 7.6 %collective-permute-start.14 = (bf16[16,256]{1,0:T(8,128)(2,1)S(1)}, bf16[16,256]{1,0:T(8,128)(2,1)S(1)}, u32[]{:S(2)}, u32[]{:S(2)}) collective-permute-start(bf16[16,256]{1,0:T(8,128)(2,1)S(1)} %get-tuple-element.63), channel_id=1, source_target_pairs={{0,1},{1,2},{2,3},{3,0},{4,5},{5,6},{6,7},{7,4},{8,9},{9,10},{10,1... | collective-permute-start | bytes 24584 | tf_op jit(solution)/shard_map/ppermute | solution.py:491
  39.9 7.5 %collective-permute-start.15 = (bf16[16,256]{1,0:T(8,128)(2,1)S(1)}, bf16[16,256]{1,0:T(8,128)(2,1)S(1)}, u32[]{:S(2)}, u32[]{:S(2)}) collective-permute-start(bf16[16,256]{1,0:T(8,128)(2,1)S(1)} %get-tuple-element.62), channel_id=1, source_target_pairs={{0,3},{1,0},{2,1},{3,2},{4,7},{5,4},{6,5},{7,6},{8,11},{9,8},{10,9... | collective-permute-start | bytes 24584 | tf_op jit(solution)/shard_map/ppermute | solution.py:491
  48.5 1.8 %collective-permute-start.16 = (bf16[768,256]{1,0:T(8,128)(2,1)S(1)}, bf16[768,256]{1,0:T(8,128)(2,1)S(1)}, u32[]{:S(2)}, u32[]{:S(2)}) collective-permute-start(bf16[768,256]{1,0:T(8,128)(2,1)S(1)} %update_36.1.refs_3_), channel_id=1, source_target_pairs={{0,1},{1,0},{2,3},{3,2},{4,5},{5,4},{6,7},{7,6},{8,9},{9,8},{10,11... | collective-permute-start | bytes 1179656 | tf_op jit(solution)/shard_map/ppermute | solution.py:486
  52.4 6.4 %collective-permute-start.19 = (s16[144,256]{1,0:T(8,128)(2,1)S(1)}, s16[144,256]{1,0:T(8,128)(2,1)S(1)}, u32[]{:S(2)}, u32[]{:S(2)}) collective-permute-start(s16[144,256]{1,0:T(8,128)(2,1)S(1)} %get-tuple-element.57), channel_id=1, source_target_pairs={{0,4},{4,0},{8,12},{12,8},{16,20},{20,16},{24,28},{28,24},{1,5},{5... | collective-permute-start | bytes 221192 | tf_op jit(solution)/shard_map/ppermute | solution.py:486
  53.8 9.1 %collective-permute-start.17 = (s16[144,256]{1,0:T(8,128)(2,1)S(1)}, s16[144,256]{1,0:T(8,128)(2,1)S(1)}, u32[]{:S(2)}, u32[]{:S(2)}) collective-permute-start(s16[144,256]{1,0:T(8,128)(2,1)S(1)} %get-tuple-element.50.refs_6_), channel_id=1, source_target_pairs={{0,16},{4,20},{8,24},{12,28},{16,0},{20,4},{24,8},{28,12},{1,17},{... | collective-permute-start | bytes 221192 | tf_op jit(solution)/shard_map/ppermute | solution.py:486
  56.4 9.4 %collective-permute-start.18 = (s16[144,256]{1,0:T(8,128)(2,1)S(1)}, s16[144,256]{1,0:T(8,128)(2,1)S(1)}, u32[]{:S(2)}, u32[]{:S(2)}) collective-permute-start(s16[144,256]{1,0:T(8,128)(2,1)S(1)} %get-tuple-element.52), channel_id=1, source_target_pairs={{0,20},{4,16},{8,28},{12,24},{16,4},{20,0},{24,12},{28,8},{1,21},{... | collective-permute-start | bytes 221192 | tf_op jit(solution)/shard_map/ppermute | solution.py:486
  58.9 6.8 %collective-permute-start.20 = (s16[144,256]{1,0:T(8,128)(2,1)S(1)}, s16[144,256]{1,0:T(8,128)(2,1)S(1)}, u32[]{:S(2)}, u32[]{:S(2)}) collective-permute-start(s16[144,256]{1,0:T(8,128)(2,1)S(1)} %get-tuple-element.58), channel_id=1, source_target_pairs={{0,4},{4,0},{8,12},{12,8},{16,20},{20,16},{24,28},{28,24},{1,5},{5... | collective-permute-start | bytes 221192 | tf_op jit(solution)/shard_map/ppermute | solution.py:486
  60.3 5.5 %collective-permute-start.21 = (s16[144,256]{1,0:T(8,128)(2,1)S(1)}, s16[144,256]{1,0:T(8,128)(2,1)S(1)}, u32[]{:S(2)}, u32[]{:S(2)}) collective-permute-start(s16[144,256]{1,0:T(8,128)(2,1)S(1)} %get-tuple-element.59), channel_id=1, source_target_pairs={{0,8},{4,12},{8,0},{12,4},{16,24},{20,28},{24,16},{28,20},{1,9},{5... | collective-permute-start | bytes 221192 | tf_op jit(solution)/shard_map/ppermute | solution.py:486
  62.0 5.3 %collective-permute-start.22 = (s16[144,256]{1,0:T(8,128)(2,1)S(1)}, s16[144,256]{1,0:T(8,128)(2,1)S(1)}, u32[]{:S(2)}, u32[]{:S(2)}) collective-permute-start(s16[144,256]{1,0:T(8,128)(2,1)S(1)} %get-tuple-element.60), channel_id=1, source_target_pairs={{0,12},{4,8},{8,4},{12,0},{16,28},{20,24},{24,20},{28,16},{1,13},{... | collective-permute-start | bytes 221192 | tf_op jit(solution)/shard_map/ppermute | solution.py:486
  62.9 6.2 %collective-permute-start.23 = (s16[144,256]{1,0:T(8,128)(2,1)S(1)}, s16[144,256]{1,0:T(8,128)(2,1)S(1)}, u32[]{:S(2)}, u32[]{:S(2)}) collective-permute-start(s16[144,256]{1,0:T(8,128)(2,1)S(1)} %get-tuple-element.61), channel_id=1, source_target_pairs={{0,24},{4,28},{8,16},{12,20},{16,8},{20,12},{24,0},{28,4},{1,25},{... | collective-permute-start | bytes 221192 | tf_op jit(solution)/shard_map/ppermute | solution.py:486
  69.3 6.5 %collective-permute-start.24 = (bf16[128,256]{1,0:T(8,128)(2,1)S(1)}, bf16[128,256]{1,0:T(8,128)(2,1)S(1)}, u32[]{:S(2)}, u32[]{:S(2)}) collective-permute-start(bf16[128,256]{1,0:T(8,128)(2,1)S(1)} %last_step.1.refs_3_), channel_id=1, source_target_pairs={{0,24},{4,28},{8,16},{12,20},{16,8},{20,12},{24,0},{28,4},{1,25},{... | collective-permute-start | bytes 196616 | tf_op jit(solution)/shard_map/ppermute | solution.py:486
  72.2 5.3 %collective-permute-start.25 = (bf16[128,256]{1,0:T(8,128)(2,1)S(1)}, bf16[128,256]{1,0:T(8,128)(2,1)S(1)}, u32[]{:S(2)}, u32[]{:S(2)}) collective-permute-start(bf16[128,256]{1,0:T(8,128)(2,1)S(1)} %last_step.1.refs_3_), channel_id=1, source_target_pairs={{0,16},{4,20},{8,24},{12,28},{16,0},{20,4},{24,8},{28,12},{1,17},{... | collective-permute-start | bytes 196616 | tf_op jit(solution)/shard_map/ppermute | solution.py:486
  72.2 6.8 %collective-permute-start.26 = (bf16[128,256]{1,0:T(8,128)(2,1)S(1)}, bf16[128,256]{1,0:T(8,128)(2,1)S(1)}, u32[]{:S(2)}, u32[]{:S(2)}) collective-permute-start(bf16[128,256]{1,0:T(8,128)(2,1)S(1)} %last_step.1.refs_3_), channel_id=1, source_target_pairs={{0,8},{4,12},{8,0},{12,4},{16,24},{20,28},{24,16},{28,20},{1,9},{5... | collective-permute-start | bytes 196616 | tf_op jit(solution)/shard_map/ppermute | solution.py:486
  73.7 5.8 %collective-permute-start.30 = (bf16[128,256]{1,0:T(8,128)(2,1)S(1)}, bf16[128,256]{1,0:T(8,128)(2,1)S(1)}, u32[]{:S(2)}, u32[]{:S(2)}) collective-permute-start(bf16[128,256]{1,0:T(8,128)(2,1)S(1)} %last_step.1.refs_3_), channel_id=1, source_target_pairs={{0,4},{4,0},{8,12},{12,8},{16,20},{20,16},{24,28},{28,24},{1,5},{5... | collective-permute-start | bytes 196616 | tf_op jit(solution)/shard_map/ppermute | solution.py:486
  75.7 4.4 %collective-permute-start.27 = (bf16[128,256]{1,0:T(8,128)(2,1)S(1)}, bf16[128,256]{1,0:T(8,128)(2,1)S(1)}, u32[]{:S(2)}, u32[]{:S(2)}) collective-permute-start(bf16[128,256]{1,0:T(8,128)(2,1)S(1)} %collective-permute-done.24.refs_0_), channel_id=1, source_target_pairs={{0,4},{4,0},{8,12},{12,8},{16,20},{20,16},{24,28},{28,24},{1,5},{5... | collective-permute-start | bytes 196616 | tf_op jit(solution)/shard_map/ppermute | solution.py:486
  77.5 4.3 %collective-permute-start.28 = (bf16[128,256]{1,0:T(8,128)(2,1)S(1)}, bf16[128,256]{1,0:T(8,128)(2,1)S(1)}, u32[]{:S(2)}, u32[]{:S(2)}) collective-permute-start(bf16[128,256]{1,0:T(8,128)(2,1)S(1)} %collective-permute-done.25.refs_1_), channel_id=1, source_target_pairs={{0,4},{4,0},{8,12},{12,8},{16,20},{20,16},{24,28},{28,24},{1,5},{5... | collective-permute-start | bytes 196616 | tf_op jit(solution)/shard_map/ppermute | solution.py:486
  79.1 4.3 %collective-permute-start.29 = (bf16[128,256]{1,0:T(8,128)(2,1)S(1)}, bf16[128,256]{1,0:T(8,128)(2,1)S(1)}, u32[]{:S(2)}, u32[]{:S(2)}) collective-permute-start(bf16[128,256]{1,0:T(8,128)(2,1)S(1)} %collective-permute-done.26.refs_2_), channel_id=1, source_target_pairs={{0,4},{4,0},{8,12},{12,8},{16,20},{20,16},{24,28},{28,24},{1,5},{5... | collective-permute-start | bytes 196616 | tf_op jit(solution)/shard_map/ppermute | solution.py:486
